TPU v7x, 32 devices: a whole 2x2x4 slice. The times are simulated.
32 devices in a mesh: slab: 8 (over z, y), grid: 4 (over x, core).
Axes of the slice: x: 2, y: 2, z: 4, core: 2. Of those that a mesh axis runs over, the one named last changes fastest.
Arguments:
- orbitals: bfloat16 [64, 110592], P(None, 'grid'), may hold values from -6 to 6
- targets: int32 [16], replicated, may hold values from 0 to 63
- points: int32 [32], P('slab'), may hold values from 0 to 110591, as said below
- fit: float32 [32, 4], P('slab'), may hold values from -2 to 4, as said below
Outputs:
- applied_exchange: float32 [16, 110592], P('slab', 'grid')
Inputs may be any that keep to these rules, and one draw needn't show every extreme that they name: `points`: 32 distinct grid cells. `fit`: each block of 4 rows is a symmetric matrix.
All inputs are finite; a program needn't handle non-finite values.
Results may differ from a plain program's by a relative error of at most 0.004.
Values may be sent and summed in bfloat16 or wider, within the bound.
No kernel may reach another device: no remote copies, remote signals or barrier semaphores. Data moves between devices by JAX's collectives and lax.ppermute only.
A program may use at most 64 MiB of HBM per device.

v0:
```python
import math

import jax
import jax.numpy as jnp
from jax import lax
from jax.sharding import PartitionSpec as P

NG = 48


screening = 4.0
careful = lax.Precision.HIGH


def dft_tables(length):
    positions = jnp.arange(length, dtype=jnp.int32)
    product = positions[:, None] * positions[None, :] % length
    angles = product.astype(jnp.float32) * (2.0 * math.pi / length)
    return (jnp.cos(angles), jnp.sin(angles))


def kernel_table():
    full_index = jnp.arange(NG, dtype=jnp.int32)
    wrapped = jnp.where(full_index > NG // 2, full_index - NG, full_index).astype(jnp.float32)
    half_index = jnp.arange(NG // 2 + 1, dtype=jnp.int32).astype(jnp.float32)
    step_size = 2.0 * math.pi / NG
    full_sq = wrapped * step_size * (wrapped * step_size)
    half_sq = half_index * step_size * (half_index * step_size)
    summed = full_sq[:, None, None] + full_sq[None, :, None] + half_sq[None, None, :]
    return screening / (screening + summed)


def apply_axis(values, matrix, pattern):
    return jnp.einsum(
        pattern, values, matrix, precision=careful, preferred_element_type=jnp.float32
    )


def split_apply(values, matrix, pattern):
    upper = matrix.astype(jnp.bfloat16)
    lower = (matrix - upper.astype(jnp.float32)).astype(jnp.bfloat16)
    first = jnp.einsum(pattern, values, upper, preferred_element_type=jnp.float32)
    return first + jnp.einsum(pattern, values, lower, preferred_element_type=jnp.float32)


def solve_one(vector_row):
    half_len = NG // 2 + 1
    cosine, sin_table = dft_tables(NG)
    cos_half = cosine[:, :half_len]
    sin_half = sin_table[:, :half_len]
    cube_vals = vector_row.reshape(NG, NG, NG)
    real_part = split_apply(cube_vals, cos_half, "xyz,zm->xym")
    imag_part = -split_apply(cube_vals, sin_half, "xyz,zm->xym")
    for pattern in ("xym,yb->xbm", "xym,xb->bym"):
        real_next = apply_axis(real_part, cosine, pattern) + apply_axis(
            imag_part, sin_table, pattern
        )
        imag_part = apply_axis(imag_part, cosine, pattern) - apply_axis(
            real_part, sin_table, pattern
        )
        real_part = real_next
    weights = kernel_table()
    real_part = real_part * weights
    imag_part = imag_part * weights
    for pattern in ("xym,xb->bym", "xym,yb->xbm"):
        real_next = apply_axis(real_part, cosine, pattern) - apply_axis(
            imag_part, sin_table, pattern
        )
        imag_part = apply_axis(real_part, sin_table, pattern) + apply_axis(
            imag_part, cosine, pattern
        )
        real_part = real_next
    frequency = jnp.arange(half_len, dtype=jnp.int32)
    fold_weight = jnp.where((frequency == 0) | (frequency == NG // 2), 1.0, 2.0).astype(jnp.float32)
    result = apply_axis(real_part * fold_weight, cos_half, "xym,zm->xyz") - apply_axis(
        imag_part * fold_weight, sin_half, "xym,zm->xyz"
    )
    return (result * (1.0 / (NG * NG * NG))).reshape(-1).astype(jnp.bfloat16)


def body(orbitals, targets, points, fit):
    occupied, shard_len = orbitals.shape
    target_count = targets.shape[0]
    group_size = points.shape[0]
    slab_count = lax.axis_size("slab")
    offsets = points - lax.axis_index("grid") * shard_len
    cell_ids = lax.broadcasted_iota(jnp.int32, (group_size, shard_len), 1)
    one_hot = (cell_ids == offsets[:, None]).astype(jnp.bfloat16)
    point_terms = lax.dot_general(
        orbitals, one_hot, (((1,), (1,)), ((), ())), preferred_element_type=jnp.float32
    )
    at_points = lax.psum(point_terms, "grid").astype(jnp.bfloat16)
    chosen = jnp.take(orbitals, targets, axis=0)
    target_points = jnp.take(at_points, targets, axis=0)
    contract_first = (((0,), (0,)), ((), ()))
    density = lax.dot_general(
        at_points, orbitals, contract_first, preferred_element_type=jnp.float32
    ) * (1.0 / math.sqrt(occupied))
    target_density = lax.dot_general(
        target_points, chosen, contract_first, preferred_element_type=jnp.float32
    ) * (1.0 / math.sqrt(target_count))
    pairs = density * target_density
    fitted = lax.dot_general(
        fit,
        pairs,
        contract_first,
        precision=lax.Precision.HIGHEST,
        preferred_element_type=jnp.float32,
    ).astype(jnp.bfloat16)
    vectors = lax.all_to_all(fitted, "grid", split_axis=0, concat_axis=1, tiled=True)
    potential = lax.map(solve_one, vectors)
    returned = lax.all_to_all(potential, "grid", split_axis=1, concat_axis=0, tiled=True)
    weighted = (returned.astype(jnp.float32) * density).astype(jnp.bfloat16)
    prefactor = -1.0 / math.sqrt(group_size * slab_count)
    regrouped = lax.all_to_all(weighted, "slab", split_axis=1, concat_axis=0, tiled=True)
    all_targets = lax.all_gather(target_points, "slab", axis=1, tiled=True)
    block_out = jnp.dot(all_targets, regrouped, preferred_element_type=jnp.float32)
    summed = lax.all_to_all(block_out, "slab", split_axis=0, concat_axis=1, tiled=True)
    return summed * prefactor


def solution(mesh):
    in_specs = (P(None, "grid"), P(), P("slab"), P("slab", None))
    out_specs = P("slab", "grid")
    return jax.shard_map(body, mesh=mesh, in_specs=in_specs, out_specs=out_specs, check_vma=False)
```

profile of v0, /device:TPU:0, one launch (start us, length us, event | category | flops | bytes accessed | tf_op | source)
XLA Modules:
  0.0 131.0 jit_solution(4554894141643493492)
XLA Ops:
  0.0 0.0 copy-start
  0.0 1.3 %compare_and_fusion = pred[16]{0:T(512)(128)(4,1)} fusion(s32[16]{0:T(128)} %param.5), kind=kLoop, calls=%fused_computation.103 | loop fusion | flops 96 | bytes 80 | tf_op jit(solution)/shard_map/jit(_take)/and | solution.py:94
  1.3 1.2 compare_select_fusion.1
  2.6 0.7 broadcast_subtract_fusion
  3.2 0.0 copy-done
  3.2 1.1 convolution_bitcast_fusion
  4.3 8.9 %psum.7 = bf16[64,4]{0,1:T(4,128)(2,1)} all-reduce(f32[64,4]{0,1:T(4,128)S(1)} %convolution_bitcast_fusion), channel_id=1, replica_groups=mesh['slab'=8,'grid'=4] {'grid'}, use_global_device_ids=true, to_apply=%region_0.0 | all-reduce | flops 256 | bytes 1536 | tf_op jit(solution)/shard_map/psum | solution.py:92
  13.2 0.8 copy.54
  14.0 2.0 %convolution_multiply_fusion.1 = f32[4,27648]{1,0:T(4,128)} fusion(bf16[64,4]{0,1:T(4,128)(2,1)} %psum.7, bf16[64,27648]{1,0:T(8,128)(2,1)S(1)} %copy-done), kind=kOutput, calls=%fused_computation.4 | convolution fusion | flops 14266368 | bytes 3981824 | tf_op jit(solution)/shard_map/dot_general | solution.py:96
  16.0 0.6 pad_clamp_fusion
  16.6 2.2 %gather_fusion.1 = bf16[16,27648]{1,0:T(8,128)(2,1)} fusion(bf16[64,27648]{1,0:T(8,128)(2,1)S(1)} %copy-done, s32[1024]{0:T(1024)} %pad_clamp_fusion), kind=kCustom, calls=%fused_computation.1 | custom fusion | bytes 1769536 | tf_op jit(solution)/shard_map/jit(_take)/gather | solution.py:93
  18.8 1.3 gather_fusion
  20.0 1.7 %fusion = f32[4,27648]{1,0:T(4,128)S(1)} fusion(f32[4,27648]{1,0:T(4,128)} %convolution_multiply_fusion.1, bf16[16,27648]{1,0:T(8,128)(2,1)} %gather_fusion.1, pred[16]{0:T(512)(128)(4,1)} %compare_and_fusion, bf16[16,4]{1,0:T(8,128)(2,1)} %gather_fusion), kind=kOutput, calls=%fused_computation.3 | convolution fusion | flops 4202560 | bytes 1769616 | tf_op jit(solution)/shard_map/dot_general | solution.py:99
  21.7 2.3 %fusion.1 = bf16[4,1,27648]{2,0,1:T(4,128)(2,1)} fusion(f32[4,27648]{1,0:T(4,128)S(1)} %fusion, f32[4,4]{1,0:T(4,128)} %param.7), kind=kOutput, calls=%fused_computation.6 | convolution fusion | flops 5419008 | bytes 663616 | tf_op jit(solution)/shard_map/dot_general | solution.py:103
  24.0 0.5 broadcast.207
  24.5 2.5 %reduce.1 = bf16[4,27648]{1,0:T(4,128)(2,1)} reduce(bf16[4,1,27648]{2,0,1:T(4,128)(2,1)} %fusion.1, bf16[]{:T(256)} %broadcast.207), dimensions={1}, to_apply=%copy.57.reduce_sub_computation | reduce | bytes 442370 | tf_op jit(solution)/shard_map/all_to_all | solution.py:110
  27.1 1.7 %reshape.154 = bf16[4,2,13824]{2,1,0:T(2,128)(2,1)} reshape(bf16[4,27648]{1,0:T(4,128)(2,1)} %reduce.1) | data formatting | bytes 442368
  28.8 4.0 %all-to-all-start = ((bf16[4,2,13824]{2,1,0:T(2,128)(2,1)}), bf16[4,2,13824]{2,1,0:T(2,128)(2,1)}, u32[]{:S(2)}, u32[]{:S(2)}) async-start(bf16[4,2,13824]{2,1,0:T(2,128)(2,1)} %reshape.154), calls=%async_computation | async-start | bytes 442368 | tf_op jit(solution)/shard_map/all_to_all | solution.py:110
  32.8 0.7 fusion.55
  33.5 0.7 broadcast_add_fusion
  34.2 0.7 fusion.54
  35.0 3.5 %all-to-all-done = bf16[4,2,13824]{2,1,0:T(2,128)(2,1)} async-done(((bf16[4,2,13824]{2,1,0:T(2,128)(2,1)}), bf16[4,2,13824]{2,1,0:T(2,128)(2,1)}, u32[]{:S(2)}, u32[]{:S(2)}) %all-to-all-start) | async-done | bytes 221216 | tf_op jit(solution)/shard_map/all_to_all | solution.py:110
  38.4 1.8 %reshape.155 = bf16[4,1,27648]{2,1,0:T(2,128)(2,1)} reshape(bf16[4,2,13824]{2,1,0:T(2,128)(2,1)} %all-to-all-done) | data formatting | bytes 442368
  40.2 3.0 %reduce = bf16[4,27648]{1,0:T(4,128)(2,1)} reduce(bf16[4,1,27648]{2,1,0:T(2,128)(2,1)} %reshape.155, bf16[]{:T(256)} %constant.89), dimensions={1}, to_apply=%all_to_all.41.reduce_sub_computation | reduce | bytes 442370 | tf_op jit(solution)/shard_map/all_to_all | solution.py:110
  43.2 2.3 %reshape.117 = bf16[48,48,48]{2,1,0:T(8,128)(2,1)} reshape(bf16[4,27648]{1,0:T(4,128)(2,1)} %reduce) | data formatting | bytes 442368 | tf_op jit(solution)/shard_map/while/body/eval_jaxpr/reshape | solution.py:51
  45.5 1.9 %fusion.82 = f32[48,48,25]{1,2,0:T(8,128)S(1)} fusion(bf16[48,48,48]{2,1,0:T(8,128)(2,1)} %reshape.117, f32[48,48]{0,1:T(8,128)} %fusion.54), kind=kOutput, calls=%fused_computation.92 | convolution fusion | flops 5529600 | bytes 828416 | tf_op jit(solution)/shard_map/while/body/eval_jaxpr/xyz,zm->xym/dot_general | solution.py:42
  47.4 1.9 %fusion.8 = f32[48,48,25]{1,2,0:T(8,128)S(1)} fusion(f32[48,48,25]{1,2,0:T(8,128)S(1)} %fusion.82, bf16[48,48,48]{2,1,0:T(8,128)(2,1)} %reshape.117, f32[48,48]{0,1:T(8,128)} %fusion.54), kind=kOutput, calls=%fused_computation.17 | convolution fusion | flops 5649600 | bytes 1067008 | tf_op jit(solution)/shard_map/while/body/eval_jaxpr/xyz,zm->xym/dot_general | solution.py:43
  49.2 1.3 fusion.21
  50.5 0.7 fusion.84
  51.2 0.8 convolution_add_fusion.2
  52.0 1.3 fusion.25
  53.3 1.3 fusion.11
  54.5 1.3 fusion.12
  55.8 1.2 fusion.48
  57.0 1.2 fusion.43
  58.1 1.2 fusion.10
  59.3 0.5 fusion.34
  59.8 0.5 fusion.45
  60.3 1.2 fusion.9
  61.5 0.7 convolution_subtract_fusion.2
  62.2 0.7 fusion.17
  62.9 0.7 fusion.19
  63.6 0.5 convolution_add_fusion.3
  64.2 0.7 fusion.7
  64.9 0.7 fusion.5
  65.6 1.1 fusion.58
  66.7 2.0 %fusion.3 = bf16[48,48,48]{2,1,0:T(8,128)(2,1)} fusion(f32[48,48,48]{2,1,0:T(8,128)S(1)} %fusion.58, f32[48,48,25]{1,2,0:T(8,128)S(1)} %fusion.7, f32[48,48]{0,1:T(8,128)S(1)} %copy-done.3), kind=kOutput, calls=%fused_computation.9 | convolution fusion | flops 16920576 | bytes 2203648 | tf_op jit(solution)/shard_map/while/body/eval_jaxpr/xym,zm->xyz/dot_general | solution.py:34
  68.7 2.4 %convert_element_type.150 = bf16[1,4,27648]{2,0,1:T(2,128)(2,1)} reshape(bf16[48,48,48]{2,1,0:T(8,128)(2,1)} %fusion.3) | data formatting | bytes 442368 | tf_op jit(solution)/shard_map/while/body/eval_jaxpr/convert_element_type | solution.py:78
  71.1 3.6 %reduce.2 = bf16[4,27648]{1,0:T(4,128)(2,1)} reduce(bf16[4,1,27648]{2,1,0:T(2,128)(2,1)} %bitcast.108, bf16[]{:T(256)} %broadcast.207), dimensions={1}, to_apply=%bitcast.85.reduce_sub_computation | reduce | bytes 442370
  74.7 1.7 %reshape.156 = bf16[4,2,13824]{2,1,0:T(2,128)(2,1)} reshape(bf16[4,27648]{1,0:T(4,128)(2,1)} %reduce.2) | data formatting | bytes 442368
  76.5 9.7 %all_to_all.52 = bf16[4,2,13824]{2,1,0:T(2,128)(2,1)} all-to-all(bf16[4,2,13824]{2,1,0:T(2,128)(2,1)} %reshape.156), channel_id=1, replica_groups=mesh['slab'=8,'grid'=4] {'grid'}, dimensions={0} | all-to-all | bytes 442368 | tf_op jit(solution)/shard_map/all_to_all | solution.py:112
  86.1 1.8 %reshape.157 = bf16[4,1,27648]{2,1,0:T(2,128)(2,1)} reshape(bf16[4,2,13824]{2,1,0:T(2,128)(2,1)} %all_to_all.52) | data formatting | bytes 442368
  87.9 2.0 %fusion.27 = bf16[4,27648]{1,0:T(4,128)(2,1)} fusion(f32[4,27648]{1,0:T(4,128)} %convolution_multiply_fusion.1, bf16[1,4,27648]{2,0,1:T(2,128)(2,1)} %bitcast.107), kind=kLoop, calls=%fused_computation.46 | loop fusion | flops 331776 | bytes 884736 | tf_op jit(solution)/shard_map/convert_element_type | solution.py:113
  89.9 5.8 %all-to-all-start.2 = ((bf16[4,8,3456]{2,0,1:T(4,128)(2,1)}), bf16[4,8,3456]{2,0,1:T(4,128)(2,1)}, u32[]{:S(2)}, u32[]{:S(2)}) async-start(bf16[4,8,3456]{2,0,1:T(4,128)(2,1)} %bitcast.109), calls=%async_computation.2 | async-start | bytes 442368 | tf_op jit(solution)/shard_map/all_to_all | solution.py:115
  95.7 0.1 fusion.88
  95.8 0.1 copy.55
  95.9 21.0 %all-gather = bf16[8,4,16]{2,1,0:T(4,128)(2,1)S(1)} all-gather(bf16[1,4,16]{2,1,0:T(4,128)(2,1)S(1)} %bitcast.112), channel_id=1, replica_groups=mesh['slab'=8,'grid'=4] {'slab'}, dimensions={0}, use_global_device_ids=true | all-gather | bytes 1152 | tf_op jit(solution)/shard_map/all_gather | solution.py:116
  116.9 0.1 copy.56
  116.9 0.0 all-to-all-done.2
  116.9 1.7 %reshape.151 = bf16[32,3456,1]{1,0,2:T(8,128)(2,1)} reshape(bf16[8,4,3456]{2,1,0:T(4,128)(2,1)} %bitcast.26) | data formatting | bytes 442368 | tf_op jit(solution)/shard_map/all_to_all | solution.py:115
  118.6 1.1 fusion.86
  119.7 0.1 copy.78
  119.9 10.4 %all_to_all.53 = f32[8,2,3456]{2,1,0:T(2,128)S(1)} all-to-all(f32[8,2,3456]{2,1,0:T(2,128)S(1)} %copy.78), channel_id=1, replica_groups=mesh['slab'=8,'grid'=4] {'slab'}, dimensions={0} | all-to-all | bytes 442368 | tf_op jit(solution)/shard_map/all_to_all | solution.py:118
  130.2 0.8 broadcast_multiply_fusion
  (17 shorter events, 0.0 us)
Async XLA Ops:
  0.0 3.2 %copy-start = (bf16[64,27648]{1,0:T(8,128)(2,1)S(1)}, bf16[64,27648]{1,0:T(8,128)(2,1)}, u32[]{:S(2)}) copy-start(bf16[64,27648]{1,0:T(8,128)(2,1)} %param.4) | copy-start | bytes 10616836
  14.0 2.0 %copy-start.7 = (s32[16]{0:T(128)S(1)}, s32[16]{0:T(128)}, u32[]{:S(2)}) copy-start(s32[16]{0:T(128)} %compare_select_fusion.1) | copy-start | bytes 196
  28.8 9.7 %all-to-all-start = ((bf16[4,2,13824]{2,1,0:T(2,128)(2,1)}), bf16[4,2,13824]{2,1,0:T(2,128)(2,1)}, u32[]{:S(2)}, u32[]{:S(2)}) async-start(bf16[4,2,13824]{2,1,0:T(2,128)(2,1)} %reshape.154), calls=%async_computation | async-start | bytes 442368 | tf_op jit(solution)/shard_map/all_to_all | solution.py:110
  45.5 5.0 %copy-start.1 = (bf16[48,48,48]{2,1,0:T(8,128)(2,1)S(1)}, bf16[48,48,48]{2,1,0:T(8,128)(2,1)}, u32[]{:S(2)}) copy-start(bf16[48,48,48]{2,1,0:T(8,128)(2,1)} %reshape.117) | copy-start | bytes 663556
  45.5 5.0 %copy-start.2 = (f32[48,48]{0,1:T(8,128)S(1)}, f32[48,48]{0,1:T(8,128)}, u32[]{:S(2)}) copy-start(f32[48,48]{0,1:T(8,128)} %fusion.55) | copy-start | bytes 27652
  52.0 6.1 %copy-start.5 = (f32[48,48]{1,0:T(8,128)S(1)}, f32[48,48]{1,0:T(8,128)}, u32[]{:S(2)}) copy-start(f32[48,48]{1,0:T(8,128)} %broadcast_add_fusion) | copy-start | bytes 27652
  64.2 2.6 %copy-start.3 = (f32[48,48]{0,1:T(8,128)S(1)}, f32[48,48]{0,1:T(8,128)}, u32[]{:S(2)}) copy-start(f32[48,48]{0,1:T(8,128)} %fusion.54) | copy-start | bytes 27652
  66.7 29.0 %copy-start.4 = (bf16[16,4]{1,0:T(8,128)(2,1)S(1)}, bf16[16,4]{1,0:T(8,128)(2,1)}, u32[]{:S(2)}) copy-start(bf16[16,4]{1,0:T(8,128)(2,1)} %gather_fusion) | copy-start | bytes 388
  66.7 29.0 %copy-start.6 = (pred[16]{0:T(512)(128)(4,1)S(1)}, pred[16]{0:T(512)(128)(4,1)}, u32[]{:S(2)}) copy-start(pred[16]{0:T(512)(128)(4,1)} %compare_and_fusion) | copy-start | bytes 52
  89.9 27.1 %all-to-all-start.2 = ((bf16[4,8,3456]{2,0,1:T(4,128)(2,1)}), bf16[4,8,3456]{2,0,1:T(4,128)(2,1)}, u32[]{:S(2)}, u32[]{:S(2)}) async-start(bf16[4,8,3456]{2,0,1:T(4,128)(2,1)} %bitcast.109), calls=%async_computation.2 | async-start | bytes 442368 | tf_op jit(solution)/shard_map/all_to_all | solution.py:115
where the time goes:
time: 132 us; the launch traced here: 131 us
  blocking collectives  49.9 us (38%)
  matrix products  31.2 us (24%)
  local copies, waits for them, and re-layouts  18.4 us (14%)
  other arithmetic  18 us (14%)
  starting transfers between devices  9.84 us (7%)
  waiting for transfers between devices  3.49 us (3%)
    all_gather x1, blocking collectives, body(): all_targets = lax.all_gather(target_points, 'slab', axis=1, tiled=True)  21 us
    dot_general x18, matrix products, apply_axis(): jnp.einsum(pattern, values, matrix, precision=careful, preferred_element_...  17.8 us
    all_to_all x1, blocking collectives, body(): lax.all_to_all(block_out, 'slab', split_axis=0, concat_axis=1, tiled=True)  10.4 us
    all_to_all x1, blocking collectives, body(): lax.all_to_all(potential, 'grid', split_axis=1, concat_axis=0, tiled=True)  9.68 us
    psum x1, blocking collectives, body(): at_points = lax.psum(point_terms, 'grid').astype(jnp.bfloat16)  8.88 us
    unnamed x22, local copies, waits for them, and re-layouts  7.15 us
    all_to_all x1, starting transfers between devices, body(): lax.all_to_all(weighted, 'slab', split_axis=1, concat_axis=0, tiled=True)  5.83 us
    all_to_all x2, other arithmetic, body(): lax.all_to_all(fitted, 'grid', split_axis=0, concat_axis=1, tiled=True)  5.52 us
  transfers between devices with their start and end apart: 2, of which 1 were waited for; matrix products, arithmetic and copies ran while one was open for 2% of the time, Pallas kernels for 0%

commit v1 on v0

--- a/solution.py
+++ b/solution.py
@@ -2,7 +2,11 @@
 
 import jax
 import jax.numpy as jnp
+import ml_dtypes
+import numpy as np
 from jax import lax
+from jax.experimental import pallas as pl
+from jax.experimental.pallas import tpu as pltpu
 from jax.sharding import PartitionSpec as P
 
 NG = 48
@@ -10,6 +14,11 @@
 
 screening = 4.0
 careful = lax.Precision.HIGH
+lanes = 128
+f32 = jnp.float32
+bf16 = jnp.bfloat16
+everyone = ("slab", "grid")
+contract_last = (((1,), (1,)), ((), ()))
 
 
 def dft_tables(length):
@@ -78,7 +87,7 @@
     return (result * (1.0 / (NG * NG * NG))).reshape(-1).astype(jnp.bfloat16)
 
 
-def body(orbitals, targets, points, fit):
+def plain_body(orbitals, targets, points, fit):
     occupied, shard_len = orbitals.shape
     target_count = targets.shape[0]
     group_size = points.shape[0]
@@ -119,7 +128,354 @@
     return summed * prefactor
 
 
+def hartley(length):
+    product = np.outer(np.arange(length), np.arange(length)) % length
+    angles = product * (2.0 * math.pi / length)
+    return (np.cos(angles) + np.sin(angles)) / math.sqrt(length)
+
+
+def split_table(table):
+    upper = table.astype(ml_dtypes.bfloat16)
+    lower = (table - upper.astype(np.float64)).astype(ml_dtypes.bfloat16)
+    return upper, lower
+
+
+def split_value(value):
+    upper = value.astype(bf16)
+    return upper, (value - upper.astype(jnp.float32)).astype(bf16)
+
+
+class Plan:
+    def __init__(self, edge):
+        self.edge = edge
+        self.half = edge // 2
+        self.slot = lanes // 2
+        self.inner = lanes // math.gcd(edge, lanes)
+        self.outer = edge // self.inner
+        self.block = self.inner * edge
+        self.block_rows = self.block // lanes
+        self.plane_rows = edge * edge // lanes
+        self.rows = edge * self.plane_rows
+        matrix = hartley(edge)
+        pairs = self.inner // 2
+        wide = np.zeros((2, self.inner, edge, self.inner, 2, self.slot))
+        for h in range(2):
+            for y in range(self.inner):
+                wide[h, y, :, y, h, :edge] = matrix
+        wide = wide.reshape(2, self.block, self.inner * lanes)
+        self.forward = []
+        for j in range(pairs):
+            low = 2 * j * edge // lanes * lanes
+            high = -(-(2 * j + 2) * edge // lanes) * lanes
+            part = wide[:, low:high, 2 * j * lanes:(2 * j + 2) * lanes].reshape(2 * (high - low), 2 * lanes)
+            self.forward.append((low, high, part))
+        back = np.transpose(wide, (2, 0, 1))
+        self.backward = []
+        for c in range(self.block_rows):
+            low = c * lanes // edge * lanes
+            high = -(-(c + 1) * lanes // edge) * lanes
+            part = back[low:high, :, c * lanes:(c + 1) * lanes].reshape(high - low, 2 * lanes)
+            self.backward.append((low, high, part))
+        step = 2.0 * math.pi / edge
+        index = np.arange(edge)
+        square = (np.where(index > edge // 2, index - edge, index) * step) ** 2
+        weights = screening / (screening + square[:, None, None] + square[None, :, None] + square[None, None, :])
+        weights = weights.reshape(2, self.half, edge, edge)
+        table = np.zeros((self.half, edge, 2, self.slot))
+        table[..., :edge] = np.transpose(weights, (1, 2, 0, 3))
+        self.weights = table.reshape(self.half, edge, lanes).astype(np.float32)
+        self.left = np.concatenate([*split_table(matrix), split_table(matrix)[0]], axis=1)
+
+    def tables(self):
+        fh, fl = split_table(np.concatenate([p for _, _, p in self.forward]))
+        bh, bl = split_table(np.concatenate([p for _, _, p in self.backward]))
+        return [self.left, fh, fl, bh, bl, self.weights]
+
+
+def three(value):
+    upper, lower = split_value(value)
+    return jnp.concatenate([upper, upper, lower], axis=0)
+
+
+def dot(a, b):
+    return jnp.dot(a, b, preferred_element_type=jnp.float32)
+
+
+def solve(plan, cube, left, fh, fl, bh, bl, weights, mid):
+    edge, half, inner, outer = plan.edge, plan.half, plan.inner, plan.outer
+    left_all = left[...]
+    values = jnp.concatenate(
+        [cube[pl.ds(c, edge, stride=plan.plane_rows), :].astype(bf16) for c in range(plan.plane_rows)], axis=1)
+    spectrum = dot(left_all[:, :2 * edge], jnp.concatenate([values, values], axis=0))
+    folded = jnp.concatenate([
+        jnp.concatenate([spectrum[:half, b * plan.block:(b + 1) * plan.block],
+                         spectrum[half:, b * plan.block:(b + 1) * plan.block]], axis=1)
+        for b in range(outer)], axis=0)
+    upper, lower = split_value(folded)
+    at = 0
+    for j, (low, high, part) in enumerate(plan.forward):
+        window = lambda v: jnp.concatenate([v[:, low:high], v[:, plan.block + low:plan.block + high]], axis=1)
+        u, l = window(upper), window(lower)
+        th, tl = fh[at:at + part.shape[0], :], fl[at:at + part.shape[0], :]
+        at += part.shape[0]
+        result = dot(u, th) + dot(l, th) + dot(u, tl)
+        for b in range(outer):
+            for o in range(2):
+                y = b * inner + 2 * j + o
+                mid[y * half:(y + 1) * half, :] = result[b * half:(b + 1) * half, o * lanes:(o + 1) * lanes]
+    for k in range(0, half, 2):
+        value = jnp.concatenate([mid[pl.ds(k + o, edge, stride=half), :] for o in range(2)], axis=1)
+        value = dot(left_all, three(value))
+        value = value * jnp.concatenate([weights[k], weights[k + 1]], axis=1)
+        value = dot(left_all, three(value))
+        for o in range(2):
+            mid[pl.ds(k + o, edge, stride=half), :] = value[:, o * lanes:(o + 1) * lanes]
+    value = jnp.concatenate([
+        jnp.concatenate([mid[(b * inner + y) * half:(b * inner + y + 1) * half, :] for y in range(inner)], axis=1)
+        for b in range(outer)], axis=0)
+    upper, lower = split_value(value)
+    at = 0
+    pieces = []
+    for low, high, part in plan.backward:
+        u, l = upper[:, low:high], lower[:, low:high]
+        th, tl = bh[at:at + part.shape[0], :], bl[at:at + part.shape[0], :]
+        at += part.shape[0]
+        pieces.append(dot(u, th) + dot(l, th) + dot(u, tl))
+    value = jnp.concatenate([
+        jnp.concatenate([pieces[c][b * half:(b + 1) * half, :lanes], pieces[c][b * half:(b + 1) * half, lanes:]], axis=0)
+        for b in range(outer) for c in range(plan.block_rows)], axis=1)
+    value = dot(left_all, three(value))
+    for c in range(plan.plane_rows):
+        cube[pl.ds(c, edge, stride=plan.plane_rows), :] = value[:, c * lanes:(c + 1) * lanes]
+
+
+def params(mebibytes):
+    return pltpu.CompilerParams(vmem_limit_bytes=mebibytes * 1024 * 1024)
+
+
+whole = pl.BlockSpec(memory_space=pltpu.VMEM)
+scalars = pl.BlockSpec(memory_space=pltpu.SMEM)
+anywhere = pl.BlockSpec(memory_space=pl.ANY)
+
+
+def iota(shape, axis):
+    return lax.broadcasted_iota(jnp.int32, shape, axis)
+
+
+def read_points(orbitals, points):
+    occupied, shard_len = orbitals.shape
+    group = points.shape[0]
+
+    def kernel(points_ref, orbitals_ref, out_ref, tiles, sems):
+        base = lax.axis_index("grid") * shard_len
+        rows, columns = iota((8, group * lanes), 0), iota((8, group * lanes), 1)
+        chosen = jnp.zeros((8, group * lanes), f32)
+        copies = []
+        for m in range(group):
+            local = points_ref[m] - base
+            inside = (local >= 0) & (local < shard_len)
+            local = jnp.clip(local, 0, shard_len - 1)
+            first = pl.multiple_of(local // lanes * lanes, lanes)
+            copy = pltpu.make_async_copy(
+                orbitals_ref.at[:, pl.ds(first, lanes)], tiles.at[:, pl.ds(m * lanes, lanes)], sems.at[m])
+            copy.start()
+            copies.append(copy)
+            column = jnp.where(inside, local - first + m * lanes, -1)
+            chosen = jnp.where((rows == m) & (columns == column), 1.0, chosen)
+        for copy in copies:
+            copy.wait()
+        chosen = jnp.concatenate([chosen, jnp.zeros_like(chosen)], axis=0).astype(bf16)
+        out = lax.dot_general(chosen, tiles[...], contract_last, preferred_element_type=f32)
+        out_ref[...] = jnp.concatenate([out[:8], jnp.zeros((8, lanes - occupied), f32)], axis=1)
+
+    return pl.pallas_call(
+        kernel,
+        out_shape=jax.ShapeDtypeStruct((8, lanes), f32),
+        in_specs=[scalars, anywhere],
+        out_specs=whole,
+        scratch_shapes=[pltpu.VMEM((occupied, group * lanes), bf16), pltpu.SemaphoreType.DMA((group,))],
+        compiler_params=params(4),
+        name="read_points",
+    )(points, orbitals)
+
+
+def fit_pairs(orbitals, targets, fit, shares):
+    occupied, shard_len = orbitals.shape
+    count, group = targets.shape[0], fit.shape[0]
+    shard_rows = shard_len // lanes
+    step = shard_rows // 8
+    scale = 1.0 / math.sqrt(occupied) / math.sqrt(count)
+
+    def kernel(targets_ref, fit_ref, orbitals_ref, *refs):
+        share_refs, out_refs, at_ref, mid = refs[:group], refs[group:2 * group], refs[2 * group], refs[2 * group + 1]
+        me = lax.axis_index("grid")
+        at = share_refs[0][...]
+        for ref in share_refs[1:]:
+            at = at + ref[...]
+        at_ref[...] = at
+        rows, columns = iota((8, lanes), 0), iota((8, lanes), 1)
+        counts = jnp.zeros((8, lanes), f32)
+        for k in range(count):
+            counts = counts + jnp.where(columns == targets_ref[k], 1.0, 0.0)
+        twice = jnp.where(rows < group, at, pltpu.roll(at, group, 0))
+        weighted = counts * twice
+        upper = weighted.astype(bf16).astype(f32)
+        left = jnp.concatenate([twice, upper, weighted - upper, jnp.zeros((8, lanes), f32)], axis=0)
+        left = left.astype(bf16)[:, :occupied]
+        coefficients = []
+        for j in range(group):
+            value = jnp.zeros((8, lanes), f32)
+            for r in range(8):
+                d = r % group
+                value = jnp.where(rows == r, fit_ref[(d + j) % group, jnp.bitwise_xor(me, d)], value)
+            coefficients.append(value * scale)
+        for c in range(0, shard_rows, step):
+            product = jnp.dot(left, orbitals_ref[:, c * lanes:(c + step) * lanes], preferred_element_type=f32)
+            for r in range(step):
+                part = product[:, r * lanes:(r + 1) * lanes]
+                pair = part[:8] * (part[8:16] + part[16:24])
+                value = pair * coefficients[0]
+                for j in range(1, group):
+                    value = value + pltpu.roll(pair, 8 - j, 0) * coefficients[j]
+                mid[(c + r) * 8:(c + r + 1) * 8, :] = value
+        for d in range(group):
+            out_refs[d][...] = mid[pl.ds(d, shard_rows, stride=8), :].astype(bf16)
+
+    piece = jax.ShapeDtypeStruct((shard_rows, lanes), bf16)
+    return pl.pallas_call(
+        kernel,
+        out_shape=[piece] * group + [jax.ShapeDtypeStruct((8, lanes), f32)],
+        in_specs=[scalars, scalars, whole] + [whole] * group,
+        out_specs=[whole] * (group + 1),
+        scratch_shapes=[pltpu.VMEM((shard_rows * 8, lanes), f32)],
+        compiler_params=params(16),
+        name="fit_pairs",
+    )(targets, fit, orbitals, *shares)
+
+
+def potentials(plan, pieces, at, slab_count):
+    grid_count, piece_rows = len(pieces), pieces[0].shape[0]
+    part = piece_rows // slab_count
+    tables = plan.tables()
+
+    def kernel(at_ref, *refs):
+        piece_refs, refs = refs[:grid_count], refs[grid_count:]
+        table_refs, (out_ref, cube, mid) = refs[:len(tables)], refs[len(tables):]
+        me = lax.axis_index("grid")
+        for d, ref in enumerate(piece_refs):
+            start = pl.multiple_of(jnp.bitwise_xor(me, d) * piece_rows, 8)
+            cube[pl.ds(start, piece_rows), :] = ref[...].astype(f32)
+        solve(plan, cube, *table_refs, mid)
+        own = jnp.broadcast_to(at_ref[pl.ds(me, 1), :], (part + 1, lanes))
+        last = iota((part + 1, lanes), 0) == part
+        for g in range(grid_count):
+            for s in range(slab_count):
+                first = g * piece_rows + s * part
+                out_ref[s * grid_count + g] = jnp.where(last, own, cube[first:first + part + 1, :]).astype(bf16)
+
+    return pl.pallas_call(
+        kernel,
+        out_shape=jax.ShapeDtypeStruct((slab_count * grid_count, part + 1, lanes), bf16),
+        in_specs=[whole] * (1 + grid_count + len(tables)),
+        out_specs=whole,
+        scratch_shapes=[
+            pltpu.VMEM((plan.rows + 8, lanes), f32),
+            pltpu.VMEM((plan.edge * plan.half, lanes), f32),
+        ],
+        compiler_params=params(24),
+        name="potentials",
+    )(at, *pieces, *tables)
+
+
+def apply_part(orbitals, targets, received, slab_count):
+    occupied, shard_len = orbitals.shape
+    count = targets.shape[0]
+    points, part = received.shape[0], received.shape[1] - 1
+    keep = count // slab_count
+    pitch = -(-(part + 1) // 8) * 8
+    prefactor = -1.0 / math.sqrt(points)
+
+    def kernel(targets_ref, orbitals_ref, received_ref, out_ref, spread, mid):
+        for m in range(points):
+            spread[m * pitch:m * pitch + part + 1, :] = received_ref[m].astype(f32)
+        at = spread[pl.ds(part, points, stride=pitch), :][:, :occupied].astype(bf16)
+        first = pl.multiple_of(lax.axis_index("slab") * (part * lanes), lanes)
+        density = jnp.dot(at, orbitals_ref[:, pl.ds(first, part * lanes)], preferred_element_type=f32)
+        rows, columns = iota((count, occupied), 0), iota((count, occupied), 1)
+        chosen = jnp.zeros((count, occupied), f32)
+        for k in range(count):
+            chosen = jnp.where((rows == k) & (columns == targets_ref[k]), 1.0, chosen)
+        target_points = lax.dot_general(
+            chosen.astype(bf16), at, contract_last, preferred_element_type=f32).astype(bf16)
+        potential = jnp.concatenate([spread[pl.ds(r, points, stride=pitch), :] for r in range(part)], axis=1)
+        weighted = (potential * (density * (1.0 / math.sqrt(occupied)))).astype(bf16)
+        applied = jnp.dot(target_points, weighted, preferred_element_type=f32) * prefactor
+        for r in range(part):
+            mid[r * count:(r + 1) * count, :] = applied[:, r * lanes:(r + 1) * lanes]
+        for s in range(slab_count):
+            for k in range(keep):
+                out_ref[s, pl.ds(k, part, stride=keep), :] = mid[pl.ds(s * keep + k, part, stride=count), :]
+
+    return pl.pallas_call(
+        kernel,
+        out_shape=jax.ShapeDtypeStruct((slab_count, part * keep, lanes), f32),
+        in_specs=[scalars, whole, whole],
+        out_specs=whole,
+        scratch_shapes=[pltpu.VMEM((points * pitch, lanes), f32), pltpu.VMEM((part * count, lanes), f32)],
+        compiler_params=params(16),
+        name="apply_part",
+    )(targets, orbitals, received)
+
+
+def exchange(value, grid_count, offset):
+    return lax.ppermute(value, "grid", [(i, i ^ offset) for i in range(grid_count)])
+
+
+def quick_body(orbitals, targets, points, fit):
+    grid_count, slab_count = lax.axis_size("grid"), lax.axis_size("slab")
+    shard_len = orbitals.shape[1]
+    edge = round((shard_len * grid_count) ** (1 / 3))
+    keep = targets.shape[0] // slab_count
+    plan = Plan(edge)
+    share = read_points(orbitals, points)
+    shares = [share] + [exchange(share, grid_count, d) for d in range(1, grid_count)]
+    *pieces, at = fit_pairs(orbitals, targets, fit, shares)
+    pieces = pieces[:1] + [exchange(pieces[d], grid_count, d) for d in range(1, grid_count)]
+    sent = potentials(plan, pieces, at, slab_count)
+    received = lax.all_to_all(sent, everyone, 0, 0)
+    blocks = apply_part(orbitals, targets, received, slab_count)
+    kept = lax.all_to_all(blocks, "slab", 0, 0)
+    kept = kept.reshape(-1, keep, lanes)
+    return jnp.transpose(kept, (1, 0, 2)).reshape(keep, shard_len)
+
+
+def quick_fits(mesh, orbitals, targets, points, fit):
+    grid_count, slab_count = mesh.shape["grid"], mesh.shape["slab"]
+    occupied, cells = orbitals.shape
+    group, edge = fit.shape[1], round(cells ** (1 / 3))
+    shard_rows = cells // grid_count // lanes
+    return (
+        group == grid_count
+        and 2 * group == 8
+        and occupied <= lanes
+        and occupied % 16 == 0
+        and edge ** 3 == cells
+        and edge % 16 == 0
+        and edge <= lanes // 2
+        and cells % (grid_count * lanes) == 0
+        and shard_rows % 8 == 0
+        and shard_rows % slab_count == 0
+        and targets.shape[0] % slab_count == 0
+        and targets.shape[0] % 8 == 0
+    )
+
+
 def solution(mesh):
     in_specs = (P(None, "grid"), P(), P("slab"), P("slab", None))
     out_specs = P("slab", "grid")
-    return jax.shard_map(body, mesh=mesh, in_specs=in_specs, out_specs=out_specs, check_vma=False)
+
+    def run(*arrays):
+        body = quick_body if quick_fits(mesh, *arrays) else plain_body
+        return jax.shard_map(body, mesh=mesh, in_specs=in_specs, out_specs=out_specs, check_vma=False)(*arrays)
+
+    return run

time: 132 us -> 48.4 us (0.37)
  matrix products: 31.2 us -> 0 us
  blocking collectives: 49.9 us -> 26.9 us
  other arithmetic: 18 us -> 0 us
  local copies, waits for them, and re-layouts: 18.4 us -> 4.84 us
  Pallas kernels: 0 us -> 5.24 us
  starting transfers between devices: 9.84 us -> 5.05 us
  waiting for transfers between devices: 3.49 us -> 6.09 us
    dot_general x27 -> x0, matrix products: 31.2 us -> none  [the longest x18 17.8 us: apply_axis(): jnp.einsum(pattern, values, matrix, precision=careful, preferred_element_...]
    all_gather x1 -> x0, blocking collectives: 21 us -> none  [body(): all_targets = lax.all_gather(target_points, 'slab', axis=1, tiled=True)]
    all_to_all x2 -> x0, starting transfers between devices: 9.84 us -> none  [the longest x1 5.83 us: body(): lax.all_to_all(weighted, 'slab', split_axis=1, concat_axis=0, tiled=True)]
    psum x1 -> x0, blocking collectives: 8.88 us -> none  [body(): at_points = lax.psum(point_terms, 'grid').astype(jnp.bfloat16)]
    all_to_all x2, blocking collectives: 20 us -> 26.9 us  [the longest x1 15.7 us: quick_body(): received = lax.all_to_all(sent, everyone, 0, 0)]
    ppermute x0 -> x6, waiting for transfers between devices: none -> 6.09 us  [exchange(): lax.ppermute(value, 'grid', [(i, i ^ offset) for i in range(grid_count)])]
    all_to_all x2 -> x0, other arithmetic: 5.52 us -> none  [body(): lax.all_to_all(fitted, 'grid', split_axis=0, concat_axis=1, tiled=True)]
    pallas_call x0 -> x4, Pallas kernels: none -> 5.24 us  [the longest x1 2 us: potentials(): pl.pallas_call(kernel, out_shape=jax.ShapeDtypeStruct((slab_count * grid_...]
  transfers between devices with their start and end apart: 2 -> 6, of which waited for: 1 -> 4; matrix products, arithmetic and copies ran while one was open for 2% -> 0% of each run, Pallas kernels for 0% -> 0%
where the time goes in v1:
time: 48.4 us; the launch traced here: 48.2 us
  blocking collectives  26.9 us (56%)
  waiting for transfers between devices  6.09 us (13%)
  Pallas kernels  5.24 us (11%)
  starting transfers between devices  5.05 us (10%)
  local copies, waits for them, and re-layouts  4.84 us (10%)
    all_to_all x1, blocking collectives, quick_body(): received = lax.all_to_all(sent, everyone, 0, 0)  15.7 us
    all_to_all x1, blocking collectives, quick_body(): kept = lax.all_to_all(blocks, 'slab', 0, 0)  11.2 us
    ppermute x6, waiting for transfers between devices, exchange(): lax.ppermute(value, 'grid', [(i, i ^ offset) for i in range(grid_count)])  6.09 us
    ppermute x6, starting transfers between devices, exchange(): lax.ppermute(value, 'grid', [(i, i ^ offset) for i in range(grid_count)])  5.05 us
    unnamed x24, local copies, waits for them, and re-layouts  4.03 us
    pallas_call x1, Pallas kernels, potentials(): pl.pallas_call(kernel, out_shape=jax.ShapeDtypeStruct((slab_count * grid_...  2 us
    pallas_call x1, Pallas kernels, fit_pairs(): pl.pallas_call(kernel, out_shape=[piece] * group + [jax.ShapeDtypeStruct(...  1.37 us
    pallas_call x1, Pallas kernels, apply_part(): pl.pallas_call(kernel, out_shape=jax.ShapeDtypeStruct((slab_count, part *...  1.09 us
  transfers between devices with their start and end apart: 6, of which 4 were waited for; matrix products, arithmetic and copies ran while one was open for 0% of the time, Pallas kernels for 0%

profile of v1, /device:TPU:0, one launch (start us, length us, event | category | flops | bytes accessed | tf_op | source)
XLA Modules:
  0.0 48.2 jit_solution(11374489738921385755)
XLA Ops:
  0.0 0.0 copy-start
  0.0 2.0 %copy-done = bf16[64,27648]{1,0:T(8,128)(2,1)S(1)} copy-done((bf16[64,27648]{1,0:T(8,128)(2,1)S(1)}, bf16[64,27648]{1,0:T(8,128)(2,1)}, u32[]{:S(2)}) %copy-start) | copy-done | bytes 3538968
  2.0 0.0 copy-start.11
  2.0 0.7 %copy-done.11 = s32[4]{0:T(128)S(1)} copy-done((s32[4]{0:T(128)S(1)}, s32[4]{0:T(128)}, u32[]{:S(2)}) %copy-start.11) | copy-done | bytes 40
  2.7 0.0 copy-start.1
  2.7 0.0 copy-start.2
  2.7 0.0 copy-start.3
  2.7 0.0 copy-start.4
  2.7 0.0 copy-start.5
  2.7 0.0 copy-start.6
  2.7 0.0 copy-start.7
  2.7 0.8 %read_points.1.refs_0_ = f32[8,128]{1,0:T(8,128)S(1)} custom-call(s32[4]{0:T(128)S(1)} %copy-done.11, bf16[64,27648]{1,0:T(8,128)(2,1)S(1)} %copy-done), custom_call_target="tpu_custom_call" | custom-call | tf_op jit(solution)/shard_map/read_points/pallas_call | solution.py:291
  3.5 2.4 %collective-permute-start.2 = (f32[8,128]{1,0:T(8,128)S(1)}, f32[8,128]{1,0:T(8,128)S(1)}, u32[]{:S(2)}, u32[]{:S(2)}) collective-permute-start(f32[8,128]{1,0:T(8,128)S(1)} %read_points.1.refs_0_), channel_id=1, source_target_pairs={{0,3},{1,2},{2,1},{3,0},{4,7},{5,6},{6,5},{7,4},{8,11},{9,10},{10,... | collective-permute-start | bytes 12296 | tf_op jit(solution)/shard_map/ppermute | solution.py:431
  6.0 0.6 %collective-permute-start.1 = (f32[8,128]{1,0:T(8,128)S(1)}, f32[8,128]{1,0:T(8,128)S(1)}, u32[]{:S(2)}, u32[]{:S(2)}) collective-permute-start(f32[8,128]{1,0:T(8,128)S(1)} %read_points.1.refs_0_), channel_id=1, source_target_pairs={{0,2},{1,3},{2,0},{3,1},{4,6},{5,7},{6,4},{7,5},{8,10},{9,11},{10,... | collective-permute-start | bytes 12296 | tf_op jit(solution)/shard_map/ppermute | solution.py:431
  6.6 0.0 collective-permute-start
  6.6 0.6 %collective-permute-done.2.refs_3_ = f32[8,128]{1,0:T(8,128)S(1)} collective-permute-done((f32[8,128]{1,0:T(8,128)S(1)}, f32[8,128]{1,0:T(8,128)S(1)}, u32[]{:S(2)}, u32[]{:S(2)}) %collective-permute-start.2) | collective-permute-done | bytes 4128 | tf_op jit(solution)/shard_map/ppermute | solution.py:431
  7.3 2.3 %collective-permute-done.1.refs_2_ = f32[8,128]{1,0:T(8,128)S(1)} collective-permute-done((f32[8,128]{1,0:T(8,128)S(1)}, f32[8,128]{1,0:T(8,128)S(1)}, u32[]{:S(2)}, u32[]{:S(2)}) %collective-permute-start.1) | collective-permute-done | bytes 4128 | tf_op jit(solution)/shard_map/ppermute | solution.py:431
  9.6 0.0 collective-permute-done.refs_1_
  9.6 0.0 copy-done.1
  9.6 0.0 copy-start.8
  9.6 0.7 %copy-done.8 = f32[4,4]{1,0:T(4,128)S(1)} copy-done((f32[4,4]{1,0:T(4,128)S(1)}, f32[4,4]{1,0:T(4,128)}, u32[]{:S(2)}) %copy-start.8) | copy-done | bytes 88
  10.2 0.0 copy-start.9
  10.3 0.7 %copy-done.9 = s32[16]{0:T(128)S(1)} copy-done((s32[16]{0:T(128)S(1)}, s32[16]{0:T(128)}, u32[]{:S(2)}) %copy-start.9) | copy-done | bytes 88
  10.9 0.0 copy-start.10
  10.9 1.4 %fit_pairs.1 = (bf16[216,128]{1,0:T(8,128)(2,1)S(1)}, bf16[216,128]{1,0:T(8,128)(2,1)S(1)}, bf16[216,128]{1,0:T(8,128)(2,1)S(1)}, bf16[216,128]{1,0:T(8,128)(2,1)S(1)}, f32[8,128]{1,0:T(8,128)S(1)}) custom-call(s32[16]{0:T(128)S(1)} %copy-done.9, f32[4,4]{1,0:T(4,128)S(1)} %copy-done.8, bf16[64,27648]{1,0:T(8,128)(2,1)S(1)} %copy-done.1, ...), custom_call_target="tpu_custom_call" | custom-call | tf_op jit(solution)/shard_map/fit_pairs/pallas_call | solution.py:345
  12.3 0.1 collective-permute-start.3
  12.4 0.7 %collective-permute-start.4 = (bf16[216,128]{1,0:T(8,128)(2,1)S(1)}, bf16[216,128]{1,0:T(8,128)(2,1)S(1)}, u32[]{:S(2)}, u32[]{:S(2)}) collective-permute-start(bf16[216,128]{1,0:T(8,128)(2,1)S(1)} %get-tuple-element.13), channel_id=1, source_target_pairs={{0,2},{1,3},{2,0},{3,1},{4,6},{5,7},{6,4},{7,5},{8,10},{9,11},{10,... | collective-permute-start | bytes 165896 | tf_op jit(solution)/shard_map/ppermute | solution.py:431
  13.1 1.2 %collective-permute-start.5 = (bf16[216,128]{1,0:T(8,128)(2,1)S(1)}, bf16[216,128]{1,0:T(8,128)(2,1)S(1)}, u32[]{:S(2)}, u32[]{:S(2)}) collective-permute-start(bf16[216,128]{1,0:T(8,128)(2,1)S(1)} %get-tuple-element.14), channel_id=1, source_target_pairs={{0,3},{1,2},{2,1},{3,0},{4,7},{5,6},{6,5},{7,4},{8,11},{9,10},{10,... | collective-permute-start | bytes 165896 | tf_op jit(solution)/shard_map/ppermute | solution.py:431
  14.2 0.0 collective-permute-done.3.refs_1_
  14.2 2.9 %collective-permute-done.4.refs_2_ = bf16[216,128]{1,0:T(8,128)(2,1)S(1)} collective-permute-done((bf16[216,128]{1,0:T(8,128)(2,1)S(1)}, bf16[216,128]{1,0:T(8,128)(2,1)S(1)}, u32[]{:S(2)}, u32[]{:S(2)}) %collective-permute-start.4) | collective-permute-done | bytes 55328 | tf_op jit(solution)/shard_map/ppermute | solution.py:431
  17.1 0.3 collective-permute-done.5.refs_3_
  17.4 0.0 copy-done.2
  17.4 0.0 copy-done.3
  17.4 0.0 copy-done.4
  17.4 0.0 copy-done.5
  17.4 0.0 copy-done.6
  17.4 0.0 copy-done.7
  17.4 2.0 %potentials.1 = bf16[32,28,128]{2,1,0:T(8,128)(2,1)S(1)} custom-call(f32[8,128]{1,0:T(8,128)S(1)} %get-tuple-element.10.at_ref, bf16[216,128]{1,0:T(8,128)(2,1)S(1)} %get-tuple-element.11.refs_0_, bf16[216,128]{1,0:T(8,128)(2,1)S(1)} %collective-permute-done.3.refs_1_, bf16[216,128]{1,0:T(8,128)(2,1)S(1)} %collective-permute-done.4.refs_2_, ...), custom_call_target="tpu_custom_call" | custom-call | tf_op jit(solution)/shard_map/potentials/pallas_call | solution.py:376
  19.4 15.7 %all_to_all.10.received_ref = bf16[32,28,128]{2,1,0:T(8,128)(2,1)S(1)} all-to-all(bf16[32,28,128]{2,1,0:T(8,128)(2,1)S(1)} %potentials.1), channel_id=1, replica_groups=mesh['slab'=8,'grid'=4] {'slab','grid'}, dimensions={0} | all-to-all | bytes 458752 | tf_op jit(solution)/shard_map/all_to_all | solution.py:445
  35.1 0.0 copy-done.10
  35.1 1.1 %apply_part.1 = f32[8,54,128]{2,1,0:T(8,128)S(1)} custom-call(s32[16]{0:T(128)S(1)} %copy-done.10, bf16[64,27648]{1,0:T(8,128)(2,1)S(1)} %copy-done.1, bf16[32,28,128]{2,1,0:T(8,128)(2,1)S(1)} %all_to_all.10.received_ref), custom_call_target="tpu_custom_call" | custom-call | tf_op jit(solution)/shard_map/apply_part/pallas_call | solution.py:419
  36.2 11.2 %all_to_all.11 = f32[8,54,128]{2,1,0:T(8,128)S(1)} all-to-all(f32[8,54,128]{2,1,0:T(8,128)S(1)} %apply_part.1), channel_id=1, replica_groups=mesh['slab'=8,'grid'=4] {'slab'}, dimensions={0} | all-to-all | bytes 442368 | tf_op jit(solution)/shard_map/all_to_all | solution.py:447
  47.4 0.8 %reshape.6 = f32[216,2,128]{2,1,0:T(2,128)} reshape(f32[8,54,128]{2,1,0:T(8,128)S(1)} %all_to_all.11) | data formatting | bytes 442368 | tf_op jit(solution)/shard_map/reshape | solution.py:448
Async XLA Ops:
  0.0 2.0 %copy-start = (bf16[64,27648]{1,0:T(8,128)(2,1)S(1)}, bf16[64,27648]{1,0:T(8,128)(2,1)}, u32[]{:S(2)}) copy-start(bf16[64,27648]{1,0:T(8,128)(2,1)} %orbitals_ref.5) | copy-start | bytes 10616836
  2.0 0.7 %copy-start.11 = (s32[4]{0:T(128)S(1)}, s32[4]{0:T(128)}, u32[]{:S(2)}) copy-start(s32[4]{0:T(128)} %points_ref.1) | copy-start | bytes 52
  2.7 6.9 %copy-start.1 = (bf16[64,27648]{1,0:T(8,128)(2,1)S(1)}, bf16[64,27648]{1,0:T(8,128)(2,1)}, u32[]{:S(2)}) copy-start(bf16[64,27648]{1,0:T(8,128)(2,1)} %orbitals_ref.5) | copy-start | bytes 10616836
  2.7 14.7 %copy-start.2 = (bf16[1536,256]{1,0:T(8,128)(2,1)S(1)}, bf16[1536,256]{1,0:T(8,128)(2,1)}, u32[]{:S(2)}) copy-start(bf16[1536,256]{1,0:T(8,128)(2,1)} %constant.14.clone.refs_6_) | copy-start | bytes 2359300
  2.7 14.7 %copy-start.3 = (bf16[1536,256]{1,0:T(8,128)(2,1)S(1)}, bf16[1536,256]{1,0:T(8,128)(2,1)}, u32[]{:S(2)}) copy-start(bf16[1536,256]{1,0:T(8,128)(2,1)} %constant.13.clone.refs_5_) | copy-start | bytes 2359300
  2.7 14.7 %copy-start.4 = (bf16[1280,256]{1,0:T(8,128)(2,1)S(1)}, bf16[1280,256]{1,0:T(8,128)(2,1)}, u32[]{:S(2)}) copy-start(bf16[1280,256]{1,0:T(8,128)(2,1)} %constant.16.clone.refs_8_) | copy-start | bytes 1966084
  2.7 14.7 %copy-start.5 = (bf16[1280,256]{1,0:T(8,128)(2,1)S(1)}, bf16[1280,256]{1,0:T(8,128)(2,1)}, u32[]{:S(2)}) copy-start(bf16[1280,256]{1,0:T(8,128)(2,1)} %constant.15.clone.refs_7_) | copy-start | bytes 1966084
  2.7 14.7 %copy-start.6 = (f32[24,48,128]{2,1,0:T(8,128)S(1)}, f32[24,48,128]{2,1,0:T(8,128)}, u32[]{:S(2)}) copy-start(f32[24,48,128]{2,1,0:T(8,128)} %constant.17.clone.refs_9_) | copy-start | bytes 1769476
  2.7 14.7 %copy-start.7 = (bf16[48,144]{1,0:T(8,128)(2,1)S(1)}, bf16[48,144]{1,0:T(8,128)(2,1)}, u32[]{:S(2)}) copy-start(bf16[48,144]{1,0:T(8,128)(2,1)} %constant.12.clone.refs_4_) | copy-start | bytes 41476
  3.5 3.8 %collective-permute-start.2 = (f32[8,128]{1,0:T(8,128)S(1)}, f32[8,128]{1,0:T(8,128)S(1)}, u32[]{:S(2)}, u32[]{:S(2)}) collective-permute-start(f32[8,128]{1,0:T(8,128)S(1)} %read_points.1.refs_0_), channel_id=1, source_target_pairs={{0,3},{1,2},{2,1},{3,0},{4,7},{5,6},{6,5},{7,4},{8,11},{9,10},{10,... | collective-permute-start | bytes 12296 | tf_op jit(solution)/shard_map/ppermute | solution.py:431
  6.0 3.6 %collective-permute-start.1 = (f32[8,128]{1,0:T(8,128)S(1)}, f32[8,128]{1,0:T(8,128)S(1)}, u32[]{:S(2)}, u32[]{:S(2)}) collective-permute-start(f32[8,128]{1,0:T(8,128)S(1)} %read_points.1.refs_0_), channel_id=1, source_target_pairs={{0,2},{1,3},{2,0},{3,1},{4,6},{5,7},{6,4},{7,5},{8,10},{9,11},{10,... | collective-permute-start | bytes 12296 | tf_op jit(solution)/shard_map/ppermute | solution.py:431
  6.6 3.0 %collective-permute-start = (f32[8,128]{1,0:T(8,128)S(1)}, f32[8,128]{1,0:T(8,128)S(1)}, u32[]{:S(2)}, u32[]{:S(2)}) collective-permute-start(f32[8,128]{1,0:T(8,128)S(1)} %read_points.1.refs_0_), channel_id=1, source_target_pairs={{0,1},{1,0},{2,3},{3,2},{4,5},{5,4},{6,7},{7,6},{8,9},{9,8},{10,11... | collective-permute-start | bytes 12296 | tf_op jit(solution)/shard_map/ppermute | solution.py:431
  9.6 0.7 %copy-start.8 = (f32[4,4]{1,0:T(4,128)S(1)}, f32[4,4]{1,0:T(4,128)}, u32[]{:S(2)}) copy-start(f32[4,4]{1,0:T(4,128)} %fit_ref.1) | copy-start | bytes 196
  10.2 0.7 %copy-start.9 = (s32[16]{0:T(128)S(1)}, s32[16]{0:T(128)}, u32[]{:S(2)}) copy-start(s32[16]{0:T(128)} %targets_ref.3) | copy-start | bytes 196
  10.9 24.2 %copy-start.10 = (s32[16]{0:T(128)S(1)}, s32[16]{0:T(128)}, u32[]{:S(2)}) copy-start(s32[16]{0:T(128)} %targets_ref.3) | copy-start | bytes 196
  12.3 1.9 %collective-permute-start.3 = (bf16[216,128]{1,0:T(8,128)(2,1)S(1)}, bf16[216,128]{1,0:T(8,128)(2,1)S(1)}, u32[]{:S(2)}, u32[]{:S(2)}) collective-permute-start(bf16[216,128]{1,0:T(8,128)(2,1)S(1)} %get-tuple-element.12), channel_id=1, source_target_pairs={{0,1},{1,0},{2,3},{3,2},{4,5},{5,4},{6,7},{7,6},{8,9},{9,8},{10,11... | collective-permute-start | bytes 165896 | tf_op jit(solution)/shard_map/ppermute | solution.py:431
  12.4 4.7 %collective-permute-start.4 = (bf16[216,128]{1,0:T(8,128)(2,1)S(1)}, bf16[216,128]{1,0:T(8,128)(2,1)S(1)}, u32[]{:S(2)}, u32[]{:S(2)}) collective-permute-start(bf16[216,128]{1,0:T(8,128)(2,1)S(1)} %get-tuple-element.13), channel_id=1, source_target_pairs={{0,2},{1,3},{2,0},{3,1},{4,6},{5,7},{6,4},{7,5},{8,10},{9,11},{10,... | collective-permute-start | bytes 165896 | tf_op jit(solution)/shard_map/ppermute | solution.py:431
  13.1 4.3 %collective-permute-start.5 = (bf16[216,128]{1,0:T(8,128)(2,1)S(1)}, bf16[216,128]{1,0:T(8,128)(2,1)S(1)}, u32[]{:S(2)}, u32[]{:S(2)}) collective-permute-start(bf16[216,128]{1,0:T(8,128)(2,1)S(1)} %get-tuple-element.14), channel_id=1, source_target_pairs={{0,3},{1,2},{2,1},{3,0},{4,7},{5,6},{6,5},{7,4},{8,11},{9,10},{10,... | collective-permute-start | bytes 165896 | tf_op jit(solution)/shard_map/ppermute | solution.py:431

commit v2 on v1

--- a/solution.py
+++ b/solution.py
@@ -254,23 +254,32 @@
 
 
 whole = pl.BlockSpec(memory_space=pltpu.VMEM)
-scalars = pl.BlockSpec(memory_space=pltpu.SMEM)
-anywhere = pl.BlockSpec(memory_space=pl.ANY)
+far = pl.BlockSpec(memory_space=pltpu.HBM)
 
 
 def iota(shape, axis):
     return lax.broadcasted_iota(jnp.int32, shape, axis)
 
 
-def read_points(orbitals, points):
+def read_points(orbitals, targets, points, fit):
     occupied, shard_len = orbitals.shape
-    group = points.shape[0]
-
-    def kernel(points_ref, orbitals_ref, out_ref, tiles, sems):
-        base = lax.axis_index("grid") * shard_len
+    count, group = targets.shape[0], points.shape[0]
+    scale = 1.0 / math.sqrt(occupied) / math.sqrt(count)
+
+    def kernel(points_hbm, targets_hbm, fit_hbm, orbitals_ref, out_ref, notes_ref, points_ref, targets_ref, fit_ref, tiles, sems):
+        small = [
+            pltpu.make_async_copy(source, place, sems.at[group + i])
+            for i, (source, place) in enumerate(
+                ((points_hbm, points_ref), (targets_hbm, targets_ref), (fit_hbm, fit_ref)))
+        ]
+        for copy in small:
+            copy.start()
+        me = lax.axis_index("grid")
+        base = me * shard_len
         rows, columns = iota((8, group * lanes), 0), iota((8, group * lanes), 1)
         chosen = jnp.zeros((8, group * lanes), f32)
         copies = []
+        small[0].wait()
         for m in range(group):
             local = points_ref[m] - base
             inside = (local >= 0) & (local < shard_len)
@@ -282,53 +291,69 @@
             copies.append(copy)
             column = jnp.where(inside, local - first + m * lanes, -1)
             chosen = jnp.where((rows == m) & (columns == column), 1.0, chosen)
-        for copy in copies:
-            copy.wait()
         chosen = jnp.concatenate([chosen, jnp.zeros_like(chosen)], axis=0).astype(bf16)
-        out = lax.dot_general(chosen, tiles[...], contract_last, preferred_element_type=f32)
-        out_ref[...] = jnp.concatenate([out[:8], jnp.zeros((8, lanes - occupied), f32)], axis=1)
-
-    return pl.pallas_call(
-        kernel,
-        out_shape=jax.ShapeDtypeStruct((8, lanes), f32),
-        in_specs=[scalars, anywhere],
-        out_specs=whole,
-        scratch_shapes=[pltpu.VMEM((occupied, group * lanes), bf16), pltpu.SemaphoreType.DMA((group,))],
-        compiler_params=params(4),
-        name="read_points",
-    )(points, orbitals)
-
-
-def fit_pairs(orbitals, targets, fit, shares):
-    occupied, shard_len = orbitals.shape
-    count, group = targets.shape[0], fit.shape[0]
-    shard_rows = shard_len // lanes
-    step = shard_rows // 8
-    scale = 1.0 / math.sqrt(occupied) / math.sqrt(count)
-
-    def kernel(targets_ref, fit_ref, orbitals_ref, *refs):
-        share_refs, out_refs, at_ref, mid = refs[:group], refs[group:2 * group], refs[2 * group], refs[2 * group + 1]
-        me = lax.axis_index("grid")
-        at = share_refs[0][...]
-        for ref in share_refs[1:]:
-            at = at + ref[...]
-        at_ref[...] = at
+        small[1].wait()
+        small[2].wait()
         rows, columns = iota((8, lanes), 0), iota((8, lanes), 1)
         counts = jnp.zeros((8, lanes), f32)
         for k in range(count):
             counts = counts + jnp.where(columns == targets_ref[k], 1.0, 0.0)
-        twice = jnp.where(rows < group, at, pltpu.roll(at, group, 0))
-        weighted = counts * twice
-        upper = weighted.astype(bf16).astype(f32)
-        left = jnp.concatenate([twice, upper, weighted - upper, jnp.zeros((8, lanes), f32)], axis=0)
-        left = left.astype(bf16)[:, :occupied]
-        coefficients = []
+        notes_ref[:8, :] = counts
         for j in range(group):
             value = jnp.zeros((8, lanes), f32)
             for r in range(8):
                 d = r % group
                 value = jnp.where(rows == r, fit_ref[(d + j) % group, jnp.bitwise_xor(me, d)], value)
-            coefficients.append(value * scale)
+            notes_ref[8 + 8 * j:16 + 8 * j, :] = value * scale
+        rows, columns = iota((count, lanes), 0), iota((count, lanes), 1)
+        ones = jnp.zeros((count, lanes), f32)
+        for k in range(count):
+            ones = jnp.where((rows == k) & (columns == targets_ref[k]), 1.0, ones)
+        notes_ref[8 + 8 * group:, :] = ones
+        for copy in copies:
+            copy.wait()
+        out = lax.dot_general(chosen, tiles[...], contract_last, preferred_element_type=f32)
+        out_ref[...] = jnp.concatenate([out[:8], jnp.zeros((8, lanes - occupied), f32)], axis=1)
+
+    return pl.pallas_call(
+        kernel,
+        out_shape=[
+            jax.ShapeDtypeStruct((8, lanes), f32),
+            jax.ShapeDtypeStruct((8 + 8 * group + count, lanes), f32),
+        ],
+        in_specs=[far] * 4,
+        out_specs=[whole] * 2,
+        scratch_shapes=[
+            pltpu.SMEM(points.shape, jnp.int32),
+            pltpu.SMEM(targets.shape, jnp.int32),
+            pltpu.SMEM(fit.shape, f32),
+            pltpu.VMEM((occupied, group * lanes), bf16),
+            pltpu.SemaphoreType.DMA((group + 3,)),
+        ],
+        compiler_params=params(60),
+        name="read_points",
+    )(points, targets, fit, orbitals)
+
+
+def fit_pairs(orbitals, notes, shares):
+    occupied, shard_len = orbitals.shape
+    group = len(shares)
+    shard_rows = shard_len // lanes
+    step = shard_rows // 8
+
+    def kernel(notes_ref, orbitals_ref, *refs):
+        share_refs, out_refs, at_ref, mid = refs[:group], refs[group:2 * group], refs[2 * group], refs[2 * group + 1]
+        at = share_refs[0][...]
+        for ref in share_refs[1:]:
+            at = at + ref[...]
+        at_ref[...] = at
+        rows = iota((8, lanes), 0)
+        twice = jnp.where(rows < group, at, pltpu.roll(at, group, 0))
+        weighted = notes_ref[:8, :] * twice
+        upper = weighted.astype(bf16).astype(f32)
+        left = jnp.concatenate([twice, upper, weighted - upper, jnp.zeros((8, lanes), f32)], axis=0)
+        left = left.astype(bf16)[:, :occupied]
+        coefficients = [notes_ref[8 + 8 * j:16 + 8 * j, :] for j in range(group)]
         for c in range(0, shard_rows, step):
             product = jnp.dot(left, orbitals_ref[:, c * lanes:(c + step) * lanes], preferred_element_type=f32)
             for r in range(step):
@@ -345,12 +370,12 @@
     return pl.pallas_call(
         kernel,
         out_shape=[piece] * group + [jax.ShapeDtypeStruct((8, lanes), f32)],
-        in_specs=[scalars, scalars, whole] + [whole] * group,
+        in_specs=[whole] * (2 + group),
         out_specs=[whole] * (group + 1),
         scratch_shapes=[pltpu.VMEM((shard_rows * 8, lanes), f32)],
         compiler_params=params(16),
         name="fit_pairs",
-    )(targets, fit, orbitals, *shares)
+    )(notes, orbitals, *shares)
 
 
 def potentials(plan, pieces, at, slab_count):
@@ -387,26 +412,21 @@
     )(at, *pieces, *tables)
 
 
-def apply_part(orbitals, targets, received, slab_count):
+def apply_part(orbitals, notes, received, count, slab_count):
     occupied, shard_len = orbitals.shape
-    count = targets.shape[0]
     points, part = received.shape[0], received.shape[1] - 1
     keep = count // slab_count
     pitch = -(-(part + 1) // 8) * 8
     prefactor = -1.0 / math.sqrt(points)
 
-    def kernel(targets_ref, orbitals_ref, received_ref, out_ref, spread, mid):
+    def kernel(notes_ref, orbitals_ref, received_ref, out_ref, spread, mid, stage):
         for m in range(points):
             spread[m * pitch:m * pitch + part + 1, :] = received_ref[m].astype(f32)
         at = spread[pl.ds(part, points, stride=pitch), :][:, :occupied].astype(bf16)
         first = pl.multiple_of(lax.axis_index("slab") * (part * lanes), lanes)
         density = jnp.dot(at, orbitals_ref[:, pl.ds(first, part * lanes)], preferred_element_type=f32)
-        rows, columns = iota((count, occupied), 0), iota((count, occupied), 1)
-        chosen = jnp.zeros((count, occupied), f32)
-        for k in range(count):
-            chosen = jnp.where((rows == k) & (columns == targets_ref[k]), 1.0, chosen)
-        target_points = lax.dot_general(
-            chosen.astype(bf16), at, contract_last, preferred_element_type=f32).astype(bf16)
+        chosen = notes_ref[notes_ref.shape[0] - count:, :][:, :occupied].astype(bf16)
+        target_points = lax.dot_general(chosen, at, contract_last, preferred_element_type=f32).astype(bf16)
         potential = jnp.concatenate([spread[pl.ds(r, points, stride=pitch), :] for r in range(part)], axis=1)
         weighted = (potential * (density * (1.0 / math.sqrt(occupied)))).astype(bf16)
         applied = jnp.dot(target_points, weighted, preferred_element_type=f32) * prefactor
@@ -414,17 +434,42 @@
             mid[r * count:(r + 1) * count, :] = applied[:, r * lanes:(r + 1) * lanes]
         for s in range(slab_count):
             for k in range(keep):
-                out_ref[s, pl.ds(k, part, stride=keep), :] = mid[pl.ds(s * keep + k, part, stride=count), :]
+                stage[s, k * part:(k + 1) * part, :] = mid[pl.ds(s * keep + k, part, stride=count), :]
+            out_ref[s] = stage[s].astype(bf16)
 
     return pl.pallas_call(
         kernel,
-        out_shape=jax.ShapeDtypeStruct((slab_count, part * keep, lanes), f32),
-        in_specs=[scalars, whole, whole],
+        out_shape=jax.ShapeDtypeStruct((slab_count, keep * part, lanes), bf16),
+        in_specs=[whole] * 3,
         out_specs=whole,
-        scratch_shapes=[pltpu.VMEM((points * pitch, lanes), f32), pltpu.VMEM((part * count, lanes), f32)],
+        scratch_shapes=[
+            pltpu.VMEM((points * pitch, lanes), f32),
+            pltpu.VMEM((part * count, lanes), f32),
+            pltpu.VMEM((slab_count, keep * part, lanes), f32),
+        ],
         compiler_params=params(16),
         name="apply_part",
-    )(targets, orbitals, received)
+    )(notes, orbitals, received)
+
+
+def settle(kept, keep):
+    slab_count, part = kept.shape[0], kept.shape[1] // keep
+
+    def kernel(kept_ref, out_ref, stage):
+        for s in range(slab_count):
+            stage[s] = kept_ref[s].astype(f32)
+            for k in range(keep):
+                out_ref[s * part:(s + 1) * part, k, :] = stage[s, k * part:(k + 1) * part, :]
+
+    return pl.pallas_call(
+        kernel,
+        out_shape=jax.ShapeDtypeStruct((slab_count * part, keep, lanes), f32),
+        in_specs=[whole],
+        out_specs=whole,
+        scratch_shapes=[pltpu.VMEM(kept.shape, f32)],
+        compiler_params=params(4),
+        name="settle",
+    )(kept)
 
 
 def exchange(value, grid_count, offset):
@@ -437,16 +482,15 @@
     edge = round((shard_len * grid_count) ** (1 / 3))
     keep = targets.shape[0] // slab_count
     plan = Plan(edge)
-    share = read_points(orbitals, points)
+    share, notes = read_points(orbitals, targets, points, fit)
     shares = [share] + [exchange(share, grid_count, d) for d in range(1, grid_count)]
-    *pieces, at = fit_pairs(orbitals, targets, fit, shares)
+    *pieces, at = fit_pairs(orbitals, notes, shares)
     pieces = pieces[:1] + [exchange(pieces[d], grid_count, d) for d in range(1, grid_count)]
     sent = potentials(plan, pieces, at, slab_count)
     received = lax.all_to_all(sent, everyone, 0, 0)
-    blocks = apply_part(orbitals, targets, received, slab_count)
+    blocks = apply_part(orbitals, notes, received, targets.shape[0], slab_count)
     kept = lax.all_to_all(blocks, "slab", 0, 0)
-    kept = kept.reshape(-1, keep, lanes)
-    return jnp.transpose(kept, (1, 0, 2)).reshape(keep, shard_len)
+    return jnp.transpose(settle(kept, keep), (1, 0, 2)).reshape(keep, shard_len)
 
 
 def quick_fits(mesh, orbitals, targets, points, fit):

time: 48.4 us -> 45.6 us (0.942)
  local copies, waits for them, and re-layouts: 4.84 us -> 1.47 us
  Pallas kernels: 5.24 us -> 6.88 us
  blocking collectives: 26.9 us -> 25.5 us
    unnamed x24 -> x20, local copies, waits for them, and re-layouts: 4.03 us -> 1.47 us
    pallas_call x2 -> x3, Pallas kernels: 1.88 us -> 4.14 us  [the longest x1 2.77 us: read_points(): pl.pallas_call(kernel, out_shape=[jax.ShapeDtypeStruct((8, lanes), f32),...]
    all_to_all x1, blocking collectives: 11.2 us -> 9.84 us  [quick_body(): kept = lax.all_to_all(blocks, 'slab', 0, 0)]
    reshape x1 -> x0, local copies, waits for them, and re-layouts: 0.81 us -> none  [quick_body(): kept = kept.reshape(-1, keep, lanes)]
    pallas_call x1, Pallas kernels: 1.37 us -> 0.73 us  [fit_pairs(): pl.pallas_call(kernel, out_shape=[piece] * group + [jax.ShapeDtypeStruct(...]
where the time goes in v2:
time: 45.6 us; the launch traced here: 45.3 us
  blocking collectives  25.5 us (56%)
  Pallas kernels  6.88 us (15%)
  waiting for transfers between devices  6.3 us (14%)
  starting transfers between devices  5.05 us (11%)
  local copies, waits for them, and re-layouts  1.47 us (3%)
    all_to_all x1, blocking collectives, quick_body(): received = lax.all_to_all(sent, everyone, 0, 0)  15.7 us
    all_to_all x1, blocking collectives, quick_body(): kept = lax.all_to_all(blocks, 'slab', 0, 0)  9.84 us
    ppermute x6, waiting for transfers between devices, exchange(): lax.ppermute(value, 'grid', [(i, i ^ offset) for i in range(grid_count)])  6.3 us
    ppermute x6, starting transfers between devices, exchange(): lax.ppermute(value, 'grid', [(i, i ^ offset) for i in range(grid_count)])  5.05 us
    pallas_call x1, Pallas kernels, read_points(): pl.pallas_call(kernel, out_shape=[jax.ShapeDtypeStruct((8, lanes), f32),...  2.77 us
    pallas_call x1, Pallas kernels, potentials(): pl.pallas_call(kernel, out_shape=jax.ShapeDtypeStruct((slab_count * grid_...  2 us
    unnamed x20, local copies, waits for them, and re-layouts  1.47 us
  transfers between devices with their start and end apart: 6, of which 4 were waited for; matrix products, arithmetic and copies ran while one was open for 0% of the time, Pallas kernels for 0%

profile of v2, /device:TPU:0, one launch (start us, length us, event | category | flops | bytes accessed | tf_op | source)
XLA Modules:
  0.0 45.3 jit_solution(12689037393144401608)
XLA Ops:
  0.0 0.0 copy-start
  0.0 0.0 copy-start.5
  0.0 2.8 %read_points.1 = (f32[8,128]{1,0:T(8,128)}, f32[56,128]{1,0:T(8,128)}) custom-call(s32[4]{0:T(128)} %points_hbm.1, s32[16]{0:T(128)} %targets_hbm.1, f32[4,4]{1,0:T(4,128)} %fit_hbm.1, bf16[64,27648]{1,0:T(8,128)(2,1)} %orbitals_ref.5), custom_call_target="tpu_custom_call" | custom-call | tf_op jit(solution)/shard_map/read_points/pallas_call | solution.py:318
  2.8 0.0 copy-start.1
  2.8 0.0 copy-start.2
  2.8 0.0 copy-start.3
  2.8 0.0 copy-start.4
  2.8 2.4 %collective-permute-start.2 = (f32[8,128]{1,0:T(8,128)}, f32[8,128]{1,0:T(8,128)S(1)}, u32[]{:S(2)}, u32[]{:S(2)}) collective-permute-start(f32[8,128]{1,0:T(8,128)} %get-tuple-element.13.refs_0_), channel_id=1, source_target_pairs={{0,3},{1,2},{2,1},{3,0},{4,7},{5,6},{6,5},{7,4},{8,11},{9,10},{10,... | collective-permute-start | bytes 12296 | tf_op jit(solution)/shard_map/ppermute | solution.py:476
  5.3 0.6 %collective-permute-start.1 = (f32[8,128]{1,0:T(8,128)}, f32[8,128]{1,0:T(8,128)S(1)}, u32[]{:S(2)}, u32[]{:S(2)}) collective-permute-start(f32[8,128]{1,0:T(8,128)} %get-tuple-element.13.refs_0_), channel_id=1, source_target_pairs={{0,2},{1,3},{2,0},{3,1},{4,6},{5,7},{6,4},{7,5},{8,10},{9,11},{10,... | collective-permute-start | bytes 12296 | tf_op jit(solution)/shard_map/ppermute | solution.py:476
  5.9 0.0 collective-permute-start
  6.0 0.9 %collective-permute-done.2.refs_3_ = f32[8,128]{1,0:T(8,128)S(1)} collective-permute-done((f32[8,128]{1,0:T(8,128)}, f32[8,128]{1,0:T(8,128)S(1)}, u32[]{:S(2)}, u32[]{:S(2)}) %collective-permute-start.2) | collective-permute-done | bytes 4128 | tf_op jit(solution)/shard_map/ppermute | solution.py:476
  6.8 2.3 %collective-permute-done.1.refs_2_ = f32[8,128]{1,0:T(8,128)S(1)} collective-permute-done((f32[8,128]{1,0:T(8,128)}, f32[8,128]{1,0:T(8,128)S(1)}, u32[]{:S(2)}, u32[]{:S(2)}) %collective-permute-start.1) | collective-permute-done | bytes 4128 | tf_op jit(solution)/shard_map/ppermute | solution.py:476
  9.1 0.0 collective-permute-done.refs_1_
  9.1 0.0 copy-done
  9.1 0.0 copy-start.6
  9.1 0.7 %copy-done.6 = f32[56,128]{1,0:T(8,128)S(1)} copy-done((f32[56,128]{1,0:T(8,128)S(1)}, f32[56,128]{1,0:T(8,128)}, u32[]{:S(2)}) %copy-start.6) | copy-done | bytes 28696
  9.8 0.0 copy-start.9
  9.9 0.7 %copy-done.9 = f32[8,128]{1,0:T(8,128)S(1)} copy-done((f32[8,128]{1,0:T(8,128)S(1)}, f32[8,128]{1,0:T(8,128)}, u32[]{:S(2)}) %copy-start.9) | copy-done | bytes 4120
  10.5 0.0 copy-start.8
  10.5 0.0 copy-start.7
  10.5 0.7 %fit_pairs.1 = (bf16[216,128]{1,0:T(8,128)(2,1)S(1)}, bf16[216,128]{1,0:T(8,128)(2,1)S(1)}, bf16[216,128]{1,0:T(8,128)(2,1)S(1)}, bf16[216,128]{1,0:T(8,128)(2,1)S(1)}, f32[8,128]{1,0:T(8,128)S(1)}) custom-call(f32[56,128]{1,0:T(8,128)S(1)} %copy-done.6, bf16[64,27648]{1,0:T(8,128)(2,1)S(1)} %copy-done, f32[8,128]{1,0:T(8,128)S(1)} %copy-done.9, ...), custom_call_target="tpu_custom_call" | custom-call | tf_op jit(solution)/shard_map/fit_pairs/pallas_call | solution.py:370
  11.3 0.1 collective-permute-start.3
  11.3 0.7 %collective-permute-start.4 = (bf16[216,128]{1,0:T(8,128)(2,1)S(1)}, bf16[216,128]{1,0:T(8,128)(2,1)S(1)}, u32[]{:S(2)}, u32[]{:S(2)}) collective-permute-start(bf16[216,128]{1,0:T(8,128)(2,1)S(1)} %get-tuple-element.17), channel_id=1, source_target_pairs={{0,2},{1,3},{2,0},{3,1},{4,6},{5,7},{6,4},{7,5},{8,10},{9,11},{10,... | collective-permute-start | bytes 165896 | tf_op jit(solution)/shard_map/ppermute | solution.py:476
  12.1 1.2 %collective-permute-start.5 = (bf16[216,128]{1,0:T(8,128)(2,1)S(1)}, bf16[216,128]{1,0:T(8,128)(2,1)S(1)}, u32[]{:S(2)}, u32[]{:S(2)}) collective-permute-start(bf16[216,128]{1,0:T(8,128)(2,1)S(1)} %get-tuple-element.18), channel_id=1, source_target_pairs={{0,3},{1,2},{2,1},{3,0},{4,7},{5,6},{6,5},{7,4},{8,11},{9,10},{10,... | collective-permute-start | bytes 165896 | tf_op jit(solution)/shard_map/ppermute | solution.py:476
  13.2 0.0 collective-permute-done.3.refs_1_
  13.2 2.9 %collective-permute-done.4.refs_2_ = bf16[216,128]{1,0:T(8,128)(2,1)S(1)} collective-permute-done((bf16[216,128]{1,0:T(8,128)(2,1)S(1)}, bf16[216,128]{1,0:T(8,128)(2,1)S(1)}, u32[]{:S(2)}, u32[]{:S(2)}) %collective-permute-start.4) | collective-permute-done | bytes 55328 | tf_op jit(solution)/shard_map/ppermute | solution.py:476
  16.1 0.3 collective-permute-done.5.refs_3_
  16.4 0.0 copy-done.5
  16.4 0.0 copy-done.1
  16.4 0.0 copy-done.2
  16.4 0.0 copy-done.3
  16.4 0.0 copy-done.4
  16.4 0.0 copy-done.8
  16.4 2.0 %potentials.1 = bf16[32,28,128]{2,1,0:T(8,128)(2,1)S(1)} custom-call(f32[8,128]{1,0:T(8,128)S(1)} %get-tuple-element.14.at_ref, bf16[216,128]{1,0:T(8,128)(2,1)S(1)} %get-tuple-element.15.refs_0_, bf16[216,128]{1,0:T(8,128)(2,1)S(1)} %collective-permute-done.3.refs_1_, bf16[216,128]{1,0:T(8,128)(2,1)S(1)} %collective-permute-done.4.refs_2_, ...), custom_call_target="tpu_custom_call" | custom-call | tf_op jit(solution)/shard_map/potentials/pallas_call | solution.py:401
  18.4 15.7 %all_to_all.10.received_ref = bf16[32,28,128]{2,1,0:T(8,128)(2,1)S(1)} all-to-all(bf16[32,28,128]{2,1,0:T(8,128)(2,1)S(1)} %potentials.1), channel_id=1, replica_groups=mesh['slab'=8,'grid'=4] {'slab','grid'}, dimensions={0} | all-to-all | bytes 458752 | tf_op jit(solution)/shard_map/all_to_all | solution.py:490
  34.1 0.0 copy-done.7
  34.1 0.5 %apply_part.1 = bf16[8,54,128]{2,1,0:T(8,128)(2,1)S(1)} custom-call(f32[56,128]{1,0:T(8,128)S(1)} %copy-done.7, bf16[64,27648]{1,0:T(8,128)(2,1)S(1)} %copy-done, bf16[32,28,128]{2,1,0:T(8,128)(2,1)S(1)} %all_to_all.10.received_ref), custom_call_target="tpu_custom_call" | custom-call | tf_op jit(solution)/shard_map/apply_part/pallas_call | solution.py:440
  34.6 9.8 %all_to_all.11.kept_ref = bf16[8,54,128]{2,1,0:T(8,128)(2,1)S(1)} all-to-all(bf16[8,54,128]{2,1,0:T(8,128)(2,1)S(1)} %apply_part.1), channel_id=1, replica_groups=mesh['slab'=8,'grid'=4] {'slab'}, dimensions={0} | all-to-all | bytes 221184 | tf_op jit(solution)/shard_map/all_to_all | solution.py:492
  44.5 0.8 %settle.1 = f32[216,2,128]{2,1,0:T(2,128)} custom-call(bf16[8,54,128]{2,1,0:T(8,128)(2,1)S(1)} %all_to_all.11.kept_ref), custom_call_target="tpu_custom_call" | custom-call | tf_op jit(solution)/shard_map/settle/pallas_call | solution.py:464
Async XLA Ops:
  0.0 9.1 %copy-start = (bf16[64,27648]{1,0:T(8,128)(2,1)S(1)}, bf16[64,27648]{1,0:T(8,128)(2,1)}, u32[]{:S(2)}) copy-start(bf16[64,27648]{1,0:T(8,128)(2,1)} %orbitals_ref.5) | copy-start | bytes 10616836
  0.0 16.4 %copy-start.5 = (f32[24,48,128]{2,1,0:T(8,128)S(1)}, f32[24,48,128]{2,1,0:T(8,128)}, u32[]{:S(2)}) copy-start(f32[24,48,128]{2,1,0:T(8,128)} %constant.17.clone.refs_9_) | copy-start | bytes 1769476
  2.8 13.6 %copy-start.1 = (bf16[1536,256]{1,0:T(8,128)(2,1)S(1)}, bf16[1536,256]{1,0:T(8,128)(2,1)}, u32[]{:S(2)}) copy-start(bf16[1536,256]{1,0:T(8,128)(2,1)} %constant.14.clone.refs_6_) | copy-start | bytes 2359300
  2.8 13.6 %copy-start.2 = (bf16[1536,256]{1,0:T(8,128)(2,1)S(1)}, bf16[1536,256]{1,0:T(8,128)(2,1)}, u32[]{:S(2)}) copy-start(bf16[1536,256]{1,0:T(8,128)(2,1)} %constant.13.clone.refs_5_) | copy-start | bytes 2359300
  2.8 13.6 %copy-start.3 = (bf16[1280,256]{1,0:T(8,128)(2,1)S(1)}, bf16[1280,256]{1,0:T(8,128)(2,1)}, u32[]{:S(2)}) copy-start(bf16[1280,256]{1,0:T(8,128)(2,1)} %constant.16.clone.refs_8_) | copy-start | bytes 1966084
  2.8 13.6 %copy-start.4 = (bf16[1280,256]{1,0:T(8,128)(2,1)S(1)}, bf16[1280,256]{1,0:T(8,128)(2,1)}, u32[]{:S(2)}) copy-start(bf16[1280,256]{1,0:T(8,128)(2,1)} %constant.15.clone.refs_7_) | copy-start | bytes 1966084
  2.8 4.0 %collective-permute-start.2 = (f32[8,128]{1,0:T(8,128)}, f32[8,128]{1,0:T(8,128)S(1)}, u32[]{:S(2)}, u32[]{:S(2)}) collective-permute-start(f32[8,128]{1,0:T(8,128)} %get-tuple-element.13.refs_0_), channel_id=1, source_target_pairs={{0,3},{1,2},{2,1},{3,0},{4,7},{5,6},{6,5},{7,4},{8,11},{9,10},{10,... | collective-permute-start | bytes 12296 | tf_op jit(solution)/shard_map/ppermute | solution.py:476
  5.3 3.8 %collective-permute-start.1 = (f32[8,128]{1,0:T(8,128)}, f32[8,128]{1,0:T(8,128)S(1)}, u32[]{:S(2)}, u32[]{:S(2)}) collective-permute-start(f32[8,128]{1,0:T(8,128)} %get-tuple-element.13.refs_0_), channel_id=1, source_target_pairs={{0,2},{1,3},{2,0},{3,1},{4,6},{5,7},{6,4},{7,5},{8,10},{9,11},{10,... | collective-permute-start | bytes 12296 | tf_op jit(solution)/shard_map/ppermute | solution.py:476
  5.9 3.2 %collective-permute-start = (f32[8,128]{1,0:T(8,128)}, f32[8,128]{1,0:T(8,128)S(1)}, u32[]{:S(2)}, u32[]{:S(2)}) collective-permute-start(f32[8,128]{1,0:T(8,128)} %get-tuple-element.13.refs_0_), channel_id=1, source_target_pairs={{0,1},{1,0},{2,3},{3,2},{4,5},{5,4},{6,7},{7,6},{8,9},{9,8},{10,11... | collective-permute-start | bytes 12296 | tf_op jit(solution)/shard_map/ppermute | solution.py:476
  9.1 0.8 %copy-start.6 = (f32[56,128]{1,0:T(8,128)S(1)}, f32[56,128]{1,0:T(8,128)}, u32[]{:S(2)}) copy-start(f32[56,128]{1,0:T(8,128)} %get-tuple-element.12.notes_ref) | copy-start | bytes 86020
  9.8 0.7 %copy-start.9 = (f32[8,128]{1,0:T(8,128)S(1)}, f32[8,128]{1,0:T(8,128)}, u32[]{:S(2)}) copy-start(f32[8,128]{1,0:T(8,128)} %get-tuple-element.13.refs_0_) | copy-start | bytes 12292
  10.5 5.9 %copy-start.8 = (bf16[48,144]{1,0:T(8,128)(2,1)S(1)}, bf16[48,144]{1,0:T(8,128)(2,1)}, u32[]{:S(2)}) copy-start(bf16[48,144]{1,0:T(8,128)(2,1)} %constant.12.clone.refs_4_) | copy-start | bytes 41476
  10.5 23.6 %copy-start.7 = (f32[56,128]{1,0:T(8,128)S(1)}, f32[56,128]{1,0:T(8,128)}, u32[]{:S(2)}) copy-start(f32[56,128]{1,0:T(8,128)} %get-tuple-element.12.notes_ref) | copy-start | bytes 86020
  11.3 1.9 %collective-permute-start.3 = (bf16[216,128]{1,0:T(8,128)(2,1)S(1)}, bf16[216,128]{1,0:T(8,128)(2,1)S(1)}, u32[]{:S(2)}, u32[]{:S(2)}) collective-permute-start(bf16[216,128]{1,0:T(8,128)(2,1)S(1)} %get-tuple-element.16), channel_id=1, source_target_pairs={{0,1},{1,0},{2,3},{3,2},{4,5},{5,4},{6,7},{7,6},{8,9},{9,8},{10,11... | collective-permute-start | bytes 165896 | tf_op jit(solution)/shard_map/ppermute | solution.py:476
  11.3 4.7 %collective-permute-start.4 = (bf16[216,128]{1,0:T(8,128)(2,1)S(1)}, bf16[216,128]{1,0:T(8,128)(2,1)S(1)}, u32[]{:S(2)}, u32[]{:S(2)}) collective-permute-start(bf16[216,128]{1,0:T(8,128)(2,1)S(1)} %get-tuple-element.17), channel_id=1, source_target_pairs={{0,2},{1,3},{2,0},{3,1},{4,6},{5,7},{6,4},{7,5},{8,10},{9,11},{10,... | collective-permute-start | bytes 165896 | tf_op jit(solution)/shard_map/ppermute | solution.py:476
  12.1 4.3 %collective-permute-start.5 = (bf16[216,128]{1,0:T(8,128)(2,1)S(1)}, bf16[216,128]{1,0:T(8,128)(2,1)S(1)}, u32[]{:S(2)}, u32[]{:S(2)}) collective-permute-start(bf16[216,128]{1,0:T(8,128)(2,1)S(1)} %get-tuple-element.18), channel_id=1, source_target_pairs={{0,3},{1,2},{2,1},{3,0},{4,7},{5,6},{6,5},{7,4},{8,11},{9,10},{10,... | collective-permute-start | bytes 165896 | tf_op jit(solution)/shard_map/ppermute | solution.py:476

commit v3 on v2

--- a/solution.py
+++ b/solution.py
@@ -318,8 +318,8 @@
     return pl.pallas_call(
         kernel,
         out_shape=[
-            jax.ShapeDtypeStruct((8, lanes), f32),
-            jax.ShapeDtypeStruct((8 + 8 * group + count, lanes), f32),
+            pltpu.VMEM((8, lanes), f32),
+            pltpu.VMEM((8 + 8 * group + count, lanes), f32),
         ],
         in_specs=[far] * 4,
         out_specs=[whole] * 2,
@@ -330,9 +330,9 @@
             pltpu.VMEM((occupied, group * lanes), bf16),
             pltpu.SemaphoreType.DMA((group + 3,)),
         ],
-        compiler_params=params(60),
+        compiler_params=params(4),
         name="read_points",
-    )(points, targets, fit, orbitals)
+    )(*[pltpu.with_memory_space_constraint(value, pltpu.HBM) for value in (points, targets, fit, orbitals)])
 
 
 def fit_pairs(orbitals, notes, shares):

time: 45.6 us -> 43.3 us (0.950)
  local copies, waits for them, and re-layouts: 1.47 us -> 0.03 us
  Pallas kernels: 6.88 us -> 6.3 us
    unnamed x20 -> x14, local copies, waits for them, and re-layouts: 1.47 us -> 0.03 us
    pallas_call x1, Pallas kernels: 2.77 us -> 2.17 us  [read_points(): pl.pallas_call(kernel, out_shape=[pltpu.VMEM((8, lanes), f32), pltpu.VMEM...]
where the time goes in v3:
time: 43.3 us; the launch traced here: 43.1 us
  blocking collectives  25.5 us (59%)
  Pallas kernels  6.3 us (15%)
  waiting for transfers between devices  6.09 us (14%)
  starting transfers between devices  5.08 us (12%)
    all_to_all x1, blocking collectives, quick_body(): received = lax.all_to_all(sent, everyone, 0, 0)  15.7 us
    all_to_all x1, blocking collectives, quick_body(): kept = lax.all_to_all(blocks, 'slab', 0, 0)  9.83 us
    ppermute x6, waiting for transfers between devices, exchange(): lax.ppermute(value, 'grid', [(i, i ^ offset) for i in range(grid_count)])  6.09 us
    ppermute x6, starting transfers between devices, exchange(): lax.ppermute(value, 'grid', [(i, i ^ offset) for i in range(grid_count)])  5.08 us
    pallas_call x1, Pallas kernels, read_points(): pl.pallas_call(kernel, out_shape=[pltpu.VMEM((8, lanes), f32), pltpu.VMEM...  2.17 us
    pallas_call x1, Pallas kernels, potentials(): pl.pallas_call(kernel, out_shape=jax.ShapeDtypeStruct((slab_count * grid_...  2 us
  transfers between devices with their start and end apart: 6, of which 4 were waited for; matrix products, arithmetic and copies ran while one was open for 0% of the time, Pallas kernels for 0%

profile of v3, /device:TPU:0, one launch (start us, length us, event | category | flops | bytes accessed | tf_op | source)
XLA Modules:
  0.0 43.1 jit_solution(15402507322506797545)
XLA Ops:
  0.0 0.0 copy-start
  0.0 0.0 copy-start.1
  0.0 0.0 copy-start.2
  0.0 0.0 copy-start.3
  0.0 0.0 copy-start.4
  0.0 0.0 copy-start.5
  0.0 0.0 copy-start.6
  0.0 2.2 %read_points.1 = (f32[8,128]{1,0:T(8,128)S(1)}, f32[56,128]{1,0:T(8,128)S(1)}) custom-call(s32[4]{0:T(128)} %points_hbm.1, s32[16]{0:T(128)} %targets_hbm.1, f32[4,4]{1,0:T(4,128)} %fit_hbm.1, bf16[64,27648]{1,0:T(8,128)(2,1)} %orbitals_ref.5), custom_call_target="tpu_custom_call" | custom-call | tf_op jit(solution)/shard_map/read_points/pallas_call | solution.py:318
  2.2 2.5 %collective-permute-start.2 = (f32[8,128]{1,0:T(8,128)S(1)}, f32[8,128]{1,0:T(8,128)S(1)}, u32[]{:S(2)}, u32[]{:S(2)}) collective-permute-start(f32[8,128]{1,0:T(8,128)S(1)} %get-tuple-element.13.refs_0_), channel_id=1, source_target_pairs={{0,3},{1,2},{2,1},{3,0},{4,7},{5,6},{6,5},{7,4},{8,11},{9,10},{10,... | collective-permute-start | bytes 12296 | tf_op jit(solution)/shard_map/ppermute | solution.py:476
  4.7 0.6 %collective-permute-start.1 = (f32[8,128]{1,0:T(8,128)S(1)}, f32[8,128]{1,0:T(8,128)S(1)}, u32[]{:S(2)}, u32[]{:S(2)}) collective-permute-start(f32[8,128]{1,0:T(8,128)S(1)} %get-tuple-element.13.refs_0_), channel_id=1, source_target_pairs={{0,2},{1,3},{2,0},{3,1},{4,6},{5,7},{6,4},{7,5},{8,10},{9,11},{10,... | collective-permute-start | bytes 12296 | tf_op jit(solution)/shard_map/ppermute | solution.py:476
  5.3 0.0 collective-permute-start
  5.4 0.6 %collective-permute-done.2.refs_3_ = f32[8,128]{1,0:T(8,128)S(1)} collective-permute-done((f32[8,128]{1,0:T(8,128)S(1)}, f32[8,128]{1,0:T(8,128)S(1)}, u32[]{:S(2)}, u32[]{:S(2)}) %collective-permute-start.2) | collective-permute-done | bytes 4128 | tf_op jit(solution)/shard_map/ppermute | solution.py:476
  6.0 2.3 %collective-permute-done.1.refs_2_ = f32[8,128]{1,0:T(8,128)S(1)} collective-permute-done((f32[8,128]{1,0:T(8,128)S(1)}, f32[8,128]{1,0:T(8,128)S(1)}, u32[]{:S(2)}, u32[]{:S(2)}) %collective-permute-start.1) | collective-permute-done | bytes 4128 | tf_op jit(solution)/shard_map/ppermute | solution.py:476
  8.3 0.0 collective-permute-done.refs_1_
  8.3 0.0 copy-done
  8.3 0.7 %fit_pairs.1 = (bf16[216,128]{1,0:T(8,128)(2,1)S(1)}, bf16[216,128]{1,0:T(8,128)(2,1)S(1)}, bf16[216,128]{1,0:T(8,128)(2,1)S(1)}, bf16[216,128]{1,0:T(8,128)(2,1)S(1)}, f32[8,128]{1,0:T(8,128)S(1)}) custom-call(f32[56,128]{1,0:T(8,128)S(1)} %get-tuple-element.12.notes_ref, bf16[64,27648]{1,0:T(8,128)(2,1)S(1)} %copy-done, ...), custom_call_target="tpu_custom_call" | custom-call | tf_op jit(solution)/shard_map/fit_pairs/pallas_call | solution.py:370
  9.1 0.1 collective-permute-start.3
  9.1 0.7 %collective-permute-start.4 = (bf16[216,128]{1,0:T(8,128)(2,1)S(1)}, bf16[216,128]{1,0:T(8,128)(2,1)S(1)}, u32[]{:S(2)}, u32[]{:S(2)}) collective-permute-start(bf16[216,128]{1,0:T(8,128)(2,1)S(1)} %get-tuple-element.17), channel_id=1, source_target_pairs={{0,2},{1,3},{2,0},{3,1},{4,6},{5,7},{6,4},{7,5},{8,10},{9,11},{10,... | collective-permute-start | bytes 165896 | tf_op jit(solution)/shard_map/ppermute | solution.py:476
  9.8 1.2 %collective-permute-start.5 = (bf16[216,128]{1,0:T(8,128)(2,1)S(1)}, bf16[216,128]{1,0:T(8,128)(2,1)S(1)}, u32[]{:S(2)}, u32[]{:S(2)}) collective-permute-start(bf16[216,128]{1,0:T(8,128)(2,1)S(1)} %get-tuple-element.18), channel_id=1, source_target_pairs={{0,3},{1,2},{2,1},{3,0},{4,7},{5,6},{6,5},{7,4},{8,11},{9,10},{10,... | collective-permute-start | bytes 165896 | tf_op jit(solution)/shard_map/ppermute | solution.py:476
  11.0 0.0 collective-permute-done.3.refs_1_
  11.0 2.9 %collective-permute-done.4.refs_2_ = bf16[216,128]{1,0:T(8,128)(2,1)S(1)} collective-permute-done((bf16[216,128]{1,0:T(8,128)(2,1)S(1)}, bf16[216,128]{1,0:T(8,128)(2,1)S(1)}, u32[]{:S(2)}, u32[]{:S(2)}) %collective-permute-start.4) | collective-permute-done | bytes 55328 | tf_op jit(solution)/shard_map/ppermute | solution.py:476
  13.9 0.3 collective-permute-done.5.refs_3_
  14.2 0.0 copy-done.1
  14.2 0.0 copy-done.2
  14.2 0.0 copy-done.3
  14.2 0.0 copy-done.4
  14.2 0.0 copy-done.5
  14.2 0.0 copy-done.6
  14.2 2.0 %potentials.1 = bf16[32,28,128]{2,1,0:T(8,128)(2,1)S(1)} custom-call(f32[8,128]{1,0:T(8,128)S(1)} %get-tuple-element.14.at_ref, bf16[216,128]{1,0:T(8,128)(2,1)S(1)} %get-tuple-element.15.refs_0_, bf16[216,128]{1,0:T(8,128)(2,1)S(1)} %collective-permute-done.3.refs_1_, bf16[216,128]{1,0:T(8,128)(2,1)S(1)} %collective-permute-done.4.refs_2_, ...), custom_call_target="tpu_custom_call" | custom-call | tf_op jit(solution)/shard_map/potentials/pallas_call | solution.py:401
  16.2 15.7 %all_to_all.10.received_ref = bf16[32,28,128]{2,1,0:T(8,128)(2,1)S(1)} all-to-all(bf16[32,28,128]{2,1,0:T(8,128)(2,1)S(1)} %potentials.1), channel_id=1, replica_groups=mesh['slab'=8,'grid'=4] {'slab','grid'}, dimensions={0} | all-to-all | bytes 458752 | tf_op jit(solution)/shard_map/all_to_all | solution.py:490
  31.9 0.5 %apply_part.1 = bf16[8,54,128]{2,1,0:T(8,128)(2,1)S(1)} custom-call(f32[56,128]{1,0:T(8,128)S(1)} %get-tuple-element.12.notes_ref, bf16[64,27648]{1,0:T(8,128)(2,1)S(1)} %copy-done, bf16[32,28,128]{2,1,0:T(8,128)(2,1)S(1)} %all_to_all.10.received_ref), custom_call_target="tpu_custom_call" | custom-call | tf_op jit(solution)/shard_map/apply_part/pallas_call | solution.py:440
  32.4 9.8 %all_to_all.11.kept_ref = bf16[8,54,128]{2,1,0:T(8,128)(2,1)S(1)} all-to-all(bf16[8,54,128]{2,1,0:T(8,128)(2,1)S(1)} %apply_part.1), channel_id=1, replica_groups=mesh['slab'=8,'grid'=4] {'slab'}, dimensions={0} | all-to-all | bytes 221184 | tf_op jit(solution)/shard_map/all_to_all | solution.py:492
  42.3 0.8 %settle.1 = f32[216,2,128]{2,1,0:T(2,128)} custom-call(bf16[8,54,128]{2,1,0:T(8,128)(2,1)S(1)} %all_to_all.11.kept_ref), custom_call_target="tpu_custom_call" | custom-call | tf_op jit(solution)/shard_map/settle/pallas_call | solution.py:464
Async XLA Ops:
  0.0 8.3 %copy-start = (bf16[64,27648]{1,0:T(8,128)(2,1)S(1)}, bf16[64,27648]{1,0:T(8,128)(2,1)}, u32[]{:S(2)}) copy-start(bf16[64,27648]{1,0:T(8,128)(2,1)} %orbitals_ref.5) | copy-start | bytes 10616836
  0.0 14.2 %copy-start.1 = (bf16[1536,256]{1,0:T(8,128)(2,1)S(1)}, bf16[1536,256]{1,0:T(8,128)(2,1)}, u32[]{:S(2)}) copy-start(bf16[1536,256]{1,0:T(8,128)(2,1)} %constant.14.clone.refs_6_) | copy-start | bytes 2359300
  0.0 14.2 %copy-start.2 = (bf16[1536,256]{1,0:T(8,128)(2,1)S(1)}, bf16[1536,256]{1,0:T(8,128)(2,1)}, u32[]{:S(2)}) copy-start(bf16[1536,256]{1,0:T(8,128)(2,1)} %constant.13.clone.refs_5_) | copy-start | bytes 2359300
  0.0 14.2 %copy-start.3 = (bf16[1280,256]{1,0:T(8,128)(2,1)S(1)}, bf16[1280,256]{1,0:T(8,128)(2,1)}, u32[]{:S(2)}) copy-start(bf16[1280,256]{1,0:T(8,128)(2,1)} %constant.16.clone.refs_8_) | copy-start | bytes 1966084
  0.0 14.2 %copy-start.4 = (bf16[1280,256]{1,0:T(8,128)(2,1)S(1)}, bf16[1280,256]{1,0:T(8,128)(2,1)}, u32[]{:S(2)}) copy-start(bf16[1280,256]{1,0:T(8,128)(2,1)} %constant.15.clone.refs_7_) | copy-start | bytes 1966084
  0.0 14.2 %copy-start.5 = (f32[24,48,128]{2,1,0:T(8,128)S(1)}, f32[24,48,128]{2,1,0:T(8,128)}, u32[]{:S(2)}) copy-start(f32[24,48,128]{2,1,0:T(8,128)} %constant.17.clone.refs_9_) | copy-start | bytes 1769476
  0.0 14.2 %copy-start.6 = (bf16[48,144]{1,0:T(8,128)(2,1)S(1)}, bf16[48,144]{1,0:T(8,128)(2,1)}, u32[]{:S(2)}) copy-start(bf16[48,144]{1,0:T(8,128)(2,1)} %constant.12.clone.refs_4_) | copy-start | bytes 41476
  2.2 3.8 %collective-permute-start.2 = (f32[8,128]{1,0:T(8,128)S(1)}, f32[8,128]{1,0:T(8,128)S(1)}, u32[]{:S(2)}, u32[]{:S(2)}) collective-permute-start(f32[8,128]{1,0:T(8,128)S(1)} %get-tuple-element.13.refs_0_), channel_id=1, source_target_pairs={{0,3},{1,2},{2,1},{3,0},{4,7},{5,6},{6,5},{7,4},{8,11},{9,10},{10,... | collective-permute-start | bytes 12296 | tf_op jit(solution)/shard_map/ppermute | solution.py:476
  4.7 3.6 %collective-permute-start.1 = (f32[8,128]{1,0:T(8,128)S(1)}, f32[8,128]{1,0:T(8,128)S(1)}, u32[]{:S(2)}, u32[]{:S(2)}) collective-permute-start(f32[8,128]{1,0:T(8,128)S(1)} %get-tuple-element.13.refs_0_), channel_id=1, source_target_pairs={{0,2},{1,3},{2,0},{3,1},{4,6},{5,7},{6,4},{7,5},{8,10},{9,11},{10,... | collective-permute-start | bytes 12296 | tf_op jit(solution)/shard_map/ppermute | solution.py:476
  5.3 3.0 %collective-permute-start = (f32[8,128]{1,0:T(8,128)S(1)}, f32[8,128]{1,0:T(8,128)S(1)}, u32[]{:S(2)}, u32[]{:S(2)}) collective-permute-start(f32[8,128]{1,0:T(8,128)S(1)} %get-tuple-element.13.refs_0_), channel_id=1, source_target_pairs={{0,1},{1,0},{2,3},{3,2},{4,5},{5,4},{6,7},{7,6},{8,9},{9,8},{10,11... | collective-permute-start | bytes 12296 | tf_op jit(solution)/shard_map/ppermute | solution.py:476
  9.1 1.9 %collective-permute-start.3 = (bf16[216,128]{1,0:T(8,128)(2,1)S(1)}, bf16[216,128]{1,0:T(8,128)(2,1)S(1)}, u32[]{:S(2)}, u32[]{:S(2)}) collective-permute-start(bf16[216,128]{1,0:T(8,128)(2,1)S(1)} %get-tuple-element.16), channel_id=1, source_target_pairs={{0,1},{1,0},{2,3},{3,2},{4,5},{5,4},{6,7},{7,6},{8,9},{9,8},{10,11... | collective-permute-start | bytes 165896 | tf_op jit(solution)/shard_map/ppermute | solution.py:476
  9.1 4.7 %collective-permute-start.4 = (bf16[216,128]{1,0:T(8,128)(2,1)S(1)}, bf16[216,128]{1,0:T(8,128)(2,1)S(1)}, u32[]{:S(2)}, u32[]{:S(2)}) collective-permute-start(bf16[216,128]{1,0:T(8,128)(2,1)S(1)} %get-tuple-element.17), channel_id=1, source_target_pairs={{0,2},{1,3},{2,0},{3,1},{4,6},{5,7},{6,4},{7,5},{8,10},{9,11},{10,... | collective-permute-start | bytes 165896 | tf_op jit(solution)/shard_map/ppermute | solution.py:476
  9.8 4.3 %collective-permute-start.5 = (bf16[216,128]{1,0:T(8,128)(2,1)S(1)}, bf16[216,128]{1,0:T(8,128)(2,1)S(1)}, u32[]{:S(2)}, u32[]{:S(2)}) collective-permute-start(bf16[216,128]{1,0:T(8,128)(2,1)S(1)} %get-tuple-element.18), channel_id=1, source_target_pairs={{0,3},{1,2},{2,1},{3,0},{4,7},{5,6},{6,5},{7,4},{8,11},{9,10},{10,... | collective-permute-start | bytes 165896 | tf_op jit(solution)/shard_map/ppermute | solution.py:476

commit v4 on v3

--- a/solution.py
+++ b/solution.py
@@ -157,25 +157,20 @@
         self.plane_rows = edge * edge // lanes
         self.rows = edge * self.plane_rows
         matrix = hartley(edge)
-        pairs = self.inner // 2
-        wide = np.zeros((2, self.inner, edge, self.inner, 2, self.slot))
-        for h in range(2):
-            for y in range(self.inner):
-                wide[h, y, :, y, h, :edge] = matrix
-        wide = wide.reshape(2, self.block, self.inner * lanes)
-        self.forward = []
-        for j in range(pairs):
-            low = 2 * j * edge // lanes * lanes
-            high = -(-(2 * j + 2) * edge // lanes) * lanes
-            part = wide[:, low:high, 2 * j * lanes:(2 * j + 2) * lanes].reshape(2 * (high - low), 2 * lanes)
-            self.forward.append((low, high, part))
-        back = np.transpose(wide, (2, 0, 1))
-        self.backward = []
-        for c in range(self.block_rows):
-            low = c * lanes // edge * lanes
-            high = -(-(c + 1) * lanes // edge) * lanes
-            part = back[low:high, :, c * lanes:(c + 1) * lanes].reshape(high - low, 2 * lanes)
-            self.backward.append((low, high, part))
+        self.windows = []
+        tables = []
+        for j in range(self.inner // 2):
+            low, high = 2 * j * edge, (2 * j + 2) * edge
+            base = low // lanes * lanes
+            self.windows.append((low, high, base))
+            table = np.zeros((2 * lanes, 2, 2, self.slot))
+            for h in range(2):
+                for y in range(2):
+                    for z in range(edge):
+                        table[(low + y * edge + z - base + h * lanes) % (2 * lanes), y, h, :edge] = matrix[z]
+            tables.append(table.reshape(2 * lanes, 2 * lanes))
+        self.forward = np.concatenate(tables)
+        self.backward = np.concatenate([table.T for table in tables])
         step = 2.0 * math.pi / edge
         index = np.arange(edge)
         square = (np.where(index > edge // 2, index - edge, index) * step) ** 2
@@ -187,8 +182,8 @@
         self.left = np.concatenate([*split_table(matrix), split_table(matrix)[0]], axis=1)
 
     def tables(self):
-        fh, fl = split_table(np.concatenate([p for _, _, p in self.forward]))
-        bh, bl = split_table(np.concatenate([p for _, _, p in self.backward]))
+        fh, fl = split_table(self.forward)
+        bh, bl = split_table(self.backward)
         return [self.left, fh, fl, bh, bl, self.weights]
 
 
@@ -201,24 +196,35 @@
     return jnp.dot(a, b, preferred_element_type=jnp.float32)
 
 
+def product(value, upper_table, lower_table):
+    rows = value.shape[0]
+    upper, lower = split_value(value)
+    both = dot(jnp.concatenate([upper, lower], axis=0), upper_table)
+    return both[:rows] + both[rows:] + dot(upper, lower_table)
+
+
 def solve(plan, cube, left, fh, fl, bh, bl, weights, mid):
-    edge, half, inner, outer = plan.edge, plan.half, plan.inner, plan.outer
+    edge, half, inner, outer, block = plan.edge, plan.half, plan.inner, plan.outer, plan.block
     left_all = left[...]
     values = jnp.concatenate(
         [cube[pl.ds(c, edge, stride=plan.plane_rows), :].astype(bf16) for c in range(plan.plane_rows)], axis=1)
     spectrum = dot(left_all[:, :2 * edge], jnp.concatenate([values, values], axis=0))
-    folded = jnp.concatenate([
-        jnp.concatenate([spectrum[:half, b * plan.block:(b + 1) * plan.block],
-                         spectrum[half:, b * plan.block:(b + 1) * plan.block]], axis=1)
-        for b in range(outer)], axis=0)
-    upper, lower = split_value(folded)
-    at = 0
-    for j, (low, high, part) in enumerate(plan.forward):
-        window = lambda v: jnp.concatenate([v[:, low:high], v[:, plan.block + low:plan.block + high]], axis=1)
-        u, l = window(upper), window(lower)
-        th, tl = fh[at:at + part.shape[0], :], fl[at:at + part.shape[0], :]
-        at += part.shape[0]
-        result = dot(u, th) + dot(l, th) + dot(u, tl)
+
+    def tile(h, c):
+        return jnp.concatenate([
+            spectrum[h * half:(h + 1) * half, b * block + c * lanes:b * block + (c + 1) * lanes] for b in range(outer)], axis=0)
+
+    lane = lax.broadcasted_iota(jnp.int32, (outer * half, lanes), 1)
+    tiles = [[tile(h, c) for c in range(plan.block_rows)] for h in range(2)]
+    for j, (low, high, base) in enumerate(plan.windows):
+        c = base // lanes
+        if high - base <= lanes:
+            window = [tiles[0][c], tiles[1][c]]
+        else:
+            window = [jnp.where(lane >= low - base, tiles[0][c], tiles[1][c + 1]),
+                      jnp.where(lane < high - base - lanes, tiles[0][c + 1], tiles[1][c])]
+        rows = slice(2 * lanes * j, 2 * lanes * (j + 1))
+        result = product(jnp.concatenate(window, axis=1), fh[rows, :], fl[rows, :])
         for b in range(outer):
             for o in range(2):
                 y = b * inner + 2 * j + o
@@ -230,19 +236,26 @@
         value = dot(left_all, three(value))
         for o in range(2):
             mid[pl.ds(k + o, edge, stride=half), :] = value[:, o * lanes:(o + 1) * lanes]
+    results = []
+    for j in range(len(plan.windows)):
+        rows = slice(2 * lanes * j, 2 * lanes * (j + 1))
+        value = jnp.concatenate([
+            jnp.concatenate([mid[(b * inner + 2 * j + o) * half:(b * inner + 2 * j + o + 1) * half, :] for b in range(outer)], axis=0)
+            for o in range(2)], axis=1)
+        results.append(product(value, bh[rows, :], bl[rows, :]))
+
+    def gathered(h, c):
+        value = None
+        for (low, high, base), result in zip(plan.windows, results):
+            if low < (c + 1) * lanes and high > c * lanes:
+                place = (c * lanes - base + h * lanes) % (2 * lanes)
+                part = result[:, place:place + lanes]
+                value = part if value is None else jnp.where(lane >= low - c * lanes, part, value)
+        return value
+
+    tiles = [[gathered(h, c) for c in range(plan.block_rows)] for h in range(2)]
     value = jnp.concatenate([
-        jnp.concatenate([mid[(b * inner + y) * half:(b * inner + y + 1) * half, :] for y in range(inner)], axis=1)
-        for b in range(outer)], axis=0)
-    upper, lower = split_value(value)
-    at = 0
-    pieces = []
-    for low, high, part in plan.backward:
-        u, l = upper[:, low:high], lower[:, low:high]
-        th, tl = bh[at:at + part.shape[0], :], bl[at:at + part.shape[0], :]
-        at += part.shape[0]
-        pieces.append(dot(u, th) + dot(l, th) + dot(u, tl))
-    value = jnp.concatenate([
-        jnp.concatenate([pieces[c][b * half:(b + 1) * half, :lanes], pieces[c][b * half:(b + 1) * half, lanes:]], axis=0)
+        jnp.concatenate([tiles[h][c][b * half:(b + 1) * half] for h in range(2)], axis=0)
         for b in range(outer) for c in range(plan.block_rows)], axis=1)
     value = dot(left_all, three(value))
     for c in range(plan.plane_rows):
@@ -381,6 +394,7 @@
 def potentials(plan, pieces, at, slab_count):
     grid_count, piece_rows = len(pieces), pieces[0].shape[0]
     part = piece_rows // slab_count
+    sent = 2 * (part // 2 + 1)
     tables = plan.tables()
 
     def kernel(at_ref, *refs):
@@ -391,16 +405,17 @@
             start = pl.multiple_of(jnp.bitwise_xor(me, d) * piece_rows, 8)
             cube[pl.ds(start, piece_rows), :] = ref[...].astype(f32)
         solve(plan, cube, *table_refs, mid)
-        own = jnp.broadcast_to(at_ref[pl.ds(me, 1), :], (part + 1, lanes))
-        last = iota((part + 1, lanes), 0) == part
+        own = jnp.broadcast_to(at_ref[pl.ds(me, 1), :], (sent, lanes))
+        last = iota((sent, lanes), 0) >= part
         for g in range(grid_count):
             for s in range(slab_count):
                 first = g * piece_rows + s * part
-                out_ref[s * grid_count + g] = jnp.where(last, own, cube[first:first + part + 1, :]).astype(bf16)
+                value = jnp.where(last, own, cube[first:first + sent, :]).astype(bf16)
+                out_ref[s * grid_count + g] = value.reshape(sent // 2, 2, lanes)
 
     return pl.pallas_call(
         kernel,
-        out_shape=jax.ShapeDtypeStruct((slab_count * grid_count, part + 1, lanes), bf16),
+        out_shape=jax.ShapeDtypeStruct((slab_count * grid_count, sent // 2, 2, lanes), bf16),
         in_specs=[whole] * (1 + grid_count + len(tables)),
         out_specs=whole,
         scratch_shapes=[
@@ -412,16 +427,16 @@
     )(at, *pieces, *tables)
 
 
-def apply_part(orbitals, notes, received, count, slab_count):
+def apply_part(orbitals, notes, received, part, count, slab_count):
     occupied, shard_len = orbitals.shape
-    points, part = received.shape[0], received.shape[1] - 1
+    points, sent = received.shape[0], 2 * received.shape[1]
     keep = count // slab_count
-    pitch = -(-(part + 1) // 8) * 8
+    pitch = -(-sent // 8) * 8
     prefactor = -1.0 / math.sqrt(points)
 
     def kernel(notes_ref, orbitals_ref, received_ref, out_ref, spread, mid, stage):
         for m in range(points):
-            spread[m * pitch:m * pitch + part + 1, :] = received_ref[m].astype(f32)
+            spread[m * pitch:m * pitch + sent, :] = received_ref[m].reshape(sent, lanes).astype(f32)
         at = spread[pl.ds(part, points, stride=pitch), :][:, :occupied].astype(bf16)
         first = pl.multiple_of(lax.axis_index("slab") * (part * lanes), lanes)
         density = jnp.dot(at, orbitals_ref[:, pl.ds(first, part * lanes)], preferred_element_type=f32)
@@ -488,7 +503,7 @@
     pieces = pieces[:1] + [exchange(pieces[d], grid_count, d) for d in range(1, grid_count)]
     sent = potentials(plan, pieces, at, slab_count)
     received = lax.all_to_all(sent, everyone, 0, 0)
-    blocks = apply_part(orbitals, notes, received, targets.shape[0], slab_count)
+    blocks = apply_part(orbitals, notes, received, shard_len // lanes // slab_count, targets.shape[0], slab_count)
     kept = lax.all_to_all(blocks, "slab", 0, 0)
     return jnp.transpose(settle(kept, keep), (1, 0, 2)).reshape(keep, shard_len)
 

time: 43.3 us -> 42.6 us (0.984)
  blocking collectives: 25.5 us -> 24.9 us
    all_to_all x1, blocking collectives: 15.7 us -> 14.9 us  [quick_body(): received = lax.all_to_all(sent, everyone, 0, 0)]
where the time goes in v4:
time: 42.6 us; the launch traced here: 42.4 us
  blocking collectives  24.9 us (58%)
  Pallas kernels  6.14 us (14%)
  waiting for transfers between devices  6.09 us (14%)
  starting transfers between devices  5.08 us (12%)
    all_to_all x1, blocking collectives, quick_body(): received = lax.all_to_all(sent, everyone, 0, 0)  14.9 us
    all_to_all x1, blocking collectives, quick_body(): kept = lax.all_to_all(blocks, 'slab', 0, 0)  10 us
    ppermute x6, waiting for transfers between devices, exchange(): lax.ppermute(value, 'grid', [(i, i ^ offset) for i in range(grid_count)])  6.09 us
    ppermute x6, starting transfers between devices, exchange(): lax.ppermute(value, 'grid', [(i, i ^ offset) for i in range(grid_count)])  5.08 us
    pallas_call x1, Pallas kernels, read_points(): pl.pallas_call(kernel, out_shape=[pltpu.VMEM((8, lanes), f32), pltpu.VMEM...  2.17 us
    pallas_call x1, Pallas kernels, potentials(): pl.pallas_call(kernel, out_shape=jax.ShapeDtypeStruct((slab_count * grid_...  1.77 us
  transfers between devices with their start and end apart: 6, of which 4 were waited for; matrix products, arithmetic and copies ran while one was open for 0% of the time, Pallas kernels for 0%

profile of v4, /device:TPU:0, one launch (start us, length us, event | category | flops | bytes accessed | tf_op | source)
XLA Modules:
  0.0 42.4 jit_solution(13168194517452503185)
XLA Ops:
  0.0 0.0 copy-start
  0.0 0.0 copy-start.1
  0.0 0.0 copy-start.2
  0.0 0.0 copy-start.3
  0.0 0.0 copy-start.4
  0.0 0.0 copy-start.5
  0.0 0.0 copy-start.6
  0.0 2.2 %read_points.1 = (f32[8,128]{1,0:T(8,128)S(1)}, f32[56,128]{1,0:T(8,128)S(1)}) custom-call(s32[4]{0:T(128)} %points_hbm.1, s32[16]{0:T(128)} %targets_hbm.1, f32[4,4]{1,0:T(4,128)} %fit_hbm.1, bf16[64,27648]{1,0:T(8,128)(2,1)} %orbitals_ref.5), custom_call_target="tpu_custom_call" | custom-call | tf_op jit(solution)/shard_map/read_points/pallas_call | solution.py:331
  2.2 2.5 %collective-permute-start.2 = (f32[8,128]{1,0:T(8,128)S(1)}, f32[8,128]{1,0:T(8,128)S(1)}, u32[]{:S(2)}, u32[]{:S(2)}) collective-permute-start(f32[8,128]{1,0:T(8,128)S(1)} %get-tuple-element.13.refs_0_), channel_id=1, source_target_pairs={{0,3},{1,2},{2,1},{3,0},{4,7},{5,6},{6,5},{7,4},{8,11},{9,10},{10,... | collective-permute-start | bytes 12296 | tf_op jit(solution)/shard_map/ppermute | solution.py:491
  4.7 0.6 %collective-permute-start.1 = (f32[8,128]{1,0:T(8,128)S(1)}, f32[8,128]{1,0:T(8,128)S(1)}, u32[]{:S(2)}, u32[]{:S(2)}) collective-permute-start(f32[8,128]{1,0:T(8,128)S(1)} %get-tuple-element.13.refs_0_), channel_id=1, source_target_pairs={{0,2},{1,3},{2,0},{3,1},{4,6},{5,7},{6,4},{7,5},{8,10},{9,11},{10,... | collective-permute-start | bytes 12296 | tf_op jit(solution)/shard_map/ppermute | solution.py:491
  5.3 0.0 collective-permute-start
  5.4 0.6 %collective-permute-done.2.refs_3_ = f32[8,128]{1,0:T(8,128)S(1)} collective-permute-done((f32[8,128]{1,0:T(8,128)S(1)}, f32[8,128]{1,0:T(8,128)S(1)}, u32[]{:S(2)}, u32[]{:S(2)}) %collective-permute-start.2) | collective-permute-done | bytes 4128 | tf_op jit(solution)/shard_map/ppermute | solution.py:491
  6.0 2.3 %collective-permute-done.1.refs_2_ = f32[8,128]{1,0:T(8,128)S(1)} collective-permute-done((f32[8,128]{1,0:T(8,128)S(1)}, f32[8,128]{1,0:T(8,128)S(1)}, u32[]{:S(2)}, u32[]{:S(2)}) %collective-permute-start.1) | collective-permute-done | bytes 4128 | tf_op jit(solution)/shard_map/ppermute | solution.py:491
  8.3 0.0 collective-permute-done.refs_1_
  8.3 0.0 copy-done
  8.3 0.7 %fit_pairs.1 = (bf16[216,128]{1,0:T(8,128)(2,1)S(1)}, bf16[216,128]{1,0:T(8,128)(2,1)S(1)}, bf16[216,128]{1,0:T(8,128)(2,1)S(1)}, bf16[216,128]{1,0:T(8,128)(2,1)S(1)}, f32[8,128]{1,0:T(8,128)S(1)}) custom-call(f32[56,128]{1,0:T(8,128)S(1)} %get-tuple-element.12.notes_ref, bf16[64,27648]{1,0:T(8,128)(2,1)S(1)} %copy-done, ...), custom_call_target="tpu_custom_call" | custom-call | tf_op jit(solution)/shard_map/fit_pairs/pallas_call | solution.py:383
  9.1 0.1 collective-permute-start.3
  9.1 0.7 %collective-permute-start.4 = (bf16[216,128]{1,0:T(8,128)(2,1)S(1)}, bf16[216,128]{1,0:T(8,128)(2,1)S(1)}, u32[]{:S(2)}, u32[]{:S(2)}) collective-permute-start(bf16[216,128]{1,0:T(8,128)(2,1)S(1)} %get-tuple-element.17), channel_id=1, source_target_pairs={{0,2},{1,3},{2,0},{3,1},{4,6},{5,7},{6,4},{7,5},{8,10},{9,11},{10,... | collective-permute-start | bytes 165896 | tf_op jit(solution)/shard_map/ppermute | solution.py:491
  9.8 1.2 %collective-permute-start.5 = (bf16[216,128]{1,0:T(8,128)(2,1)S(1)}, bf16[216,128]{1,0:T(8,128)(2,1)S(1)}, u32[]{:S(2)}, u32[]{:S(2)}) collective-permute-start(bf16[216,128]{1,0:T(8,128)(2,1)S(1)} %get-tuple-element.18), channel_id=1, source_target_pairs={{0,3},{1,2},{2,1},{3,0},{4,7},{5,6},{6,5},{7,4},{8,11},{9,10},{10,... | collective-permute-start | bytes 165896 | tf_op jit(solution)/shard_map/ppermute | solution.py:491
  11.0 0.0 collective-permute-done.3.refs_1_
  11.0 2.9 %collective-permute-done.4.refs_2_ = bf16[216,128]{1,0:T(8,128)(2,1)S(1)} collective-permute-done((bf16[216,128]{1,0:T(8,128)(2,1)S(1)}, bf16[216,128]{1,0:T(8,128)(2,1)S(1)}, u32[]{:S(2)}, u32[]{:S(2)}) %collective-permute-start.4) | collective-permute-done | bytes 55328 | tf_op jit(solution)/shard_map/ppermute | solution.py:491
  13.9 0.3 collective-permute-done.5.refs_3_
  14.2 0.0 copy-done.1
  14.2 0.0 copy-done.2
  14.2 0.0 copy-done.3
  14.2 0.0 copy-done.4
  14.2 0.0 copy-done.5
  14.2 0.0 copy-done.6
  14.2 1.8 %potentials.1 = bf16[32,14,2,128]{3,2,1,0:T(2,128)(2,1)S(1)} custom-call(f32[8,128]{1,0:T(8,128)S(1)} %get-tuple-element.14.at_ref, bf16[216,128]{1,0:T(8,128)(2,1)S(1)} %get-tuple-element.15.refs_0_, bf16[216,128]{1,0:T(8,128)(2,1)S(1)} %collective-permute-done.3.refs_1_, bf16[216,128]{1,0:T(8,128)(2,1)S(1)} %collective-permute-done.4.refs_2_, ...), custom_call_target="tpu_custom_call" | custom-call | tf_op jit(solution)/shard_map/potentials/pallas_call | solution.py:416
  16.0 14.9 %all_to_all.10.received_ref = bf16[32,14,2,128]{3,2,1,0:T(2,128)(2,1)S(1)} all-to-all(bf16[32,14,2,128]{3,2,1,0:T(2,128)(2,1)S(1)} %potentials.1), channel_id=1, replica_groups=mesh['slab'=8,'grid'=4] {'slab','grid'}, dimensions={0} | all-to-all | bytes 458752 | tf_op jit(solution)/shard_map/all_to_all | solution.py:505
  30.9 0.6 %apply_part.1 = bf16[8,54,128]{2,1,0:T(8,128)(2,1)S(1)} custom-call(f32[56,128]{1,0:T(8,128)S(1)} %get-tuple-element.12.notes_ref, bf16[64,27648]{1,0:T(8,128)(2,1)S(1)} %copy-done, bf16[32,14,2,128]{3,2,1,0:T(2,128)(2,1)S(1)} %all_to_all.10.received_ref), custom_call_target="tpu_custom_call" | custom-call | tf_op jit(solution)/shard_map/apply_part/pallas_call | solution.py:455
  31.5 10.0 %all_to_all.11.kept_ref = bf16[8,54,128]{2,1,0:T(8,128)(2,1)S(1)} all-to-all(bf16[8,54,128]{2,1,0:T(8,128)(2,1)S(1)} %apply_part.1), channel_id=1, replica_groups=mesh['slab'=8,'grid'=4] {'slab'}, dimensions={0} | all-to-all | bytes 221184 | tf_op jit(solution)/shard_map/all_to_all | solution.py:507
  41.5 0.8 %settle.1 = f32[216,2,128]{2,1,0:T(2,128)} custom-call(bf16[8,54,128]{2,1,0:T(8,128)(2,1)S(1)} %all_to_all.11.kept_ref), custom_call_target="tpu_custom_call" | custom-call | tf_op jit(solution)/shard_map/settle/pallas_call | solution.py:479
Async XLA Ops:
  0.0 8.3 %copy-start = (bf16[64,27648]{1,0:T(8,128)(2,1)S(1)}, bf16[64,27648]{1,0:T(8,128)(2,1)}, u32[]{:S(2)}) copy-start(bf16[64,27648]{1,0:T(8,128)(2,1)} %orbitals_ref.5) | copy-start | bytes 10616836
  0.0 14.2 %copy-start.1 = (f32[24,48,128]{2,1,0:T(8,128)S(1)}, f32[24,48,128]{2,1,0:T(8,128)}, u32[]{:S(2)}) copy-start(f32[24,48,128]{2,1,0:T(8,128)} %constant.17.clone.refs_9_) | copy-start | bytes 1769476
  0.0 14.2 %copy-start.2 = (bf16[1024,256]{1,0:T(8,128)(2,1)S(1)}, bf16[1024,256]{1,0:T(8,128)(2,1)}, u32[]{:S(2)}) copy-start(bf16[1024,256]{1,0:T(8,128)(2,1)} %constant.16.clone.refs_8_) | copy-start | bytes 1572868
  0.0 14.2 %copy-start.3 = (bf16[1024,256]{1,0:T(8,128)(2,1)S(1)}, bf16[1024,256]{1,0:T(8,128)(2,1)}, u32[]{:S(2)}) copy-start(bf16[1024,256]{1,0:T(8,128)(2,1)} %constant.15.clone.refs_7_) | copy-start | bytes 1572868
  0.0 14.2 %copy-start.4 = (bf16[1024,256]{1,0:T(8,128)(2,1)S(1)}, bf16[1024,256]{1,0:T(8,128)(2,1)}, u32[]{:S(2)}) copy-start(bf16[1024,256]{1,0:T(8,128)(2,1)} %constant.14.clone.refs_6_) | copy-start | bytes 1572868
  0.0 14.2 %copy-start.5 = (bf16[1024,256]{1,0:T(8,128)(2,1)S(1)}, bf16[1024,256]{1,0:T(8,128)(2,1)}, u32[]{:S(2)}) copy-start(bf16[1024,256]{1,0:T(8,128)(2,1)} %constant.13.clone.refs_5_) | copy-start | bytes 1572868
  0.0 14.2 %copy-start.6 = (bf16[48,144]{1,0:T(8,128)(2,1)S(1)}, bf16[48,144]{1,0:T(8,128)(2,1)}, u32[]{:S(2)}) copy-start(bf16[48,144]{1,0:T(8,128)(2,1)} %constant.12.clone.refs_4_) | copy-start | bytes 41476
  2.2 3.8 %collective-permute-start.2 = (f32[8,128]{1,0:T(8,128)S(1)}, f32[8,128]{1,0:T(8,128)S(1)}, u32[]{:S(2)}, u32[]{:S(2)}) collective-permute-start(f32[8,128]{1,0:T(8,128)S(1)} %get-tuple-element.13.refs_0_), channel_id=1, source_target_pairs={{0,3},{1,2},{2,1},{3,0},{4,7},{5,6},{6,5},{7,4},{8,11},{9,10},{10,... | collective-permute-start | bytes 12296 | tf_op jit(solution)/shard_map/ppermute | solution.py:491
  4.7 3.6 %collective-permute-start.1 = (f32[8,128]{1,0:T(8,128)S(1)}, f32[8,128]{1,0:T(8,128)S(1)}, u32[]{:S(2)}, u32[]{:S(2)}) collective-permute-start(f32[8,128]{1,0:T(8,128)S(1)} %get-tuple-element.13.refs_0_), channel_id=1, source_target_pairs={{0,2},{1,3},{2,0},{3,1},{4,6},{5,7},{6,4},{7,5},{8,10},{9,11},{10,... | collective-permute-start | bytes 12296 | tf_op jit(solution)/shard_map/ppermute | solution.py:491
  5.3 3.0 %collective-permute-start = (f32[8,128]{1,0:T(8,128)S(1)}, f32[8,128]{1,0:T(8,128)S(1)}, u32[]{:S(2)}, u32[]{:S(2)}) collective-permute-start(f32[8,128]{1,0:T(8,128)S(1)} %get-tuple-element.13.refs_0_), channel_id=1, source_target_pairs={{0,1},{1,0},{2,3},{3,2},{4,5},{5,4},{6,7},{7,6},{8,9},{9,8},{10,11... | collective-permute-start | bytes 12296 | tf_op jit(solution)/shard_map/ppermute | solution.py:491
  9.1 1.9 %collective-permute-start.3 = (bf16[216,128]{1,0:T(8,128)(2,1)S(1)}, bf16[216,128]{1,0:T(8,128)(2,1)S(1)}, u32[]{:S(2)}, u32[]{:S(2)}) collective-permute-start(bf16[216,128]{1,0:T(8,128)(2,1)S(1)} %get-tuple-element.16), channel_id=1, source_target_pairs={{0,1},{1,0},{2,3},{3,2},{4,5},{5,4},{6,7},{7,6},{8,9},{9,8},{10,11... | collective-permute-start | bytes 165896 | tf_op jit(solution)/shard_map/ppermute | solution.py:491
  9.1 4.7 %collective-permute-start.4 = (bf16[216,128]{1,0:T(8,128)(2,1)S(1)}, bf16[216,128]{1,0:T(8,128)(2,1)S(1)}, u32[]{:S(2)}, u32[]{:S(2)}) collective-permute-start(bf16[216,128]{1,0:T(8,128)(2,1)S(1)} %get-tuple-element.17), channel_id=1, source_target_pairs={{0,2},{1,3},{2,0},{3,1},{4,6},{5,7},{6,4},{7,5},{8,10},{9,11},{10,... | collective-permute-start | bytes 165896 | tf_op jit(solution)/shard_map/ppermute | solution.py:491
  9.8 4.3 %collective-permute-start.5 = (bf16[216,128]{1,0:T(8,128)(2,1)S(1)}, bf16[216,128]{1,0:T(8,128)(2,1)S(1)}, u32[]{:S(2)}, u32[]{:S(2)}) collective-permute-start(bf16[216,128]{1,0:T(8,128)(2,1)S(1)} %get-tuple-element.18), channel_id=1, source_target_pairs={{0,3},{1,2},{2,1},{3,0},{4,7},{5,6},{6,5},{7,4},{8,11},{9,10},{10,... | collective-permute-start | bytes 165896 | tf_op jit(solution)/shard_map/ppermute | solution.py:491

commit v5 on v4

--- a/solution.py
+++ b/solution.py
@@ -7,6 +7,7 @@
 from jax import lax
 from jax.experimental import pallas as pl
 from jax.experimental.pallas import tpu as pltpu
+from jax.sharding import Mesh
 from jax.sharding import PartitionSpec as P
 
 NG = 48
@@ -17,7 +18,6 @@
 lanes = 128
 f32 = jnp.float32
 bf16 = jnp.bfloat16
-everyone = ("slab", "grid")
 contract_last = (((1,), (1,)), ((), ()))
 
 
@@ -391,10 +391,10 @@
     )(notes, orbitals, *shares)
 
 
-def potentials(plan, pieces, at, slab_count):
+def potentials(plan, pieces, at, parts):
     grid_count, piece_rows = len(pieces), pieces[0].shape[0]
-    part = piece_rows // slab_count
-    sent = 2 * (part // 2 + 1)
+    part = piece_rows // parts
+    sent = -(-(part + 1) // 8) * 8
     tables = plan.tables()
 
     def kernel(at_ref, *refs):
@@ -408,14 +408,13 @@
         own = jnp.broadcast_to(at_ref[pl.ds(me, 1), :], (sent, lanes))
         last = iota((sent, lanes), 0) >= part
         for g in range(grid_count):
-            for s in range(slab_count):
-                first = g * piece_rows + s * part
-                value = jnp.where(last, own, cube[first:first + sent, :]).astype(bf16)
-                out_ref[s * grid_count + g] = value.reshape(sent // 2, 2, lanes)
+            for q in range(parts):
+                first = g * piece_rows + q * part
+                out_ref[q * grid_count + g] = jnp.where(last, own, cube[first:first + sent, :]).astype(bf16)
 
     return pl.pallas_call(
         kernel,
-        out_shape=jax.ShapeDtypeStruct((slab_count * grid_count, sent // 2, 2, lanes), bf16),
+        out_shape=jax.ShapeDtypeStruct((parts * grid_count, sent, lanes), bf16),
         in_specs=[whole] * (1 + grid_count + len(tables)),
         out_specs=whole,
         scratch_shapes=[
@@ -427,18 +426,17 @@
     )(at, *pieces, *tables)
 
 
-def apply_part(orbitals, notes, received, part, count, slab_count):
+def apply_part(orbitals, notes, received, part, count, slab_count, halves):
     occupied, shard_len = orbitals.shape
-    points, sent = received.shape[0], 2 * received.shape[1]
+    points, pitch = received.shape[:2]
     keep = count // slab_count
-    pitch = -(-sent // 8) * 8
-    prefactor = -1.0 / math.sqrt(points)
+    prefactor = -1.0 / math.sqrt(points * halves)
 
     def kernel(notes_ref, orbitals_ref, received_ref, out_ref, spread, mid, stage):
         for m in range(points):
-            spread[m * pitch:m * pitch + sent, :] = received_ref[m].reshape(sent, lanes).astype(f32)
+            spread[m * pitch:(m + 1) * pitch, :] = received_ref[m].astype(f32)
         at = spread[pl.ds(part, points, stride=pitch), :][:, :occupied].astype(bf16)
-        first = pl.multiple_of(lax.axis_index("slab") * (part * lanes), lanes)
+        first = pl.multiple_of(lax.axis_index("part") * (part * lanes), lanes)
         density = jnp.dot(at, orbitals_ref[:, pl.ds(first, part * lanes)], preferred_element_type=f32)
         chosen = notes_ref[notes_ref.shape[0] - count:, :][:, :occupied].astype(bf16)
         target_points = lax.dot_general(chosen, at, contract_last, preferred_element_type=f32).astype(bf16)
@@ -467,21 +465,25 @@
     )(notes, orbitals, received)
 
 
-def settle(kept, keep):
-    slab_count, part = kept.shape[0], kept.shape[1] // keep
+def settle(kept, keep, halves):
+    parts, rows = kept.shape[0] // halves, kept.shape[1]
+    part = rows // keep
 
     def kernel(kept_ref, out_ref, stage):
-        for s in range(slab_count):
-            stage[s] = kept_ref[s].astype(f32)
+        for q in range(parts):
+            total = kept_ref[q].astype(f32)
+            for h in range(1, halves):
+                total = total + kept_ref[h * parts + q].astype(f32)
+            stage[q] = total
             for k in range(keep):
-                out_ref[s * part:(s + 1) * part, k, :] = stage[s, k * part:(k + 1) * part, :]
+                out_ref[q * part:(q + 1) * part, k, :] = stage[q, k * part:(k + 1) * part, :]
 
     return pl.pallas_call(
         kernel,
-        out_shape=jax.ShapeDtypeStruct((slab_count * part, keep, lanes), f32),
+        out_shape=jax.ShapeDtypeStruct((parts * part, keep, lanes), f32),
         in_specs=[whole],
         out_specs=whole,
-        scratch_shapes=[pltpu.VMEM(kept.shape, f32)],
+        scratch_shapes=[pltpu.VMEM((parts, rows, lanes), f32)],
         compiler_params=params(4),
         name="settle",
     )(kept)
@@ -492,20 +494,21 @@
 
 
 def quick_body(orbitals, targets, points, fit):
-    grid_count, slab_count = lax.axis_size("grid"), lax.axis_size("slab")
-    shard_len = orbitals.shape[1]
-    edge = round((shard_len * grid_count) ** (1 / 3))
-    keep = targets.shape[0] // slab_count
-    plan = Plan(edge)
+    grid_count, part_count, halves = (lax.axis_size(name) for name in ("grid", "part", "half"))
+    shard_len, slab_count = orbitals.shape[1], part_count * halves
+    count = targets.shape[0]
+    keep = count // slab_count
+    part = shard_len // lanes // part_count
+    plan = Plan(round((shard_len * grid_count) ** (1 / 3)))
     share, notes = read_points(orbitals, targets, points, fit)
     shares = [share] + [exchange(share, grid_count, d) for d in range(1, grid_count)]
     *pieces, at = fit_pairs(orbitals, notes, shares)
     pieces = pieces[:1] + [exchange(pieces[d], grid_count, d) for d in range(1, grid_count)]
-    sent = potentials(plan, pieces, at, slab_count)
-    received = lax.all_to_all(sent, everyone, 0, 0)
-    blocks = apply_part(orbitals, notes, received, shard_len // lanes // slab_count, targets.shape[0], slab_count)
-    kept = lax.all_to_all(blocks, "slab", 0, 0)
-    return jnp.transpose(settle(kept, keep), (1, 0, 2)).reshape(keep, shard_len)
+    sent = potentials(plan, pieces, at, part_count)
+    received = lax.all_to_all(sent, ("part", "grid"), 0, 0)
+    blocks = apply_part(orbitals, notes, received, part, count, slab_count, halves)
+    kept = lax.all_to_all(blocks, ("half", "part"), 0, 0)
+    return jnp.transpose(settle(kept, keep, halves), (1, 0, 2)).reshape(keep, shard_len)
 
 
 def quick_fits(mesh, orbitals, targets, points, fit):
@@ -523,18 +526,25 @@
         and edge <= lanes // 2
         and cells % (grid_count * lanes) == 0
         and shard_rows % 8 == 0
-        and shard_rows % slab_count == 0
+        and slab_count % 2 == 0
+        and shard_rows % (slab_count // 2) == 0
         and targets.shape[0] % slab_count == 0
         and targets.shape[0] % 8 == 0
     )
 
 
 def solution(mesh):
-    in_specs = (P(None, "grid"), P(), P("slab"), P("slab", None))
+    grid_count, slab_count = mesh.shape["grid"], mesh.shape["slab"]
     out_specs = P("slab", "grid")
 
     def run(*arrays):
-        body = quick_body if quick_fits(mesh, *arrays) else plain_body
-        return jax.shard_map(body, mesh=mesh, in_specs=in_specs, out_specs=out_specs, check_vma=False)(*arrays)
+        if not quick_fits(mesh, *arrays):
+            in_specs = (P(None, "grid"), P(), P("slab"), P("slab", None))
+            return jax.shard_map(plain_body, mesh=mesh, in_specs=in_specs, out_specs=out_specs, check_vma=False)(*arrays)
+        halved = Mesh(mesh.devices.reshape(2, slab_count // 2, grid_count), ("half", "part", "grid"))
+        slab = ("half", "part")
+        in_specs = (P(None, "grid"), P(), P(slab), P(slab, None))
+        return jax.shard_map(
+            quick_body, mesh=halved, in_specs=in_specs, out_specs=P(slab, "grid"), check_vma=False)(*arrays)
 
     return run

time: 42.6 us -> 41.2 us (0.967)
  blocking collectives: 24.9 us -> 23.7 us
    all_to_all x2, blocking collectives: 24.9 us -> 23.7 us  [the longest x1 12.3 us: quick_body(): kept = lax.all_to_all(blocks, ('half', 'part'), 0, 0)]
where the time goes in v5:
time: 41.2 us; the launch traced here: 41 us
  blocking collectives  23.7 us (58%)
  waiting for transfers between devices  6.09 us (15%)
  Pallas kernels  5.98 us (15%)
  starting transfers between devices  5.08 us (12%)
    all_to_all x1, blocking collectives, quick_body(): kept = lax.all_to_all(blocks, ('half', 'part'), 0, 0)  12.3 us
    all_to_all x1, blocking collectives, quick_body(): received = lax.all_to_all(sent, ('part', 'grid'), 0, 0)  11.4 us
    ppermute x6, waiting for transfers between devices, exchange(): lax.ppermute(value, 'grid', [(i, i ^ offset) for i in range(grid_count)])  6.09 us
    ppermute x6, starting transfers between devices, exchange(): lax.ppermute(value, 'grid', [(i, i ^ offset) for i in range(grid_count)])  5.08 us
    pallas_call x1, Pallas kernels, read_points(): pl.pallas_call(kernel, out_shape=[pltpu.VMEM((8, lanes), f32), pltpu.VMEM...  2.17 us
    pallas_call x1, Pallas kernels, potentials(): pl.pallas_call(kernel, out_shape=jax.ShapeDtypeStruct((parts * grid_count...  1.67 us
    pallas_call x1, Pallas kernels, settle(): pl.pallas_call(kernel, out_shape=jax.ShapeDtypeStruct((parts * part, keep...  0.84 us
  transfers between devices with their start and end apart: 6, of which 4 were waited for; matrix products, arithmetic and copies ran while one was open for 0% of the time, Pallas kernels for 0%

profile of v5, /device:TPU:0, one launch (start us, length us, event | category | flops | bytes accessed | tf_op | source)
XLA Modules:
  0.0 41.0 jit_solution(18170804490358266537)
XLA Ops:
  0.0 0.0 copy-start
  0.0 0.0 copy-start.1
  0.0 0.0 copy-start.2
  0.0 0.0 copy-start.3
  0.0 0.0 copy-start.4
  0.0 0.0 copy-start.5
  0.0 0.0 copy-start.6
  0.0 2.2 %read_points.1 = (f32[8,128]{1,0:T(8,128)S(1)}, f32[56,128]{1,0:T(8,128)S(1)}) custom-call(s32[4]{0:T(128)} %points_hbm.1, s32[16]{0:T(128)} %targets_hbm.1, f32[4,4]{1,0:T(4,128)} %fit_hbm.1, bf16[64,27648]{1,0:T(8,128)(2,1)} %orbitals_ref.5), custom_call_target="tpu_custom_call" | custom-call | tf_op jit(solution)/shard_map/read_points/pallas_call | solution.py:331
  2.2 2.5 %collective-permute-start.2 = (f32[8,128]{1,0:T(8,128)S(1)}, f32[8,128]{1,0:T(8,128)S(1)}, u32[]{:S(2)}, u32[]{:S(2)}) collective-permute-start(f32[8,128]{1,0:T(8,128)S(1)} %get-tuple-element.13.refs_0_), channel_id=1, source_target_pairs={{0,3},{1,2},{2,1},{3,0},{4,7},{5,6},{6,5},{7,4},{8,11},{9,10},{10,... | collective-permute-start | bytes 12296 | tf_op jit(solution)/shard_map/ppermute | solution.py:493
  4.7 0.6 %collective-permute-start.1 = (f32[8,128]{1,0:T(8,128)S(1)}, f32[8,128]{1,0:T(8,128)S(1)}, u32[]{:S(2)}, u32[]{:S(2)}) collective-permute-start(f32[8,128]{1,0:T(8,128)S(1)} %get-tuple-element.13.refs_0_), channel_id=1, source_target_pairs={{0,2},{1,3},{2,0},{3,1},{4,6},{5,7},{6,4},{7,5},{8,10},{9,11},{10,... | collective-permute-start | bytes 12296 | tf_op jit(solution)/shard_map/ppermute | solution.py:493
  5.3 0.0 collective-permute-start
  5.4 0.6 %collective-permute-done.2.refs_3_ = f32[8,128]{1,0:T(8,128)S(1)} collective-permute-done((f32[8,128]{1,0:T(8,128)S(1)}, f32[8,128]{1,0:T(8,128)S(1)}, u32[]{:S(2)}, u32[]{:S(2)}) %collective-permute-start.2) | collective-permute-done | bytes 4128 | tf_op jit(solution)/shard_map/ppermute | solution.py:493
  6.0 2.3 %collective-permute-done.1.refs_2_ = f32[8,128]{1,0:T(8,128)S(1)} collective-permute-done((f32[8,128]{1,0:T(8,128)S(1)}, f32[8,128]{1,0:T(8,128)S(1)}, u32[]{:S(2)}, u32[]{:S(2)}) %collective-permute-start.1) | collective-permute-done | bytes 4128 | tf_op jit(solution)/shard_map/ppermute | solution.py:493
  8.3 0.0 collective-permute-done.refs_1_
  8.3 0.0 copy-done
  8.3 0.7 %fit_pairs.1 = (bf16[216,128]{1,0:T(8,128)(2,1)S(1)}, bf16[216,128]{1,0:T(8,128)(2,1)S(1)}, bf16[216,128]{1,0:T(8,128)(2,1)S(1)}, bf16[216,128]{1,0:T(8,128)(2,1)S(1)}, f32[8,128]{1,0:T(8,128)S(1)}) custom-call(f32[56,128]{1,0:T(8,128)S(1)} %get-tuple-element.12.notes_ref, bf16[64,27648]{1,0:T(8,128)(2,1)S(1)} %copy-done, ...), custom_call_target="tpu_custom_call" | custom-call | tf_op jit(solution)/shard_map/fit_pairs/pallas_call | solution.py:383
  9.1 0.1 collective-permute-start.3
  9.1 0.7 %collective-permute-start.4 = (bf16[216,128]{1,0:T(8,128)(2,1)S(1)}, bf16[216,128]{1,0:T(8,128)(2,1)S(1)}, u32[]{:S(2)}, u32[]{:S(2)}) collective-permute-start(bf16[216,128]{1,0:T(8,128)(2,1)S(1)} %get-tuple-element.17), channel_id=1, source_target_pairs={{0,2},{1,3},{2,0},{3,1},{4,6},{5,7},{6,4},{7,5},{8,10},{9,11},{10,... | collective-permute-start | bytes 165896 | tf_op jit(solution)/shard_map/ppermute | solution.py:493
  9.8 1.2 %collective-permute-start.5 = (bf16[216,128]{1,0:T(8,128)(2,1)S(1)}, bf16[216,128]{1,0:T(8,128)(2,1)S(1)}, u32[]{:S(2)}, u32[]{:S(2)}) collective-permute-start(bf16[216,128]{1,0:T(8,128)(2,1)S(1)} %get-tuple-element.18), channel_id=1, source_target_pairs={{0,3},{1,2},{2,1},{3,0},{4,7},{5,6},{6,5},{7,4},{8,11},{9,10},{10,... | collective-permute-start | bytes 165896 | tf_op jit(solution)/shard_map/ppermute | solution.py:493
  11.0 0.0 collective-permute-done.3.refs_1_
  11.0 2.9 %collective-permute-done.4.refs_2_ = bf16[216,128]{1,0:T(8,128)(2,1)S(1)} collective-permute-done((bf16[216,128]{1,0:T(8,128)(2,1)S(1)}, bf16[216,128]{1,0:T(8,128)(2,1)S(1)}, u32[]{:S(2)}, u32[]{:S(2)}) %collective-permute-start.4) | collective-permute-done | bytes 55328 | tf_op jit(solution)/shard_map/ppermute | solution.py:493
  13.9 0.3 collective-permute-done.5.refs_3_
  14.2 0.0 copy-done.1
  14.2 0.0 copy-done.2
  14.2 0.0 copy-done.3
  14.2 0.0 copy-done.4
  14.2 0.0 copy-done.5
  14.2 0.0 copy-done.6
  14.2 1.7 %potentials.1 = bf16[16,56,128]{2,1,0:T(8,128)(2,1)S(1)} custom-call(f32[8,128]{1,0:T(8,128)S(1)} %get-tuple-element.14.at_ref, bf16[216,128]{1,0:T(8,128)(2,1)S(1)} %get-tuple-element.15.refs_0_, bf16[216,128]{1,0:T(8,128)(2,1)S(1)} %collective-permute-done.3.refs_1_, bf16[216,128]{1,0:T(8,128)(2,1)S(1)} %collective-permute-done.4.refs_2_, ...), custom_call_target="tpu_custom_call" | custom-call | tf_op jit(solution)/shard_map/potentials/pallas_call | solution.py:415
  15.9 11.4 %all_to_all.10.received_ref = bf16[16,56,128]{2,1,0:T(8,128)(2,1)S(1)} all-to-all(bf16[16,56,128]{2,1,0:T(8,128)(2,1)S(1)} %potentials.1), channel_id=1, replica_groups=mesh['half'=2,'part'=4,'grid'=4] {'part','grid'}, dimensions={0} | all-to-all | bytes 458752 | tf_op jit(solution)/shard_map/all_to_all | solution.py:508
  27.3 0.6 %apply_part.1 = bf16[8,108,128]{2,1,0:T(8,128)(2,1)S(1)} custom-call(f32[56,128]{1,0:T(8,128)S(1)} %get-tuple-element.12.notes_ref, bf16[64,27648]{1,0:T(8,128)(2,1)S(1)} %copy-done, bf16[16,56,128]{2,1,0:T(8,128)(2,1)S(1)} %all_to_all.10.received_ref), custom_call_target="tpu_custom_call" | custom-call | tf_op jit(solution)/shard_map/apply_part/pallas_call | solution.py:453
  27.9 12.3 %all_to_all.11.kept_ref = bf16[8,108,128]{2,1,0:T(8,128)(2,1)S(1)} all-to-all(bf16[8,108,128]{2,1,0:T(8,128)(2,1)S(1)} %apply_part.1), channel_id=1, replica_groups=mesh['half'=2,'part'=4,'grid'=4] {'half','part'}, dimensions={0} | all-to-all | bytes 442368 | tf_op jit(solution)/shard_map/all_to_all | solution.py:510
  40.2 0.8 %settle.1 = f32[216,2,128]{2,1,0:T(2,128)} custom-call(bf16[8,108,128]{2,1,0:T(8,128)(2,1)S(1)} %all_to_all.11.kept_ref), custom_call_target="tpu_custom_call" | custom-call | tf_op jit(solution)/shard_map/settle/pallas_call | solution.py:481
Async XLA Ops:
  0.0 8.3 %copy-start = (bf16[64,27648]{1,0:T(8,128)(2,1)S(1)}, bf16[64,27648]{1,0:T(8,128)(2,1)}, u32[]{:S(2)}) copy-start(bf16[64,27648]{1,0:T(8,128)(2,1)} %orbitals_ref.5) | copy-start | bytes 10616836
  0.0 14.2 %copy-start.1 = (f32[24,48,128]{2,1,0:T(8,128)S(1)}, f32[24,48,128]{2,1,0:T(8,128)}, u32[]{:S(2)}) copy-start(f32[24,48,128]{2,1,0:T(8,128)} %constant.17.clone.refs_9_) | copy-start | bytes 1769476
  0.0 14.2 %copy-start.2 = (bf16[1024,256]{1,0:T(8,128)(2,1)S(1)}, bf16[1024,256]{1,0:T(8,128)(2,1)}, u32[]{:S(2)}) copy-start(bf16[1024,256]{1,0:T(8,128)(2,1)} %constant.16.clone.refs_8_) | copy-start | bytes 1572868
  0.0 14.2 %copy-start.3 = (bf16[1024,256]{1,0:T(8,128)(2,1)S(1)}, bf16[1024,256]{1,0:T(8,128)(2,1)}, u32[]{:S(2)}) copy-start(bf16[1024,256]{1,0:T(8,128)(2,1)} %constant.15.clone.refs_7_) | copy-start | bytes 1572868
  0.0 14.2 %copy-start.4 = (bf16[1024,256]{1,0:T(8,128)(2,1)S(1)}, bf16[1024,256]{1,0:T(8,128)(2,1)}, u32[]{:S(2)}) copy-start(bf16[1024,256]{1,0:T(8,128)(2,1)} %constant.14.clone.refs_6_) | copy-start | bytes 1572868
  0.0 14.2 %copy-start.5 = (bf16[1024,256]{1,0:T(8,128)(2,1)S(1)}, bf16[1024,256]{1,0:T(8,128)(2,1)}, u32[]{:S(2)}) copy-start(bf16[1024,256]{1,0:T(8,128)(2,1)} %constant.13.clone.refs_5_) | copy-start | bytes 1572868
  0.0 14.2 %copy-start.6 = (bf16[48,144]{1,0:T(8,128)(2,1)S(1)}, bf16[48,144]{1,0:T(8,128)(2,1)}, u32[]{:S(2)}) copy-start(bf16[48,144]{1,0:T(8,128)(2,1)} %constant.12.clone.refs_4_) | copy-start | bytes 41476
  2.2 3.8 %collective-permute-start.2 = (f32[8,128]{1,0:T(8,128)S(1)}, f32[8,128]{1,0:T(8,128)S(1)}, u32[]{:S(2)}, u32[]{:S(2)}) collective-permute-start(f32[8,128]{1,0:T(8,128)S(1)} %get-tuple-element.13.refs_0_), channel_id=1, source_target_pairs={{0,3},{1,2},{2,1},{3,0},{4,7},{5,6},{6,5},{7,4},{8,11},{9,10},{10,... | collective-permute-start | bytes 12296 | tf_op jit(solution)/shard_map/ppermute | solution.py:493
  4.7 3.6 %collective-permute-start.1 = (f32[8,128]{1,0:T(8,128)S(1)}, f32[8,128]{1,0:T(8,128)S(1)}, u32[]{:S(2)}, u32[]{:S(2)}) collective-permute-start(f32[8,128]{1,0:T(8,128)S(1)} %get-tuple-element.13.refs_0_), channel_id=1, source_target_pairs={{0,2},{1,3},{2,0},{3,1},{4,6},{5,7},{6,4},{7,5},{8,10},{9,11},{10,... | collective-permute-start | bytes 12296 | tf_op jit(solution)/shard_map/ppermute | solution.py:493
  5.3 3.0 %collective-permute-start = (f32[8,128]{1,0:T(8,128)S(1)}, f32[8,128]{1,0:T(8,128)S(1)}, u32[]{:S(2)}, u32[]{:S(2)}) collective-permute-start(f32[8,128]{1,0:T(8,128)S(1)} %get-tuple-element.13.refs_0_), channel_id=1, source_target_pairs={{0,1},{1,0},{2,3},{3,2},{4,5},{5,4},{6,7},{7,6},{8,9},{9,8},{10,11... | collective-permute-start | bytes 12296 | tf_op jit(solution)/shard_map/ppermute | solution.py:493
  9.1 1.9 %collective-permute-start.3 = (bf16[216,128]{1,0:T(8,128)(2,1)S(1)}, bf16[216,128]{1,0:T(8,128)(2,1)S(1)}, u32[]{:S(2)}, u32[]{:S(2)}) collective-permute-start(bf16[216,128]{1,0:T(8,128)(2,1)S(1)} %get-tuple-element.16), channel_id=1, source_target_pairs={{0,1},{1,0},{2,3},{3,2},{4,5},{5,4},{6,7},{7,6},{8,9},{9,8},{10,11... | collective-permute-start | bytes 165896 | tf_op jit(solution)/shard_map/ppermute | solution.py:493
  9.1 4.7 %collective-permute-start.4 = (bf16[216,128]{1,0:T(8,128)(2,1)S(1)}, bf16[216,128]{1,0:T(8,128)(2,1)S(1)}, u32[]{:S(2)}, u32[]{:S(2)}) collective-permute-start(bf16[216,128]{1,0:T(8,128)(2,1)S(1)} %get-tuple-element.17), channel_id=1, source_target_pairs={{0,2},{1,3},{2,0},{3,1},{4,6},{5,7},{6,4},{7,5},{8,10},{9,11},{10,... | collective-permute-start | bytes 165896 | tf_op jit(solution)/shard_map/ppermute | solution.py:493
  9.8 4.3 %collective-permute-start.5 = (bf16[216,128]{1,0:T(8,128)(2,1)S(1)}, bf16[216,128]{1,0:T(8,128)(2,1)S(1)}, u32[]{:S(2)}, u32[]{:S(2)}) collective-permute-start(bf16[216,128]{1,0:T(8,128)(2,1)S(1)} %get-tuple-element.18), channel_id=1, source_target_pairs={{0,3},{1,2},{2,1},{3,0},{4,7},{5,6},{6,5},{7,4},{8,11},{9,10},{10,... | collective-permute-start | bytes 165896 | tf_op jit(solution)/shard_map/ppermute | solution.py:493

commit v6 on v5

--- a/solution.py
+++ b/solution.py
@@ -391,7 +391,7 @@
     )(notes, orbitals, *shares)
 
 
-def potentials(plan, pieces, at, parts):
+def potentials(plan, pieces, at, parts, place):
     grid_count, piece_rows = len(pieces), pieces[0].shape[0]
     part = piece_rows // parts
     sent = -(-(part + 1) // 8) * 8
@@ -410,7 +410,7 @@
         for g in range(grid_count):
             for q in range(parts):
                 first = g * piece_rows + q * part
-                out_ref[q * grid_count + g] = jnp.where(last, own, cube[first:first + sent, :]).astype(bf16)
+                out_ref[place[q * grid_count + g]] = jnp.where(last, own, cube[first:first + sent, :]).astype(bf16)
 
     return pl.pallas_call(
         kernel,
@@ -426,9 +426,10 @@
     )(at, *pieces, *tables)
 
 
-def apply_part(orbitals, notes, received, part, count, slab_count, halves):
+def apply_part(orbitals, notes, received, part, count, place, halves):
     occupied, shard_len = orbitals.shape
     points, pitch = received.shape[:2]
+    slab_count = len(place)
     keep = count // slab_count
     prefactor = -1.0 / math.sqrt(points * halves)
 
@@ -448,7 +449,7 @@
         for s in range(slab_count):
             for k in range(keep):
                 stage[s, k * part:(k + 1) * part, :] = mid[pl.ds(s * keep + k, part, stride=count), :]
-            out_ref[s] = stage[s].astype(bf16)
+            out_ref[place[s]] = stage[s].astype(bf16)
 
     return pl.pallas_call(
         kernel,
@@ -465,16 +466,14 @@
     )(notes, orbitals, received)
 
 
-def settle(kept, keep, halves):
-    parts, rows = kept.shape[0] // halves, kept.shape[1]
+def settle(kept, keep, halves, order):
+    slab_count, rows = kept.shape[:2]
+    parts = slab_count // halves
     part = rows // keep
 
     def kernel(kept_ref, out_ref, stage):
         for q in range(parts):
-            total = kept_ref[q].astype(f32)
-            for h in range(1, halves):
-                total = total + kept_ref[h * parts + q].astype(f32)
-            stage[q] = total
+            stage[q] = sum(kept_ref[j].astype(f32) for j in range(slab_count) if order[j] % parts == q)
             for k in range(keep):
                 out_ref[q * part:(q + 1) * part, k, :] = stage[q, k * part:(k + 1) * part, :]
 
@@ -487,6 +486,10 @@
         compiler_params=params(4),
         name="settle",
     )(kept)
+
+
+def places(order):
+    return [order.index(i) for i in range(len(order))]
 
 
 def exchange(value, grid_count, offset):
@@ -504,11 +507,13 @@
     shares = [share] + [exchange(share, grid_count, d) for d in range(1, grid_count)]
     *pieces, at = fit_pairs(orbitals, notes, shares)
     pieces = pieces[:1] + [exchange(pieces[d], grid_count, d) for d in range(1, grid_count)]
-    sent = potentials(plan, pieces, at, part_count)
-    received = lax.all_to_all(sent, ("part", "grid"), 0, 0)
-    blocks = apply_part(orbitals, notes, received, part, count, slab_count, halves)
-    kept = lax.all_to_all(blocks, ("half", "part"), 0, 0)
-    return jnp.transpose(settle(kept, keep, halves), (1, 0, 2)).reshape(keep, shard_len)
+    near = list(reversed(range(part_count * grid_count)))
+    far = [s ^ (slab_count // 2 + 1) for s in range(slab_count)]
+    sent = potentials(plan, pieces, at, part_count, places(near))
+    received = lax.all_to_all(sent, ("part", "grid"), 0, 0, axis_index_groups=[near])
+    blocks = apply_part(orbitals, notes, received, part, count, places(far), halves)
+    kept = lax.all_to_all(blocks, ("half", "part"), 0, 0, axis_index_groups=[far])
+    return jnp.transpose(settle(kept, keep, halves, far), (1, 0, 2)).reshape(keep, shard_len)
 
 
 def quick_fits(mesh, orbitals, targets, points, fit):

time: 41.2 us -> 38.8 us (0.942)
  blocking collectives: 23.7 us -> 21.4 us
    all_to_all x2, blocking collectives: 23.7 us -> 21.4 us  [the longest x1 12.1 us: quick_body(): lax.all_to_all(blocks, ('half', 'part'), 0, 0, axis_index_groups=[far])]
where the time goes in v6:
time: 38.8 us; the launch traced here: 38.6 us
  blocking collectives  21.4 us (55%)
  waiting for transfers between devices  6.09 us (16%)
  Pallas kernels  5.98 us (15%)
  starting transfers between devices  5.08 us (13%)
    all_to_all x1, blocking collectives, quick_body(): lax.all_to_all(blocks, ('half', 'part'), 0, 0, axis_index_groups=[far])  12.1 us
    all_to_all x1, blocking collectives, quick_body(): lax.all_to_all(sent, ('part', 'grid'), 0, 0, axis_index_groups=[near])  9.32 us
    ppermute x6, waiting for transfers between devices, exchange(): lax.ppermute(value, 'grid', [(i, i ^ offset) for i in range(grid_count)])  6.09 us
    ppermute x6, starting transfers between devices, exchange(): lax.ppermute(value, 'grid', [(i, i ^ offset) for i in range(grid_count)])  5.08 us
    pallas_call x1, Pallas kernels, read_points(): pl.pallas_call(kernel, out_shape=[pltpu.VMEM((8, lanes), f32), pltpu.VMEM...  2.17 us
    pallas_call x1, Pallas kernels, potentials(): pl.pallas_call(kernel, out_shape=jax.ShapeDtypeStruct((parts * grid_count...  1.68 us
    pallas_call x1, Pallas kernels, settle(): pl.pallas_call(kernel, out_shape=jax.ShapeDtypeStruct((parts * part, keep...  0.84 us
  transfers between devices with their start and end apart: 6, of which 4 were waited for; matrix products, arithmetic and copies ran while one was open for 0% of the time, Pallas kernels for 0%

profile of v6, /device:TPU:0, one launch (start us, length us, event | category | flops | bytes accessed | tf_op | source)
XLA Modules:
  0.0 38.6 jit_solution(9117642613544748975)
XLA Ops:
  0.0 0.0 copy-start
  0.0 0.0 copy-start.1
  0.0 0.0 copy-start.2
  0.0 0.0 copy-start.3
  0.0 0.0 copy-start.4
  0.0 0.0 copy-start.5
  0.0 0.0 copy-start.6
  0.0 2.2 %read_points.1 = (f32[8,128]{1,0:T(8,128)S(1)}, f32[56,128]{1,0:T(8,128)S(1)}) custom-call(s32[4]{0:T(128)} %points_hbm.1, s32[16]{0:T(128)} %targets_hbm.1, f32[4,4]{1,0:T(4,128)} %fit_hbm.1, bf16[64,27648]{1,0:T(8,128)(2,1)} %orbitals_ref.5), custom_call_target="tpu_custom_call" | custom-call | tf_op jit(solution)/shard_map/read_points/pallas_call | solution.py:331
  2.2 2.5 %collective-permute-start.2 = (f32[8,128]{1,0:T(8,128)S(1)}, f32[8,128]{1,0:T(8,128)S(1)}, u32[]{:S(2)}, u32[]{:S(2)}) collective-permute-start(f32[8,128]{1,0:T(8,128)S(1)} %get-tuple-element.13.refs_0_), channel_id=1, source_target_pairs={{0,3},{1,2},{2,1},{3,0},{4,7},{5,6},{6,5},{7,4},{8,11},{9,10},{10,... | collective-permute-start | bytes 12296 | tf_op jit(solution)/shard_map/ppermute | solution.py:496
  4.7 0.6 %collective-permute-start.1 = (f32[8,128]{1,0:T(8,128)S(1)}, f32[8,128]{1,0:T(8,128)S(1)}, u32[]{:S(2)}, u32[]{:S(2)}) collective-permute-start(f32[8,128]{1,0:T(8,128)S(1)} %get-tuple-element.13.refs_0_), channel_id=1, source_target_pairs={{0,2},{1,3},{2,0},{3,1},{4,6},{5,7},{6,4},{7,5},{8,10},{9,11},{10,... | collective-permute-start | bytes 12296 | tf_op jit(solution)/shard_map/ppermute | solution.py:496
  5.3 0.0 collective-permute-start
  5.4 0.6 %collective-permute-done.2.refs_3_ = f32[8,128]{1,0:T(8,128)S(1)} collective-permute-done((f32[8,128]{1,0:T(8,128)S(1)}, f32[8,128]{1,0:T(8,128)S(1)}, u32[]{:S(2)}, u32[]{:S(2)}) %collective-permute-start.2) | collective-permute-done | bytes 4128 | tf_op jit(solution)/shard_map/ppermute | solution.py:496
  6.0 2.3 %collective-permute-done.1.refs_2_ = f32[8,128]{1,0:T(8,128)S(1)} collective-permute-done((f32[8,128]{1,0:T(8,128)S(1)}, f32[8,128]{1,0:T(8,128)S(1)}, u32[]{:S(2)}, u32[]{:S(2)}) %collective-permute-start.1) | collective-permute-done | bytes 4128 | tf_op jit(solution)/shard_map/ppermute | solution.py:496
  8.3 0.0 collective-permute-done.refs_1_
  8.3 0.0 copy-done
  8.3 0.7 %fit_pairs.1 = (bf16[216,128]{1,0:T(8,128)(2,1)S(1)}, bf16[216,128]{1,0:T(8,128)(2,1)S(1)}, bf16[216,128]{1,0:T(8,128)(2,1)S(1)}, bf16[216,128]{1,0:T(8,128)(2,1)S(1)}, f32[8,128]{1,0:T(8,128)S(1)}) custom-call(f32[56,128]{1,0:T(8,128)S(1)} %get-tuple-element.12.notes_ref, bf16[64,27648]{1,0:T(8,128)(2,1)S(1)} %copy-done, ...), custom_call_target="tpu_custom_call" | custom-call | tf_op jit(solution)/shard_map/fit_pairs/pallas_call | solution.py:383
  9.1 0.1 collective-permute-start.3
  9.1 0.7 %collective-permute-start.4 = (bf16[216,128]{1,0:T(8,128)(2,1)S(1)}, bf16[216,128]{1,0:T(8,128)(2,1)S(1)}, u32[]{:S(2)}, u32[]{:S(2)}) collective-permute-start(bf16[216,128]{1,0:T(8,128)(2,1)S(1)} %get-tuple-element.17), channel_id=1, source_target_pairs={{0,2},{1,3},{2,0},{3,1},{4,6},{5,7},{6,4},{7,5},{8,10},{9,11},{10,... | collective-permute-start | bytes 165896 | tf_op jit(solution)/shard_map/ppermute | solution.py:496
  9.8 1.2 %collective-permute-start.5 = (bf16[216,128]{1,0:T(8,128)(2,1)S(1)}, bf16[216,128]{1,0:T(8,128)(2,1)S(1)}, u32[]{:S(2)}, u32[]{:S(2)}) collective-permute-start(bf16[216,128]{1,0:T(8,128)(2,1)S(1)} %get-tuple-element.18), channel_id=1, source_target_pairs={{0,3},{1,2},{2,1},{3,0},{4,7},{5,6},{6,5},{7,4},{8,11},{9,10},{10,... | collective-permute-start | bytes 165896 | tf_op jit(solution)/shard_map/ppermute | solution.py:496
  11.0 0.0 collective-permute-done.3.refs_1_
  11.0 2.9 %collective-permute-done.4.refs_2_ = bf16[216,128]{1,0:T(8,128)(2,1)S(1)} collective-permute-done((bf16[216,128]{1,0:T(8,128)(2,1)S(1)}, bf16[216,128]{1,0:T(8,128)(2,1)S(1)}, u32[]{:S(2)}, u32[]{:S(2)}) %collective-permute-start.4) | collective-permute-done | bytes 55328 | tf_op jit(solution)/shard_map/ppermute | solution.py:496
  13.9 0.3 collective-permute-done.5.refs_3_
  14.2 0.0 copy-done.1
  14.2 0.0 copy-done.2
  14.2 0.0 copy-done.3
  14.2 0.0 copy-done.4
  14.2 0.0 copy-done.5
  14.2 0.0 copy-done.6
  14.2 1.7 %potentials.1 = bf16[16,56,128]{2,1,0:T(8,128)(2,1)S(1)} custom-call(f32[8,128]{1,0:T(8,128)S(1)} %get-tuple-element.14.at_ref, bf16[216,128]{1,0:T(8,128)(2,1)S(1)} %get-tuple-element.15.refs_0_, bf16[216,128]{1,0:T(8,128)(2,1)S(1)} %collective-permute-done.3.refs_1_, bf16[216,128]{1,0:T(8,128)(2,1)S(1)} %collective-permute-done.4.refs_2_, ...), custom_call_target="tpu_custom_call" | custom-call | tf_op jit(solution)/shard_map/potentials/pallas_call | solution.py:415
  15.9 9.3 %all_to_all.10.received_ref = bf16[16,56,128]{2,1,0:T(8,128)(2,1)S(1)} all-to-all(bf16[16,56,128]{2,1,0:T(8,128)(2,1)S(1)} %potentials.1), channel_id=1, replica_groups={{15,14,13,12,11,10,9,8,7,6,5,4,3,2,1,0},{31,30,29,28,27,26,25,24,23,22,..., dimensions={0} | all-to-all | bytes 458752 | tf_op jit(solution)/shard_map/all_to_all | solution.py:513
  25.2 0.6 %apply_part.1 = bf16[8,108,128]{2,1,0:T(8,128)(2,1)S(1)} custom-call(f32[56,128]{1,0:T(8,128)S(1)} %get-tuple-element.12.notes_ref, bf16[64,27648]{1,0:T(8,128)(2,1)S(1)} %copy-done, bf16[16,56,128]{2,1,0:T(8,128)(2,1)S(1)} %all_to_all.10.received_ref), custom_call_target="tpu_custom_call" | custom-call | tf_op jit(solution)/shard_map/apply_part/pallas_call | solution.py:454
  25.8 12.1 %all_to_all.11.kept_ref = bf16[8,108,128]{2,1,0:T(8,128)(2,1)S(1)} all-to-all(bf16[8,108,128]{2,1,0:T(8,128)(2,1)S(1)} %apply_part.1), channel_id=1, replica_groups={{20,16,28,24,4,0,12,8},{21,17,29,25,5,1,13,9},{22,18,30,26,6,2,14,10},{..., dimensions={0} | all-to-all | bytes 442368 | tf_op jit(solution)/shard_map/all_to_all | solution.py:515
  37.8 0.8 %settle.1 = f32[216,2,128]{2,1,0:T(2,128)} custom-call(bf16[8,108,128]{2,1,0:T(8,128)(2,1)S(1)} %all_to_all.11.kept_ref), custom_call_target="tpu_custom_call" | custom-call | tf_op jit(solution)/shard_map/settle/pallas_call | solution.py:480
Async XLA Ops:
  0.0 8.3 %copy-start = (bf16[64,27648]{1,0:T(8,128)(2,1)S(1)}, bf16[64,27648]{1,0:T(8,128)(2,1)}, u32[]{:S(2)}) copy-start(bf16[64,27648]{1,0:T(8,128)(2,1)} %orbitals_ref.5) | copy-start | bytes 10616836
  0.0 14.2 %copy-start.1 = (f32[24,48,128]{2,1,0:T(8,128)S(1)}, f32[24,48,128]{2,1,0:T(8,128)}, u32[]{:S(2)}) copy-start(f32[24,48,128]{2,1,0:T(8,128)} %constant.17.clone.refs_9_) | copy-start | bytes 1769476
  0.0 14.2 %copy-start.2 = (bf16[1024,256]{1,0:T(8,128)(2,1)S(1)}, bf16[1024,256]{1,0:T(8,128)(2,1)}, u32[]{:S(2)}) copy-start(bf16[1024,256]{1,0:T(8,128)(2,1)} %constant.16.clone.refs_8_) | copy-start | bytes 1572868
  0.0 14.2 %copy-start.3 = (bf16[1024,256]{1,0:T(8,128)(2,1)S(1)}, bf16[1024,256]{1,0:T(8,128)(2,1)}, u32[]{:S(2)}) copy-start(bf16[1024,256]{1,0:T(8,128)(2,1)} %constant.15.clone.refs_7_) | copy-start | bytes 1572868
  0.0 14.2 %copy-start.4 = (bf16[1024,256]{1,0:T(8,128)(2,1)S(1)}, bf16[1024,256]{1,0:T(8,128)(2,1)}, u32[]{:S(2)}) copy-start(bf16[1024,256]{1,0:T(8,128)(2,1)} %constant.14.clone.refs_6_) | copy-start | bytes 1572868
  0.0 14.2 %copy-start.5 = (bf16[1024,256]{1,0:T(8,128)(2,1)S(1)}, bf16[1024,256]{1,0:T(8,128)(2,1)}, u32[]{:S(2)}) copy-start(bf16[1024,256]{1,0:T(8,128)(2,1)} %constant.13.clone.refs_5_) | copy-start | bytes 1572868
  0.0 14.2 %copy-start.6 = (bf16[48,144]{1,0:T(8,128)(2,1)S(1)}, bf16[48,144]{1,0:T(8,128)(2,1)}, u32[]{:S(2)}) copy-start(bf16[48,144]{1,0:T(8,128)(2,1)} %constant.12.clone.refs_4_) | copy-start | bytes 41476
  2.2 3.8 %collective-permute-start.2 = (f32[8,128]{1,0:T(8,128)S(1)}, f32[8,128]{1,0:T(8,128)S(1)}, u32[]{:S(2)}, u32[]{:S(2)}) collective-permute-start(f32[8,128]{1,0:T(8,128)S(1)} %get-tuple-element.13.refs_0_), channel_id=1, source_target_pairs={{0,3},{1,2},{2,1},{3,0},{4,7},{5,6},{6,5},{7,4},{8,11},{9,10},{10,... | collective-permute-start | bytes 12296 | tf_op jit(solution)/shard_map/ppermute | solution.py:496
  4.7 3.6 %collective-permute-start.1 = (f32[8,128]{1,0:T(8,128)S(1)}, f32[8,128]{1,0:T(8,128)S(1)}, u32[]{:S(2)}, u32[]{:S(2)}) collective-permute-start(f32[8,128]{1,0:T(8,128)S(1)} %get-tuple-element.13.refs_0_), channel_id=1, source_target_pairs={{0,2},{1,3},{2,0},{3,1},{4,6},{5,7},{6,4},{7,5},{8,10},{9,11},{10,... | collective-permute-start | bytes 12296 | tf_op jit(solution)/shard_map/ppermute | solution.py:496
  5.3 3.0 %collective-permute-start = (f32[8,128]{1,0:T(8,128)S(1)}, f32[8,128]{1,0:T(8,128)S(1)}, u32[]{:S(2)}, u32[]{:S(2)}) collective-permute-start(f32[8,128]{1,0:T(8,128)S(1)} %get-tuple-element.13.refs_0_), channel_id=1, source_target_pairs={{0,1},{1,0},{2,3},{3,2},{4,5},{5,4},{6,7},{7,6},{8,9},{9,8},{10,11... | collective-permute-start | bytes 12296 | tf_op jit(solution)/shard_map/ppermute | solution.py:496
  9.1 1.9 %collective-permute-start.3 = (bf16[216,128]{1,0:T(8,128)(2,1)S(1)}, bf16[216,128]{1,0:T(8,128)(2,1)S(1)}, u32[]{:S(2)}, u32[]{:S(2)}) collective-permute-start(bf16[216,128]{1,0:T(8,128)(2,1)S(1)} %get-tuple-element.16), channel_id=1, source_target_pairs={{0,1},{1,0},{2,3},{3,2},{4,5},{5,4},{6,7},{7,6},{8,9},{9,8},{10,11... | collective-permute-start | bytes 165896 | tf_op jit(solution)/shard_map/ppermute | solution.py:496
  9.1 4.7 %collective-permute-start.4 = (bf16[216,128]{1,0:T(8,128)(2,1)S(1)}, bf16[216,128]{1,0:T(8,128)(2,1)S(1)}, u32[]{:S(2)}, u32[]{:S(2)}) collective-permute-start(bf16[216,128]{1,0:T(8,128)(2,1)S(1)} %get-tuple-element.17), channel_id=1, source_target_pairs={{0,2},{1,3},{2,0},{3,1},{4,6},{5,7},{6,4},{7,5},{8,10},{9,11},{10,... | collective-permute-start | bytes 165896 | tf_op jit(solution)/shard_map/ppermute | solution.py:496
  9.8 4.3 %collective-permute-start.5 = (bf16[216,128]{1,0:T(8,128)(2,1)S(1)}, bf16[216,128]{1,0:T(8,128)(2,1)S(1)}, u32[]{:S(2)}, u32[]{:S(2)}) collective-permute-start(bf16[216,128]{1,0:T(8,128)(2,1)S(1)} %get-tuple-element.18), channel_id=1, source_target_pairs={{0,3},{1,2},{2,1},{3,0},{4,7},{5,6},{6,5},{7,4},{8,11},{9,10},{10,... | collective-permute-start | bytes 165896 | tf_op jit(solution)/shard_map/ppermute | solution.py:496

commit v7 on v6

--- a/solution.py
+++ b/solution.py
@@ -391,7 +391,7 @@
     )(notes, orbitals, *shares)
 
 
-def potentials(plan, pieces, at, parts, place):
+def potentials(plan, pieces, offsets, at, parts, place):
     grid_count, piece_rows = len(pieces), pieces[0].shape[0]
     part = piece_rows // parts
     sent = -(-(part + 1) // 8) * 8
@@ -401,7 +401,7 @@
         piece_refs, refs = refs[:grid_count], refs[grid_count:]
         table_refs, (out_ref, cube, mid) = refs[:len(tables)], refs[len(tables):]
         me = lax.axis_index("grid")
-        for d, ref in enumerate(piece_refs):
+        for d, ref in zip(offsets, piece_refs):
             start = pl.multiple_of(jnp.bitwise_xor(me, d) * piece_rows, 8)
             cube[pl.ds(start, piece_rows), :] = ref[...].astype(f32)
         solve(plan, cube, *table_refs, mid)
@@ -506,10 +506,11 @@
     share, notes = read_points(orbitals, targets, points, fit)
     shares = [share] + [exchange(share, grid_count, d) for d in range(1, grid_count)]
     *pieces, at = fit_pairs(orbitals, notes, shares)
-    pieces = pieces[:1] + [exchange(pieces[d], grid_count, d) for d in range(1, grid_count)]
+    offsets = [0] + list(reversed(range(1, grid_count)))
+    pieces = [exchange(pieces[d], grid_count, d) if d else pieces[d] for d in offsets]
     near = list(reversed(range(part_count * grid_count)))
-    far = [s ^ (slab_count // 2 + 1) for s in range(slab_count)]
-    sent = potentials(plan, pieces, at, part_count, places(near))
+    far = [s ^ (s >> 1) for s in reversed(range(slab_count))]
+    sent = potentials(plan, pieces, offsets, at, part_count, places(near))
     received = lax.all_to_all(sent, ("part", "grid"), 0, 0, axis_index_groups=[near])
     blocks = apply_part(orbitals, notes, received, part, count, places(far), halves)
     kept = lax.all_to_all(blocks, ("half", "part"), 0, 0, axis_index_groups=[far])

time: 38.8 us -> 38.5 us (level)
  no operation moved by 1% of the time
where the time goes in v7:
time: 38.5 us; the launch traced here: 38.3 us
  blocking collectives  21.3 us (55%)
  Pallas kernels  5.98 us (16%)
  waiting for transfers between devices  5.84 us (15%)
  starting transfers between devices  5.07 us (13%)
    all_to_all x1, blocking collectives, quick_body(): lax.all_to_all(blocks, ('half', 'part'), 0, 0, axis_index_groups=[far])  11.8 us
    all_to_all x1, blocking collectives, quick_body(): lax.all_to_all(sent, ('part', 'grid'), 0, 0, axis_index_groups=[near])  9.5 us
    ppermute x6, waiting for transfers between devices, exchange(): lax.ppermute(value, 'grid', [(i, i ^ offset) for i in range(grid_count)])  5.84 us
    ppermute x6, starting transfers between devices, exchange(): lax.ppermute(value, 'grid', [(i, i ^ offset) for i in range(grid_count)])  5.07 us
    pallas_call x1, Pallas kernels, read_points(): pl.pallas_call(kernel, out_shape=[pltpu.VMEM((8, lanes), f32), pltpu.VMEM...  2.17 us
    pallas_call x1, Pallas kernels, potentials(): pl.pallas_call(kernel, out_shape=jax.ShapeDtypeStruct((parts * grid_count...  1.68 us
    pallas_call x1, Pallas kernels, settle(): pl.pallas_call(kernel, out_shape=jax.ShapeDtypeStruct((parts * part, keep...  0.83 us
  transfers between devices with their start and end apart: 6, of which 4 were waited for; matrix products, arithmetic and copies ran while one was open for 0% of the time, Pallas kernels for 0%

profile of v7, /device:TPU:0, one launch (start us, length us, event | category | flops | bytes accessed | tf_op | source)
XLA Modules:
  0.0 38.3 jit_solution(7317586173053014538)
XLA Ops:
  0.0 0.0 copy-start
  0.0 0.0 copy-start.1
  0.0 0.0 copy-start.2
  0.0 0.0 copy-start.3
  0.0 0.0 copy-start.4
  0.0 0.0 copy-start.5
  0.0 0.0 copy-start.6
  0.0 2.2 %read_points.1 = (f32[8,128]{1,0:T(8,128)S(1)}, f32[56,128]{1,0:T(8,128)S(1)}) custom-call(s32[4]{0:T(128)} %points_hbm.1, s32[16]{0:T(128)} %targets_hbm.1, f32[4,4]{1,0:T(4,128)} %fit_hbm.1, bf16[64,27648]{1,0:T(8,128)(2,1)} %orbitals_ref.5), custom_call_target="tpu_custom_call" | custom-call | tf_op jit(solution)/shard_map/read_points/pallas_call | solution.py:331
  2.2 2.5 %collective-permute-start.2 = (f32[8,128]{1,0:T(8,128)S(1)}, f32[8,128]{1,0:T(8,128)S(1)}, u32[]{:S(2)}, u32[]{:S(2)}) collective-permute-start(f32[8,128]{1,0:T(8,128)S(1)} %get-tuple-element.13.refs_0_), channel_id=1, source_target_pairs={{0,3},{1,2},{2,1},{3,0},{4,7},{5,6},{6,5},{7,4},{8,11},{9,10},{10,... | collective-permute-start | bytes 12296 | tf_op jit(solution)/shard_map/ppermute | solution.py:496
  4.7 0.6 %collective-permute-start.1 = (f32[8,128]{1,0:T(8,128)S(1)}, f32[8,128]{1,0:T(8,128)S(1)}, u32[]{:S(2)}, u32[]{:S(2)}) collective-permute-start(f32[8,128]{1,0:T(8,128)S(1)} %get-tuple-element.13.refs_0_), channel_id=1, source_target_pairs={{0,2},{1,3},{2,0},{3,1},{4,6},{5,7},{6,4},{7,5},{8,10},{9,11},{10,... | collective-permute-start | bytes 12296 | tf_op jit(solution)/shard_map/ppermute | solution.py:496
  5.3 0.0 collective-permute-start
  5.4 0.6 %collective-permute-done.2.refs_3_ = f32[8,128]{1,0:T(8,128)S(1)} collective-permute-done((f32[8,128]{1,0:T(8,128)S(1)}, f32[8,128]{1,0:T(8,128)S(1)}, u32[]{:S(2)}, u32[]{:S(2)}) %collective-permute-start.2) | collective-permute-done | bytes 4128 | tf_op jit(solution)/shard_map/ppermute | solution.py:496
  6.0 2.3 %collective-permute-done.1.refs_2_ = f32[8,128]{1,0:T(8,128)S(1)} collective-permute-done((f32[8,128]{1,0:T(8,128)S(1)}, f32[8,128]{1,0:T(8,128)S(1)}, u32[]{:S(2)}, u32[]{:S(2)}) %collective-permute-start.1) | collective-permute-done | bytes 4128 | tf_op jit(solution)/shard_map/ppermute | solution.py:496
  8.3 0.0 collective-permute-done.refs_1_
  8.3 0.0 copy-done
  8.3 0.7 %fit_pairs.1 = (bf16[216,128]{1,0:T(8,128)(2,1)S(1)}, bf16[216,128]{1,0:T(8,128)(2,1)S(1)}, bf16[216,128]{1,0:T(8,128)(2,1)S(1)}, bf16[216,128]{1,0:T(8,128)(2,1)S(1)}, f32[8,128]{1,0:T(8,128)S(1)}) custom-call(f32[56,128]{1,0:T(8,128)S(1)} %get-tuple-element.12.notes_ref, bf16[64,27648]{1,0:T(8,128)(2,1)S(1)} %copy-done, ...), custom_call_target="tpu_custom_call" | custom-call | tf_op jit(solution)/shard_map/fit_pairs/pallas_call | solution.py:383
  9.1 0.1 collective-permute-start.3
  9.1 1.1 %collective-permute-start.4 = (bf16[216,128]{1,0:T(8,128)(2,1)S(1)}, bf16[216,128]{1,0:T(8,128)(2,1)S(1)}, u32[]{:S(2)}, u32[]{:S(2)}) collective-permute-start(bf16[216,128]{1,0:T(8,128)(2,1)S(1)} %get-tuple-element.17), channel_id=1, source_target_pairs={{0,2},{1,3},{2,0},{3,1},{4,6},{5,7},{6,4},{7,5},{8,10},{9,11},{10,... | collective-permute-start | bytes 165896 | tf_op jit(solution)/shard_map/ppermute | solution.py:496
  10.3 0.7 %collective-permute-start.5 = (bf16[216,128]{1,0:T(8,128)(2,1)S(1)}, bf16[216,128]{1,0:T(8,128)(2,1)S(1)}, u32[]{:S(2)}, u32[]{:S(2)}) collective-permute-start(bf16[216,128]{1,0:T(8,128)(2,1)S(1)} %get-tuple-element.18), channel_id=1, source_target_pairs={{0,1},{1,0},{2,3},{3,2},{4,5},{5,4},{6,7},{7,6},{8,9},{9,8},{10,11... | collective-permute-start | bytes 165896 | tf_op jit(solution)/shard_map/ppermute | solution.py:496
  11.0 2.3 %collective-permute-done.3.refs_1_ = bf16[216,128]{1,0:T(8,128)(2,1)S(1)} collective-permute-done((bf16[216,128]{1,0:T(8,128)(2,1)S(1)}, bf16[216,128]{1,0:T(8,128)(2,1)S(1)}, u32[]{:S(2)}, u32[]{:S(2)}) %collective-permute-start.3) | collective-permute-done | bytes 55328 | tf_op jit(solution)/shard_map/ppermute | solution.py:496
  13.3 0.6 %collective-permute-done.4.refs_2_ = bf16[216,128]{1,0:T(8,128)(2,1)S(1)} collective-permute-done((bf16[216,128]{1,0:T(8,128)(2,1)S(1)}, bf16[216,128]{1,0:T(8,128)(2,1)S(1)}, u32[]{:S(2)}, u32[]{:S(2)}) %collective-permute-start.4) | collective-permute-done | bytes 55328 | tf_op jit(solution)/shard_map/ppermute | solution.py:496
  13.9 0.0 collective-permute-done.5.refs_3_
  13.9 0.0 copy-done.1
  13.9 0.0 copy-done.2
  13.9 0.0 copy-done.3
  13.9 0.0 copy-done.4
  13.9 0.0 copy-done.5
  13.9 0.0 copy-done.6
  13.9 1.7 %potentials.1 = bf16[16,56,128]{2,1,0:T(8,128)(2,1)S(1)} custom-call(f32[8,128]{1,0:T(8,128)S(1)} %get-tuple-element.14.at_ref, bf16[216,128]{1,0:T(8,128)(2,1)S(1)} %get-tuple-element.15.refs_0_, bf16[216,128]{1,0:T(8,128)(2,1)S(1)} %collective-permute-done.3.refs_1_, bf16[216,128]{1,0:T(8,128)(2,1)S(1)} %collective-permute-done.4.refs_2_, ...), custom_call_target="tpu_custom_call" | custom-call | tf_op jit(solution)/shard_map/potentials/pallas_call | solution.py:415
  15.6 9.5 %all_to_all.10.received_ref = bf16[16,56,128]{2,1,0:T(8,128)(2,1)S(1)} all-to-all(bf16[16,56,128]{2,1,0:T(8,128)(2,1)S(1)} %potentials.1), channel_id=1, replica_groups={{15,14,13,12,11,10,9,8,7,6,5,4,3,2,1,0},{31,30,29,28,27,26,25,24,23,22,..., dimensions={0} | all-to-all | bytes 458752 | tf_op jit(solution)/shard_map/all_to_all | solution.py:514
  25.1 0.6 %apply_part.1 = bf16[8,108,128]{2,1,0:T(8,128)(2,1)S(1)} custom-call(f32[56,128]{1,0:T(8,128)S(1)} %get-tuple-element.12.notes_ref, bf16[64,27648]{1,0:T(8,128)(2,1)S(1)} %copy-done, bf16[16,56,128]{2,1,0:T(8,128)(2,1)S(1)} %all_to_all.10.received_ref), custom_call_target="tpu_custom_call" | custom-call | tf_op jit(solution)/shard_map/apply_part/pallas_call | solution.py:454
  25.7 11.8 %all_to_all.11.kept_ref = bf16[8,108,128]{2,1,0:T(8,128)(2,1)S(1)} all-to-all(bf16[8,108,128]{2,1,0:T(8,128)(2,1)S(1)} %apply_part.1), channel_id=1, replica_groups={{16,20,28,24,8,12,4,0},{17,21,29,25,9,13,5,1},{18,22,30,26,10,14,6,2},{..., dimensions={0} | all-to-all | bytes 442368 | tf_op jit(solution)/shard_map/all_to_all | solution.py:516
  37.5 0.8 %settle.1 = f32[216,2,128]{2,1,0:T(2,128)} custom-call(bf16[8,108,128]{2,1,0:T(8,128)(2,1)S(1)} %all_to_all.11.kept_ref), custom_call_target="tpu_custom_call" | custom-call | tf_op jit(solution)/shard_map/settle/pallas_call | solution.py:480
Async XLA Ops:
  0.0 8.3 %copy-start = (bf16[64,27648]{1,0:T(8,128)(2,1)S(1)}, bf16[64,27648]{1,0:T(8,128)(2,1)}, u32[]{:S(2)}) copy-start(bf16[64,27648]{1,0:T(8,128)(2,1)} %orbitals_ref.5) | copy-start | bytes 10616836
  0.0 13.9 %copy-start.1 = (f32[24,48,128]{2,1,0:T(8,128)S(1)}, f32[24,48,128]{2,1,0:T(8,128)}, u32[]{:S(2)}) copy-start(f32[24,48,128]{2,1,0:T(8,128)} %constant.17.clone.refs_9_) | copy-start | bytes 1769476
  0.0 13.9 %copy-start.2 = (bf16[1024,256]{1,0:T(8,128)(2,1)S(1)}, bf16[1024,256]{1,0:T(8,128)(2,1)}, u32[]{:S(2)}) copy-start(bf16[1024,256]{1,0:T(8,128)(2,1)} %constant.16.clone.refs_8_) | copy-start | bytes 1572868
  0.0 13.9 %copy-start.3 = (bf16[1024,256]{1,0:T(8,128)(2,1)S(1)}, bf16[1024,256]{1,0:T(8,128)(2,1)}, u32[]{:S(2)}) copy-start(bf16[1024,256]{1,0:T(8,128)(2,1)} %constant.15.clone.refs_7_) | copy-start | bytes 1572868
  0.0 13.9 %copy-start.4 = (bf16[1024,256]{1,0:T(8,128)(2,1)S(1)}, bf16[1024,256]{1,0:T(8,128)(2,1)}, u32[]{:S(2)}) copy-start(bf16[1024,256]{1,0:T(8,128)(2,1)} %constant.14.clone.refs_6_) | copy-start | bytes 1572868
  0.0 13.9 %copy-start.5 = (bf16[1024,256]{1,0:T(8,128)(2,1)S(1)}, bf16[1024,256]{1,0:T(8,128)(2,1)}, u32[]{:S(2)}) copy-start(bf16[1024,256]{1,0:T(8,128)(2,1)} %constant.13.clone.refs_5_) | copy-start | bytes 1572868
  0.0 13.9 %copy-start.6 = (bf16[48,144]{1,0:T(8,128)(2,1)S(1)}, bf16[48,144]{1,0:T(8,128)(2,1)}, u32[]{:S(2)}) copy-start(bf16[48,144]{1,0:T(8,128)(2,1)} %constant.12.clone.refs_4_) | copy-start | bytes 41476
  2.2 3.8 %collective-permute-start.2 = (f32[8,128]{1,0:T(8,128)S(1)}, f32[8,128]{1,0:T(8,128)S(1)}, u32[]{:S(2)}, u32[]{:S(2)}) collective-permute-start(f32[8,128]{1,0:T(8,128)S(1)} %get-tuple-element.13.refs_0_), channel_id=1, source_target_pairs={{0,3},{1,2},{2,1},{3,0},{4,7},{5,6},{6,5},{7,4},{8,11},{9,10},{10,... | collective-permute-start | bytes 12296 | tf_op jit(solution)/shard_map/ppermute | solution.py:496
  4.7 3.6 %collective-permute-start.1 = (f32[8,128]{1,0:T(8,128)S(1)}, f32[8,128]{1,0:T(8,128)S(1)}, u32[]{:S(2)}, u32[]{:S(2)}) collective-permute-start(f32[8,128]{1,0:T(8,128)S(1)} %get-tuple-element.13.refs_0_), channel_id=1, source_target_pairs={{0,2},{1,3},{2,0},{3,1},{4,6},{5,7},{6,4},{7,5},{8,10},{9,11},{10,... | collective-permute-start | bytes 12296 | tf_op jit(solution)/shard_map/ppermute | solution.py:496
  5.3 3.0 %collective-permute-start = (f32[8,128]{1,0:T(8,128)S(1)}, f32[8,128]{1,0:T(8,128)S(1)}, u32[]{:S(2)}, u32[]{:S(2)}) collective-permute-start(f32[8,128]{1,0:T(8,128)S(1)} %get-tuple-element.13.refs_0_), channel_id=1, source_target_pairs={{0,1},{1,0},{2,3},{3,2},{4,5},{5,4},{6,7},{7,6},{8,9},{9,8},{10,11... | collective-permute-start | bytes 12296 | tf_op jit(solution)/shard_map/ppermute | solution.py:496
  9.1 4.2 %collective-permute-start.3 = (bf16[216,128]{1,0:T(8,128)(2,1)S(1)}, bf16[216,128]{1,0:T(8,128)(2,1)S(1)}, u32[]{:S(2)}, u32[]{:S(2)}) collective-permute-start(bf16[216,128]{1,0:T(8,128)(2,1)S(1)} %get-tuple-element.16), channel_id=1, source_target_pairs={{0,3},{1,2},{2,1},{3,0},{4,7},{5,6},{6,5},{7,4},{8,11},{9,10},{10,... | collective-permute-start | bytes 165896 | tf_op jit(solution)/shard_map/ppermute | solution.py:496
  9.1 4.8 %collective-permute-start.4 = (bf16[216,128]{1,0:T(8,128)(2,1)S(1)}, bf16[216,128]{1,0:T(8,128)(2,1)S(1)}, u32[]{:S(2)}, u32[]{:S(2)}) collective-permute-start(bf16[216,128]{1,0:T(8,128)(2,1)S(1)} %get-tuple-element.17), channel_id=1, source_target_pairs={{0,2},{1,3},{2,0},{3,1},{4,6},{5,7},{6,4},{7,5},{8,10},{9,11},{10,... | collective-permute-start | bytes 165896 | tf_op jit(solution)/shard_map/ppermute | solution.py:496
  10.3 3.6 %collective-permute-start.5 = (bf16[216,128]{1,0:T(8,128)(2,1)S(1)}, bf16[216,128]{1,0:T(8,128)(2,1)S(1)}, u32[]{:S(2)}, u32[]{:S(2)}) collective-permute-start(bf16[216,128]{1,0:T(8,128)(2,1)S(1)} %get-tuple-element.18), channel_id=1, source_target_pairs={{0,1},{1,0},{2,3},{3,2},{4,5},{5,4},{6,7},{7,6},{8,9},{9,8},{10,11... | collective-permute-start | bytes 165896 | tf_op jit(solution)/shard_map/ppermute | solution.py:496

commit v8 on v7

--- a/solution.py
+++ b/solution.py
@@ -129,15 +129,14 @@
 
 
 def hartley(length):
-    product = np.outer(np.arange(length), np.arange(length)) % length
-    angles = product * (2.0 * math.pi / length)
-    return (np.cos(angles) + np.sin(angles)) / math.sqrt(length)
-
-
-def split_table(table):
-    upper = table.astype(ml_dtypes.bfloat16)
-    lower = (table - upper.astype(np.float64)).astype(ml_dtypes.bfloat16)
-    return upper, lower
+    angles = np.outer(np.arange(length), np.arange(length)) % length * (2.0 * math.pi / length)
+    matrix = np.cos(angles) + np.sin(angles)
+    values = np.unique(np.round(np.abs(matrix), 12))
+    scales = 2.0 ** (np.arange(1 << 14) / (1 << 14))
+    exact = scales[:, None] * values
+    errors = ((exact.astype(ml_dtypes.bfloat16).astype(np.float64) - exact) / scales[:, None]) ** 2
+    scale = scales[np.argmin(errors.sum(axis=1))]
+    return (matrix * scale).astype(ml_dtypes.bfloat16), scale
 
 
 def split_value(value):
@@ -156,14 +155,14 @@
         self.block_rows = self.block // lanes
         self.plane_rows = edge * edge // lanes
         self.rows = edge * self.plane_rows
-        matrix = hartley(edge)
+        matrix, scale = hartley(edge)
         self.windows = []
         tables = []
         for j in range(self.inner // 2):
             low, high = 2 * j * edge, (2 * j + 2) * edge
             base = low // lanes * lanes
             self.windows.append((low, high, base))
-            table = np.zeros((2 * lanes, 2, 2, self.slot))
+            table = np.zeros((2 * lanes, 2, 2, self.slot), ml_dtypes.bfloat16)
             for h in range(2):
                 for y in range(2):
                     for z in range(edge):
@@ -178,37 +177,33 @@
         weights = weights.reshape(2, self.half, edge, edge)
         table = np.zeros((self.half, edge, 2, self.slot))
         table[..., :edge] = np.transpose(weights, (1, 2, 0, 3))
-        self.weights = table.reshape(self.half, edge, lanes).astype(np.float32)
-        self.left = np.concatenate([*split_table(matrix), split_table(matrix)[0]], axis=1)
+        self.weights = (table.reshape(self.half, edge, lanes) / (edge * scale ** 2) ** 3).astype(np.float32)
+        self.left = np.concatenate([matrix, matrix], axis=1)
 
     def tables(self):
-        fh, fl = split_table(self.forward)
-        bh, bl = split_table(self.backward)
-        return [self.left, fh, fl, bh, bl, self.weights]
-
-
-def three(value):
-    upper, lower = split_value(value)
-    return jnp.concatenate([upper, upper, lower], axis=0)
+        return [self.left, self.forward, self.backward, self.weights]
+
+
+def both_parts(value):
+    return jnp.concatenate(split_value(value), axis=0)
 
 
 def dot(a, b):
     return jnp.dot(a, b, preferred_element_type=jnp.float32)
 
 
-def product(value, upper_table, lower_table):
+def product(value, table):
     rows = value.shape[0]
-    upper, lower = split_value(value)
-    both = dot(jnp.concatenate([upper, lower], axis=0), upper_table)
-    return both[:rows] + both[rows:] + dot(upper, lower_table)
-
-
-def solve(plan, cube, left, fh, fl, bh, bl, weights, mid):
+    both = dot(both_parts(value), table)
+    return both[:rows] + both[rows:]
+
+
+def solve(plan, cube, left, forward, backward, weights, mid):
     edge, half, inner, outer, block = plan.edge, plan.half, plan.inner, plan.outer, plan.block
     left_all = left[...]
     values = jnp.concatenate(
         [cube[pl.ds(c, edge, stride=plan.plane_rows), :].astype(bf16) for c in range(plan.plane_rows)], axis=1)
-    spectrum = dot(left_all[:, :2 * edge], jnp.concatenate([values, values], axis=0))
+    spectrum = dot(left_all[:, :edge], values)
 
     def tile(h, c):
         return jnp.concatenate([
@@ -224,16 +219,16 @@
             window = [jnp.where(lane >= low - base, tiles[0][c], tiles[1][c + 1]),
                       jnp.where(lane < high - base - lanes, tiles[0][c + 1], tiles[1][c])]
         rows = slice(2 * lanes * j, 2 * lanes * (j + 1))
-        result = product(jnp.concatenate(window, axis=1), fh[rows, :], fl[rows, :])
+        result = product(jnp.concatenate(window, axis=1), forward[rows, :])
         for b in range(outer):
             for o in range(2):
                 y = b * inner + 2 * j + o
                 mid[y * half:(y + 1) * half, :] = result[b * half:(b + 1) * half, o * lanes:(o + 1) * lanes]
     for k in range(0, half, 2):
         value = jnp.concatenate([mid[pl.ds(k + o, edge, stride=half), :] for o in range(2)], axis=1)
-        value = dot(left_all, three(value))
+        value = dot(left_all, both_parts(value))
         value = value * jnp.concatenate([weights[k], weights[k + 1]], axis=1)
-        value = dot(left_all, three(value))
+        value = dot(left_all, both_parts(value))
         for o in range(2):
             mid[pl.ds(k + o, edge, stride=half), :] = value[:, o * lanes:(o + 1) * lanes]
     results = []
@@ -242,7 +237,7 @@
         value = jnp.concatenate([
             jnp.concatenate([mid[(b * inner + 2 * j + o) * half:(b * inner + 2 * j + o + 1) * half, :] for b in range(outer)], axis=0)
             for o in range(2)], axis=1)
-        results.append(product(value, bh[rows, :], bl[rows, :]))
+        results.append(product(value, backward[rows, :]))
 
     def gathered(h, c):
         value = None
@@ -257,7 +252,7 @@
     value = jnp.concatenate([
         jnp.concatenate([tiles[h][c][b * half:(b + 1) * half] for h in range(2)], axis=0)
         for b in range(outer) for c in range(plan.block_rows)], axis=1)
-    value = dot(left_all, three(value))
+    value = dot(left_all, both_parts(value))
     for c in range(plan.plane_rows):
         cube[pl.ds(c, edge, stride=plan.plane_rows), :] = value[:, c * lanes:(c + 1) * lanes]
 

time: 38.5 us -> 38.2 us (level)
  no operation moved by 1% of the time
where the time goes in v8:
time: 38.2 us; the launch traced here: 38 us
  blocking collectives  21.3 us (56%)
  waiting for transfers between devices  5.85 us (15%)
  Pallas kernels  5.7 us (15%)
  starting transfers between devices  5.07 us (13%)
    all_to_all x1, blocking collectives, quick_body(): lax.all_to_all(blocks, ('half', 'part'), 0, 0, axis_index_groups=[far])  11.8 us
    all_to_all x1, blocking collectives, quick_body(): lax.all_to_all(sent, ('part', 'grid'), 0, 0, axis_index_groups=[near])  9.5 us
    ppermute x6, waiting for transfers between devices, exchange(): lax.ppermute(value, 'grid', [(i, i ^ offset) for i in range(grid_count)])  5.85 us
    ppermute x6, starting transfers between devices, exchange(): lax.ppermute(value, 'grid', [(i, i ^ offset) for i in range(grid_count)])  5.07 us
    pallas_call x1, Pallas kernels, read_points(): pl.pallas_call(kernel, out_shape=[pltpu.VMEM((8, lanes), f32), pltpu.VMEM...  2.18 us
    pallas_call x1, Pallas kernels, potentials(): pl.pallas_call(kernel, out_shape=jax.ShapeDtypeStruct((parts * grid_count...  1.4 us
    pallas_call x1, Pallas kernels, settle(): pl.pallas_call(kernel, out_shape=jax.ShapeDtypeStruct((parts * part, keep...  0.83 us
  transfers between devices with their start and end apart: 6, of which 4 were waited for; matrix products, arithmetic and copies ran while one was open for 0% of the time, Pallas kernels for 0%

profile of v8, /device:TPU:0, one launch (start us, length us, event | category | flops | bytes accessed | tf_op | source)
XLA Modules:
  0.0 38.0 jit_solution(4662872577687458050)
XLA Ops:
  0.0 0.0 copy-start
  0.0 0.0 copy-start.1
  0.0 0.0 copy-start.2
  0.0 0.0 copy-start.3
  0.0 0.0 copy-start.4
  0.0 2.2 %read_points.1 = (f32[8,128]{1,0:T(8,128)S(1)}, f32[56,128]{1,0:T(8,128)S(1)}) custom-call(s32[4]{0:T(128)} %points_hbm.1, s32[16]{0:T(128)} %targets_hbm.1, f32[4,4]{1,0:T(4,128)} %fit_hbm.1, bf16[64,27648]{1,0:T(8,128)(2,1)} %orbitals_ref.5), custom_call_target="tpu_custom_call" | custom-call | tf_op jit(solution)/shard_map/read_points/pallas_call | solution.py:326
  2.2 2.5 %collective-permute-start.2 = (f32[8,128]{1,0:T(8,128)S(1)}, f32[8,128]{1,0:T(8,128)S(1)}, u32[]{:S(2)}, u32[]{:S(2)}) collective-permute-start(f32[8,128]{1,0:T(8,128)S(1)} %get-tuple-element.13.refs_0_), channel_id=1, source_target_pairs={{0,3},{1,2},{2,1},{3,0},{4,7},{5,6},{6,5},{7,4},{8,11},{9,10},{10,... | collective-permute-start | bytes 12296 | tf_op jit(solution)/shard_map/ppermute | solution.py:491
  4.7 0.6 %collective-permute-start.1 = (f32[8,128]{1,0:T(8,128)S(1)}, f32[8,128]{1,0:T(8,128)S(1)}, u32[]{:S(2)}, u32[]{:S(2)}) collective-permute-start(f32[8,128]{1,0:T(8,128)S(1)} %get-tuple-element.13.refs_0_), channel_id=1, source_target_pairs={{0,2},{1,3},{2,0},{3,1},{4,6},{5,7},{6,4},{7,5},{8,10},{9,11},{10,... | collective-permute-start | bytes 12296 | tf_op jit(solution)/shard_map/ppermute | solution.py:491
  5.3 0.0 collective-permute-start
  5.4 0.6 %collective-permute-done.2.refs_3_ = f32[8,128]{1,0:T(8,128)S(1)} collective-permute-done((f32[8,128]{1,0:T(8,128)S(1)}, f32[8,128]{1,0:T(8,128)S(1)}, u32[]{:S(2)}, u32[]{:S(2)}) %collective-permute-start.2) | collective-permute-done | bytes 4128 | tf_op jit(solution)/shard_map/ppermute | solution.py:491
  6.0 2.3 %collective-permute-done.1.refs_2_ = f32[8,128]{1,0:T(8,128)S(1)} collective-permute-done((f32[8,128]{1,0:T(8,128)S(1)}, f32[8,128]{1,0:T(8,128)S(1)}, u32[]{:S(2)}, u32[]{:S(2)}) %collective-permute-start.1) | collective-permute-done | bytes 4128 | tf_op jit(solution)/shard_map/ppermute | solution.py:491
  8.3 0.0 collective-permute-done.refs_1_
  8.3 0.0 copy-done
  8.3 0.7 %fit_pairs.1 = (bf16[216,128]{1,0:T(8,128)(2,1)S(1)}, bf16[216,128]{1,0:T(8,128)(2,1)S(1)}, bf16[216,128]{1,0:T(8,128)(2,1)S(1)}, bf16[216,128]{1,0:T(8,128)(2,1)S(1)}, f32[8,128]{1,0:T(8,128)S(1)}) custom-call(f32[56,128]{1,0:T(8,128)S(1)} %get-tuple-element.12.notes_ref, bf16[64,27648]{1,0:T(8,128)(2,1)S(1)} %copy-done, ...), custom_call_target="tpu_custom_call" | custom-call | tf_op jit(solution)/shard_map/fit_pairs/pallas_call | solution.py:378
  9.0 0.1 collective-permute-start.3
  9.1 1.1 %collective-permute-start.4 = (bf16[216,128]{1,0:T(8,128)(2,1)S(1)}, bf16[216,128]{1,0:T(8,128)(2,1)S(1)}, u32[]{:S(2)}, u32[]{:S(2)}) collective-permute-start(bf16[216,128]{1,0:T(8,128)(2,1)S(1)} %get-tuple-element.17), channel_id=1, source_target_pairs={{0,2},{1,3},{2,0},{3,1},{4,6},{5,7},{6,4},{7,5},{8,10},{9,11},{10,... | collective-permute-start | bytes 165896 | tf_op jit(solution)/shard_map/ppermute | solution.py:491
  10.2 0.7 %collective-permute-start.5 = (bf16[216,128]{1,0:T(8,128)(2,1)S(1)}, bf16[216,128]{1,0:T(8,128)(2,1)S(1)}, u32[]{:S(2)}, u32[]{:S(2)}) collective-permute-start(bf16[216,128]{1,0:T(8,128)(2,1)S(1)} %get-tuple-element.18), channel_id=1, source_target_pairs={{0,1},{1,0},{2,3},{3,2},{4,5},{5,4},{6,7},{7,6},{8,9},{9,8},{10,11... | collective-permute-start | bytes 165896 | tf_op jit(solution)/shard_map/ppermute | solution.py:491
  10.9 2.3 %collective-permute-done.3.refs_1_ = bf16[216,128]{1,0:T(8,128)(2,1)S(1)} collective-permute-done((bf16[216,128]{1,0:T(8,128)(2,1)S(1)}, bf16[216,128]{1,0:T(8,128)(2,1)S(1)}, u32[]{:S(2)}, u32[]{:S(2)}) %collective-permute-start.3) | collective-permute-done | bytes 55328 | tf_op jit(solution)/shard_map/ppermute | solution.py:491
  13.3 0.6 %collective-permute-done.4.refs_2_ = bf16[216,128]{1,0:T(8,128)(2,1)S(1)} collective-permute-done((bf16[216,128]{1,0:T(8,128)(2,1)S(1)}, bf16[216,128]{1,0:T(8,128)(2,1)S(1)}, u32[]{:S(2)}, u32[]{:S(2)}) %collective-permute-start.4) | collective-permute-done | bytes 55328 | tf_op jit(solution)/shard_map/ppermute | solution.py:491
  13.9 0.0 collective-permute-done.5.refs_3_
  13.9 0.0 copy-done.1
  13.9 0.0 copy-done.2
  13.9 0.0 copy-done.3
  13.9 0.0 copy-done.4
  13.9 1.4 %potentials.1 = bf16[16,56,128]{2,1,0:T(8,128)(2,1)S(1)} custom-call(f32[8,128]{1,0:T(8,128)S(1)} %get-tuple-element.14.at_ref, bf16[216,128]{1,0:T(8,128)(2,1)S(1)} %get-tuple-element.15.refs_0_, bf16[216,128]{1,0:T(8,128)(2,1)S(1)} %collective-permute-done.3.refs_1_, bf16[216,128]{1,0:T(8,128)(2,1)S(1)} %collective-permute-done.4.refs_2_, ...), custom_call_target="tpu_custom_call" | custom-call | tf_op jit(solution)/shard_map/potentials/pallas_call | solution.py:410
  15.3 9.5 %all_to_all.10.received_ref = bf16[16,56,128]{2,1,0:T(8,128)(2,1)S(1)} all-to-all(bf16[16,56,128]{2,1,0:T(8,128)(2,1)S(1)} %potentials.1), channel_id=1, replica_groups={{15,14,13,12,11,10,9,8,7,6,5,4,3,2,1,0},{31,30,29,28,27,26,25,24,23,22,..., dimensions={0} | all-to-all | bytes 458752 | tf_op jit(solution)/shard_map/all_to_all | solution.py:509
  24.8 0.6 %apply_part.1 = bf16[8,108,128]{2,1,0:T(8,128)(2,1)S(1)} custom-call(f32[56,128]{1,0:T(8,128)S(1)} %get-tuple-element.12.notes_ref, bf16[64,27648]{1,0:T(8,128)(2,1)S(1)} %copy-done, bf16[16,56,128]{2,1,0:T(8,128)(2,1)S(1)} %all_to_all.10.received_ref), custom_call_target="tpu_custom_call" | custom-call | tf_op jit(solution)/shard_map/apply_part/pallas_call | solution.py:449
  25.4 11.8 %all_to_all.11.kept_ref = bf16[8,108,128]{2,1,0:T(8,128)(2,1)S(1)} all-to-all(bf16[8,108,128]{2,1,0:T(8,128)(2,1)S(1)} %apply_part.1), channel_id=1, replica_groups={{16,20,28,24,8,12,4,0},{17,21,29,25,9,13,5,1},{18,22,30,26,10,14,6,2},{..., dimensions={0} | all-to-all | bytes 442368 | tf_op jit(solution)/shard_map/all_to_all | solution.py:511
  37.1 0.8 %settle.1 = f32[216,2,128]{2,1,0:T(2,128)} custom-call(bf16[8,108,128]{2,1,0:T(8,128)(2,1)S(1)} %all_to_all.11.kept_ref), custom_call_target="tpu_custom_call" | custom-call | tf_op jit(solution)/shard_map/settle/pallas_call | solution.py:475
Async XLA Ops:
  0.0 8.3 %copy-start = (bf16[64,27648]{1,0:T(8,128)(2,1)S(1)}, bf16[64,27648]{1,0:T(8,128)(2,1)}, u32[]{:S(2)}) copy-start(bf16[64,27648]{1,0:T(8,128)(2,1)} %orbitals_ref.5) | copy-start | bytes 10616836
  0.0 13.9 %copy-start.1 = (f32[24,48,128]{2,1,0:T(8,128)S(1)}, f32[24,48,128]{2,1,0:T(8,128)}, u32[]{:S(2)}) copy-start(f32[24,48,128]{2,1,0:T(8,128)} %constant.11.clone.refs_7_) | copy-start | bytes 1769476
  0.0 13.9 %copy-start.2 = (bf16[1024,256]{1,0:T(8,128)(2,1)S(1)}, bf16[1024,256]{1,0:T(8,128)(2,1)}, u32[]{:S(2)}) copy-start(bf16[1024,256]{1,0:T(8,128)(2,1)} %constant.10.clone.refs_6_) | copy-start | bytes 1572868
  0.0 13.9 %copy-start.3 = (bf16[1024,256]{1,0:T(8,128)(2,1)S(1)}, bf16[1024,256]{1,0:T(8,128)(2,1)}, u32[]{:S(2)}) copy-start(bf16[1024,256]{1,0:T(8,128)(2,1)} %constant.9.clone.refs_5_) | copy-start | bytes 1572868
  0.0 13.9 %copy-start.4 = (bf16[48,96]{1,0:T(8,128)(2,1)S(1)}, bf16[48,96]{1,0:T(8,128)(2,1)}, u32[]{:S(2)}) copy-start(bf16[48,96]{1,0:T(8,128)(2,1)} %constant.8.clone.refs_4_) | copy-start | bytes 27652
  2.2 3.8 %collective-permute-start.2 = (f32[8,128]{1,0:T(8,128)S(1)}, f32[8,128]{1,0:T(8,128)S(1)}, u32[]{:S(2)}, u32[]{:S(2)}) collective-permute-start(f32[8,128]{1,0:T(8,128)S(1)} %get-tuple-element.13.refs_0_), channel_id=1, source_target_pairs={{0,3},{1,2},{2,1},{3,0},{4,7},{5,6},{6,5},{7,4},{8,11},{9,10},{10,... | collective-permute-start | bytes 12296 | tf_op jit(solution)/shard_map/ppermute | solution.py:491
  4.7 3.6 %collective-permute-start.1 = (f32[8,128]{1,0:T(8,128)S(1)}, f32[8,128]{1,0:T(8,128)S(1)}, u32[]{:S(2)}, u32[]{:S(2)}) collective-permute-start(f32[8,128]{1,0:T(8,128)S(1)} %get-tuple-element.13.refs_0_), channel_id=1, source_target_pairs={{0,2},{1,3},{2,0},{3,1},{4,6},{5,7},{6,4},{7,5},{8,10},{9,11},{10,... | collective-permute-start | bytes 12296 | tf_op jit(solution)/shard_map/ppermute | solution.py:491
  5.3 3.0 %collective-permute-start = (f32[8,128]{1,0:T(8,128)S(1)}, f32[8,128]{1,0:T(8,128)S(1)}, u32[]{:S(2)}, u32[]{:S(2)}) collective-permute-start(f32[8,128]{1,0:T(8,128)S(1)} %get-tuple-element.13.refs_0_), channel_id=1, source_target_pairs={{0,1},{1,0},{2,3},{3,2},{4,5},{5,4},{6,7},{7,6},{8,9},{9,8},{10,11... | collective-permute-start | bytes 12296 | tf_op jit(solution)/shard_map/ppermute | solution.py:491
  9.0 4.2 %collective-permute-start.3 = (bf16[216,128]{1,0:T(8,128)(2,1)S(1)}, bf16[216,128]{1,0:T(8,128)(2,1)S(1)}, u32[]{:S(2)}, u32[]{:S(2)}) collective-permute-start(bf16[216,128]{1,0:T(8,128)(2,1)S(1)} %get-tuple-element.16), channel_id=1, source_target_pairs={{0,3},{1,2},{2,1},{3,0},{4,7},{5,6},{6,5},{7,4},{8,11},{9,10},{10,... | collective-permute-start | bytes 165896 | tf_op jit(solution)/shard_map/ppermute | solution.py:491
  9.1 4.8 %collective-permute-start.4 = (bf16[216,128]{1,0:T(8,128)(2,1)S(1)}, bf16[216,128]{1,0:T(8,128)(2,1)S(1)}, u32[]{:S(2)}, u32[]{:S(2)}) collective-permute-start(bf16[216,128]{1,0:T(8,128)(2,1)S(1)} %get-tuple-element.17), channel_id=1, source_target_pairs={{0,2},{1,3},{2,0},{3,1},{4,6},{5,7},{6,4},{7,5},{8,10},{9,11},{10,... | collective-permute-start | bytes 165896 | tf_op jit(solution)/shard_map/ppermute | solution.py:491
  10.2 3.6 %collective-permute-start.5 = (bf16[216,128]{1,0:T(8,128)(2,1)S(1)}, bf16[216,128]{1,0:T(8,128)(2,1)S(1)}, u32[]{:S(2)}, u32[]{:S(2)}) collective-permute-start(bf16[216,128]{1,0:T(8,128)(2,1)S(1)} %get-tuple-element.18), channel_id=1, source_target_pairs={{0,1},{1,0},{2,3},{3,2},{4,5},{5,4},{6,7},{7,6},{8,9},{9,8},{10,11... | collective-permute-start | bytes 165896 | tf_op jit(solution)/shard_map/ppermute | solution.py:491

commit v9 on v8

--- a/solution.py
+++ b/solution.py
@@ -483,6 +483,13 @@
     )(kept)
 
 
+def bits_reversed(count):
+    order = [0]
+    while len(order) < count:
+        order = [2 * i for i in order] + [2 * i + 1 for i in order]
+    return order
+
+
 def places(order):
     return [order.index(i) for i in range(len(order))]
 
@@ -503,8 +510,8 @@
     *pieces, at = fit_pairs(orbitals, notes, shares)
     offsets = [0] + list(reversed(range(1, grid_count)))
     pieces = [exchange(pieces[d], grid_count, d) if d else pieces[d] for d in offsets]
-    near = list(reversed(range(part_count * grid_count)))
-    far = [s ^ (s >> 1) for s in reversed(range(slab_count))]
+    near = bits_reversed(part_count * grid_count)[::-1]
+    far = [s ^ (s >> 1) ^ 1 for s in reversed(range(slab_count))]
     sent = potentials(plan, pieces, offsets, at, part_count, places(near))
     received = lax.all_to_all(sent, ("part", "grid"), 0, 0, axis_index_groups=[near])
     blocks = apply_part(orbitals, notes, received, part, count, places(far), halves)
@@ -527,7 +534,8 @@
         and edge <= lanes // 2
         and cells % (grid_count * lanes) == 0
         and shard_rows % 8 == 0
-        and slab_count % 2 == 0
+        and slab_count > 1
+        and (slab_count * grid_count).bit_count() == 1
         and shard_rows % (slab_count // 2) == 0
         and targets.shape[0] % slab_count == 0
         and targets.shape[0] % 8 == 0

time: 38.2 us -> 37.8 us (0.990)
  blocking collectives: 21.3 us -> 20.9 us
where the time goes in v9:
time: 37.8 us; the launch traced here: 37.6 us
  blocking collectives  20.9 us (55%)
  waiting for transfers between devices  5.85 us (15%)
  Pallas kernels  5.7 us (15%)
  starting transfers between devices  5.07 us (13%)
    all_to_all x1, blocking collectives, quick_body(): lax.all_to_all(blocks, ('half', 'part'), 0, 0, axis_index_groups=[far])  11.7 us
    all_to_all x1, blocking collectives, quick_body(): lax.all_to_all(sent, ('part', 'grid'), 0, 0, axis_index_groups=[near])  9.24 us
    ppermute x6, waiting for transfers between devices, exchange(): lax.ppermute(value, 'grid', [(i, i ^ offset) for i in range(grid_count)])  5.85 us
    ppermute x6, starting transfers between devices, exchange(): lax.ppermute(value, 'grid', [(i, i ^ offset) for i in range(grid_count)])  5.07 us
    pallas_call x1, Pallas kernels, read_points(): pl.pallas_call(kernel, out_shape=[pltpu.VMEM((8, lanes), f32), pltpu.VMEM...  2.18 us
    pallas_call x1, Pallas kernels, potentials(): pl.pallas_call(kernel, out_shape=jax.ShapeDtypeStruct((parts * grid_count...  1.4 us
    pallas_call x1, Pallas kernels, settle(): pl.pallas_call(kernel, out_shape=jax.ShapeDtypeStruct((parts * part, keep...  0.83 us
  transfers between devices with their start and end apart: 6, of which 4 were waited for; matrix products, arithmetic and copies ran while one was open for 0% of the time, Pallas kernels for 0%

profile of v9, /device:TPU:0, one launch (start us, length us, event | category | flops | bytes accessed | tf_op | source)
XLA Modules:
  0.0 37.6 jit_solution(12698249090438986653)
XLA Ops:
  0.0 0.0 copy-start
  0.0 0.0 copy-start.1
  0.0 0.0 copy-start.2
  0.0 0.0 copy-start.3
  0.0 0.0 copy-start.4
  0.0 2.2 %read_points.1 = (f32[8,128]{1,0:T(8,128)S(1)}, f32[56,128]{1,0:T(8,128)S(1)}) custom-call(s32[4]{0:T(128)} %points_hbm.1, s32[16]{0:T(128)} %targets_hbm.1, f32[4,4]{1,0:T(4,128)} %fit_hbm.1, bf16[64,27648]{1,0:T(8,128)(2,1)} %orbitals_ref.5), custom_call_target="tpu_custom_call" | custom-call | tf_op jit(solution)/shard_map/read_points/pallas_call | solution.py:326
  2.2 2.5 %collective-permute-start.2 = (f32[8,128]{1,0:T(8,128)S(1)}, f32[8,128]{1,0:T(8,128)S(1)}, u32[]{:S(2)}, u32[]{:S(2)}) collective-permute-start(f32[8,128]{1,0:T(8,128)S(1)} %get-tuple-element.13.refs_0_), channel_id=1, source_target_pairs={{0,3},{1,2},{2,1},{3,0},{4,7},{5,6},{6,5},{7,4},{8,11},{9,10},{10,... | collective-permute-start | bytes 12296 | tf_op jit(solution)/shard_map/ppermute | solution.py:498
  4.7 0.6 %collective-permute-start.1 = (f32[8,128]{1,0:T(8,128)S(1)}, f32[8,128]{1,0:T(8,128)S(1)}, u32[]{:S(2)}, u32[]{:S(2)}) collective-permute-start(f32[8,128]{1,0:T(8,128)S(1)} %get-tuple-element.13.refs_0_), channel_id=1, source_target_pairs={{0,2},{1,3},{2,0},{3,1},{4,6},{5,7},{6,4},{7,5},{8,10},{9,11},{10,... | collective-permute-start | bytes 12296 | tf_op jit(solution)/shard_map/ppermute | solution.py:498
  5.3 0.0 collective-permute-start
  5.4 0.6 %collective-permute-done.2.refs_3_ = f32[8,128]{1,0:T(8,128)S(1)} collective-permute-done((f32[8,128]{1,0:T(8,128)S(1)}, f32[8,128]{1,0:T(8,128)S(1)}, u32[]{:S(2)}, u32[]{:S(2)}) %collective-permute-start.2) | collective-permute-done | bytes 4128 | tf_op jit(solution)/shard_map/ppermute | solution.py:498
  6.0 2.3 %collective-permute-done.1.refs_2_ = f32[8,128]{1,0:T(8,128)S(1)} collective-permute-done((f32[8,128]{1,0:T(8,128)S(1)}, f32[8,128]{1,0:T(8,128)S(1)}, u32[]{:S(2)}, u32[]{:S(2)}) %collective-permute-start.1) | collective-permute-done | bytes 4128 | tf_op jit(solution)/shard_map/ppermute | solution.py:498
  8.3 0.0 collective-permute-done.refs_1_
  8.3 0.0 copy-done
  8.3 0.7 %fit_pairs.1 = (bf16[216,128]{1,0:T(8,128)(2,1)S(1)}, bf16[216,128]{1,0:T(8,128)(2,1)S(1)}, bf16[216,128]{1,0:T(8,128)(2,1)S(1)}, bf16[216,128]{1,0:T(8,128)(2,1)S(1)}, f32[8,128]{1,0:T(8,128)S(1)}) custom-call(f32[56,128]{1,0:T(8,128)S(1)} %get-tuple-element.12.notes_ref, bf16[64,27648]{1,0:T(8,128)(2,1)S(1)} %copy-done, ...), custom_call_target="tpu_custom_call" | custom-call | tf_op jit(solution)/shard_map/fit_pairs/pallas_call | solution.py:378
  9.0 0.1 collective-permute-start.3
  9.1 1.1 %collective-permute-start.4 = (bf16[216,128]{1,0:T(8,128)(2,1)S(1)}, bf16[216,128]{1,0:T(8,128)(2,1)S(1)}, u32[]{:S(2)}, u32[]{:S(2)}) collective-permute-start(bf16[216,128]{1,0:T(8,128)(2,1)S(1)} %get-tuple-element.17), channel_id=1, source_target_pairs={{0,2},{1,3},{2,0},{3,1},{4,6},{5,7},{6,4},{7,5},{8,10},{9,11},{10,... | collective-permute-start | bytes 165896 | tf_op jit(solution)/shard_map/ppermute | solution.py:498
  10.2 0.7 %collective-permute-start.5 = (bf16[216,128]{1,0:T(8,128)(2,1)S(1)}, bf16[216,128]{1,0:T(8,128)(2,1)S(1)}, u32[]{:S(2)}, u32[]{:S(2)}) collective-permute-start(bf16[216,128]{1,0:T(8,128)(2,1)S(1)} %get-tuple-element.18), channel_id=1, source_target_pairs={{0,1},{1,0},{2,3},{3,2},{4,5},{5,4},{6,7},{7,6},{8,9},{9,8},{10,11... | collective-permute-start | bytes 165896 | tf_op jit(solution)/shard_map/ppermute | solution.py:498
  10.9 2.3 %collective-permute-done.3.refs_1_ = bf16[216,128]{1,0:T(8,128)(2,1)S(1)} collective-permute-done((bf16[216,128]{1,0:T(8,128)(2,1)S(1)}, bf16[216,128]{1,0:T(8,128)(2,1)S(1)}, u32[]{:S(2)}, u32[]{:S(2)}) %collective-permute-start.3) | collective-permute-done | bytes 55328 | tf_op jit(solution)/shard_map/ppermute | solution.py:498
  13.3 0.6 %collective-permute-done.4.refs_2_ = bf16[216,128]{1,0:T(8,128)(2,1)S(1)} collective-permute-done((bf16[216,128]{1,0:T(8,128)(2,1)S(1)}, bf16[216,128]{1,0:T(8,128)(2,1)S(1)}, u32[]{:S(2)}, u32[]{:S(2)}) %collective-permute-start.4) | collective-permute-done | bytes 55328 | tf_op jit(solution)/shard_map/ppermute | solution.py:498
  13.9 0.0 collective-permute-done.5.refs_3_
  13.9 0.0 copy-done.1
  13.9 0.0 copy-done.2
  13.9 0.0 copy-done.3
  13.9 0.0 copy-done.4
  13.9 1.4 %potentials.1 = bf16[16,56,128]{2,1,0:T(8,128)(2,1)S(1)} custom-call(f32[8,128]{1,0:T(8,128)S(1)} %get-tuple-element.14.at_ref, bf16[216,128]{1,0:T(8,128)(2,1)S(1)} %get-tuple-element.15.refs_0_, bf16[216,128]{1,0:T(8,128)(2,1)S(1)} %collective-permute-done.3.refs_1_, bf16[216,128]{1,0:T(8,128)(2,1)S(1)} %collective-permute-done.4.refs_2_, ...), custom_call_target="tpu_custom_call" | custom-call | tf_op jit(solution)/shard_map/potentials/pallas_call | solution.py:410
  15.3 9.2 %all_to_all.10.received_ref = bf16[16,56,128]{2,1,0:T(8,128)(2,1)S(1)} all-to-all(bf16[16,56,128]{2,1,0:T(8,128)(2,1)S(1)} %potentials.1), channel_id=1, replica_groups={{15,7,11,3,13,5,9,1,14,6,10,2,12,4,8,0},{31,23,27,19,29,21,25,17,30,22,..., dimensions={0} | all-to-all | bytes 458752 | tf_op jit(solution)/shard_map/all_to_all | solution.py:516
  24.5 0.6 %apply_part.1 = bf16[8,108,128]{2,1,0:T(8,128)(2,1)S(1)} custom-call(f32[56,128]{1,0:T(8,128)S(1)} %get-tuple-element.12.notes_ref, bf16[64,27648]{1,0:T(8,128)(2,1)S(1)} %copy-done, bf16[16,56,128]{2,1,0:T(8,128)(2,1)S(1)} %all_to_all.10.received_ref), custom_call_target="tpu_custom_call" | custom-call | tf_op jit(solution)/shard_map/apply_part/pallas_call | solution.py:449
  25.1 11.7 %all_to_all.11.kept_ref = bf16[8,108,128]{2,1,0:T(8,128)(2,1)S(1)} all-to-all(bf16[8,108,128]{2,1,0:T(8,128)(2,1)S(1)} %apply_part.1), channel_id=1, replica_groups={{20,16,24,28,12,8,0,4},{21,17,25,29,13,9,1,5},{22,18,26,30,14,10,2,6},{..., dimensions={0} | all-to-all | bytes 442368 | tf_op jit(solution)/shard_map/all_to_all | solution.py:518
  36.8 0.8 %settle.1 = f32[216,2,128]{2,1,0:T(2,128)} custom-call(bf16[8,108,128]{2,1,0:T(8,128)(2,1)S(1)} %all_to_all.11.kept_ref), custom_call_target="tpu_custom_call" | custom-call | tf_op jit(solution)/shard_map/settle/pallas_call | solution.py:475
Async XLA Ops:
  0.0 8.3 %copy-start = (bf16[64,27648]{1,0:T(8,128)(2,1)S(1)}, bf16[64,27648]{1,0:T(8,128)(2,1)}, u32[]{:S(2)}) copy-start(bf16[64,27648]{1,0:T(8,128)(2,1)} %orbitals_ref.5) | copy-start | bytes 10616836
  0.0 13.9 %copy-start.1 = (f32[24,48,128]{2,1,0:T(8,128)S(1)}, f32[24,48,128]{2,1,0:T(8,128)}, u32[]{:S(2)}) copy-start(f32[24,48,128]{2,1,0:T(8,128)} %constant.11.clone.refs_7_) | copy-start | bytes 1769476
  0.0 13.9 %copy-start.2 = (bf16[1024,256]{1,0:T(8,128)(2,1)S(1)}, bf16[1024,256]{1,0:T(8,128)(2,1)}, u32[]{:S(2)}) copy-start(bf16[1024,256]{1,0:T(8,128)(2,1)} %constant.10.clone.refs_6_) | copy-start | bytes 1572868
  0.0 13.9 %copy-start.3 = (bf16[1024,256]{1,0:T(8,128)(2,1)S(1)}, bf16[1024,256]{1,0:T(8,128)(2,1)}, u32[]{:S(2)}) copy-start(bf16[1024,256]{1,0:T(8,128)(2,1)} %constant.9.clone.refs_5_) | copy-start | bytes 1572868
  0.0 13.9 %copy-start.4 = (bf16[48,96]{1,0:T(8,128)(2,1)S(1)}, bf16[48,96]{1,0:T(8,128)(2,1)}, u32[]{:S(2)}) copy-start(bf16[48,96]{1,0:T(8,128)(2,1)} %constant.8.clone.refs_4_) | copy-start | bytes 27652
  2.2 3.8 %collective-permute-start.2 = (f32[8,128]{1,0:T(8,128)S(1)}, f32[8,128]{1,0:T(8,128)S(1)}, u32[]{:S(2)}, u32[]{:S(2)}) collective-permute-start(f32[8,128]{1,0:T(8,128)S(1)} %get-tuple-element.13.refs_0_), channel_id=1, source_target_pairs={{0,3},{1,2},{2,1},{3,0},{4,7},{5,6},{6,5},{7,4},{8,11},{9,10},{10,... | collective-permute-start | bytes 12296 | tf_op jit(solution)/shard_map/ppermute | solution.py:498
  4.7 3.6 %collective-permute-start.1 = (f32[8,128]{1,0:T(8,128)S(1)}, f32[8,128]{1,0:T(8,128)S(1)}, u32[]{:S(2)}, u32[]{:S(2)}) collective-permute-start(f32[8,128]{1,0:T(8,128)S(1)} %get-tuple-element.13.refs_0_), channel_id=1, source_target_pairs={{0,2},{1,3},{2,0},{3,1},{4,6},{5,7},{6,4},{7,5},{8,10},{9,11},{10,... | collective-permute-start | bytes 12296 | tf_op jit(solution)/shard_map/ppermute | solution.py:498
  5.3 3.0 %collective-permute-start = (f32[8,128]{1,0:T(8,128)S(1)}, f32[8,128]{1,0:T(8,128)S(1)}, u32[]{:S(2)}, u32[]{:S(2)}) collective-permute-start(f32[8,128]{1,0:T(8,128)S(1)} %get-tuple-element.13.refs_0_), channel_id=1, source_target_pairs={{0,1},{1,0},{2,3},{3,2},{4,5},{5,4},{6,7},{7,6},{8,9},{9,8},{10,11... | collective-permute-start | bytes 12296 | tf_op jit(solution)/shard_map/ppermute | solution.py:498
  9.0 4.2 %collective-permute-start.3 = (bf16[216,128]{1,0:T(8,128)(2,1)S(1)}, bf16[216,128]{1,0:T(8,128)(2,1)S(1)}, u32[]{:S(2)}, u32[]{:S(2)}) collective-permute-start(bf16[216,128]{1,0:T(8,128)(2,1)S(1)} %get-tuple-element.16), channel_id=1, source_target_pairs={{0,3},{1,2},{2,1},{3,0},{4,7},{5,6},{6,5},{7,4},{8,11},{9,10},{10,... | collective-permute-start | bytes 165896 | tf_op jit(solution)/shard_map/ppermute | solution.py:498
  9.1 4.8 %collective-permute-start.4 = (bf16[216,128]{1,0:T(8,128)(2,1)S(1)}, bf16[216,128]{1,0:T(8,128)(2,1)S(1)}, u32[]{:S(2)}, u32[]{:S(2)}) collective-permute-start(bf16[216,128]{1,0:T(8,128)(2,1)S(1)} %get-tuple-element.17), channel_id=1, source_target_pairs={{0,2},{1,3},{2,0},{3,1},{4,6},{5,7},{6,4},{7,5},{8,10},{9,11},{10,... | collective-permute-start | bytes 165896 | tf_op jit(solution)/shard_map/ppermute | solution.py:498
  10.2 3.6 %collective-permute-start.5 = (bf16[216,128]{1,0:T(8,128)(2,1)S(1)}, bf16[216,128]{1,0:T(8,128)(2,1)S(1)}, u32[]{:S(2)}, u32[]{:S(2)}) collective-permute-start(bf16[216,128]{1,0:T(8,128)(2,1)S(1)} %get-tuple-element.18), channel_id=1, source_target_pairs={{0,1},{1,0},{2,3},{3,2},{4,5},{5,4},{6,7},{7,6},{8,9},{9,8},{10,11... | collective-permute-start | bytes 165896 | tf_op jit(solution)/shard_map/ppermute | solution.py:498

commit v10 on v9

--- a/solution.py
+++ b/solution.py
@@ -433,6 +433,7 @@
             spread[m * pitch:(m + 1) * pitch, :] = received_ref[m].astype(f32)
         at = spread[pl.ds(part, points, stride=pitch), :][:, :occupied].astype(bf16)
         first = pl.multiple_of(lax.axis_index("part") * (part * lanes), lanes)
+        swapped = lax.axis_index("grid") % 2 == 1
         density = jnp.dot(at, orbitals_ref[:, pl.ds(first, part * lanes)], preferred_element_type=f32)
         chosen = notes_ref[notes_ref.shape[0] - count:, :][:, :occupied].astype(bf16)
         target_points = lax.dot_general(chosen, at, contract_last, preferred_element_type=f32).astype(bf16)
@@ -444,7 +445,7 @@
         for s in range(slab_count):
             for k in range(keep):
                 stage[s, k * part:(k + 1) * part, :] = mid[pl.ds(s * keep + k, part, stride=count), :]
-            out_ref[place[s]] = stage[s].astype(bf16)
+            out_ref[jnp.where(swapped, place[s ^ 1], place[s])] = stage[s].astype(bf16)
 
     return pl.pallas_call(
         kernel,
@@ -467,10 +468,12 @@
     part = rows // keep
 
     def kernel(kept_ref, out_ref, stage):
+        swapped = lax.axis_index("grid") % 2 == 1
         for q in range(parts):
             stage[q] = sum(kept_ref[j].astype(f32) for j in range(slab_count) if order[j] % parts == q)
+            first = jnp.where(swapped, q ^ 1, q) * part
             for k in range(keep):
-                out_ref[q * part:(q + 1) * part, k, :] = stage[q, k * part:(k + 1) * part, :]
+                out_ref[pl.ds(first, part), k, :] = stage[q, k * part:(k + 1) * part, :]
 
     return pl.pallas_call(
         kernel,
@@ -512,10 +515,11 @@
     pieces = [exchange(pieces[d], grid_count, d) if d else pieces[d] for d in offsets]
     near = bits_reversed(part_count * grid_count)[::-1]
     far = [s ^ (s >> 1) ^ 1 for s in reversed(range(slab_count))]
+    far_groups = [[(s ^ g % 2) * grid_count + g for s in far] for g in range(grid_count)]
     sent = potentials(plan, pieces, offsets, at, part_count, places(near))
     received = lax.all_to_all(sent, ("part", "grid"), 0, 0, axis_index_groups=[near])
     blocks = apply_part(orbitals, notes, received, part, count, places(far), halves)
-    kept = lax.all_to_all(blocks, ("half", "part"), 0, 0, axis_index_groups=[far])
+    kept = lax.all_to_all(blocks, ("half", "part", "grid"), 0, 0, axis_index_groups=far_groups)
     return jnp.transpose(settle(kept, keep, halves, far), (1, 0, 2)).reshape(keep, shard_len)
 
 
@@ -534,7 +538,7 @@
         and edge <= lanes // 2
         and cells % (grid_count * lanes) == 0
         and shard_rows % 8 == 0
-        and slab_count > 1
+        and slab_count > 2
         and (slab_count * grid_count).bit_count() == 1
         and shard_rows % (slab_count // 2) == 0
         and targets.shape[0] % slab_count == 0

time: 37.8 us -> 37.5 us (level)
  no operation moved by 1% of the time
where the time goes in v10:
time: 37.5 us; the launch traced here: 37.3 us
  blocking collectives  20.6 us (55%)
  waiting for transfers between devices  5.85 us (16%)
  Pallas kernels  5.71 us (15%)
  starting transfers between devices  5.07 us (14%)
    all_to_all x1, blocking collectives, quick_body(): lax.all_to_all(blocks, ('half', 'part', 'grid'), 0, 0, axis_index_groups=...  11.3 us
    all_to_all x1, blocking collectives, quick_body(): lax.all_to_all(sent, ('part', 'grid'), 0, 0, axis_index_groups=[near])  9.24 us
    ppermute x6, waiting for transfers between devices, exchange(): lax.ppermute(value, 'grid', [(i, i ^ offset) for i in range(grid_count)])  5.85 us
    ppermute x6, starting transfers between devices, exchange(): lax.ppermute(value, 'grid', [(i, i ^ offset) for i in range(grid_count)])  5.07 us
    pallas_call x1, Pallas kernels, read_points(): pl.pallas_call(kernel, out_shape=[pltpu.VMEM((8, lanes), f32), pltpu.VMEM...  2.18 us
    pallas_call x1, Pallas kernels, potentials(): pl.pallas_call(kernel, out_shape=jax.ShapeDtypeStruct((parts * grid_count...  1.4 us
    pallas_call x1, Pallas kernels, settle(): pl.pallas_call(kernel, out_shape=jax.ShapeDtypeStruct((parts * part, keep...  0.84 us
  transfers between devices with their start and end apart: 6, of which 4 were waited for; matrix products, arithmetic and copies ran while one was open for 0% of the time, Pallas kernels for 0%

profile of v10, /device:TPU:0, one launch (start us, length us, event | category | flops | bytes accessed | tf_op | source)
XLA Modules:
  0.0 37.3 jit_solution(8663305615825434290)
XLA Ops:
  0.0 0.0 copy-start
  0.0 0.0 copy-start.1
  0.0 0.0 copy-start.2
  0.0 0.0 copy-start.3
  0.0 0.0 copy-start.4
  0.0 2.2 %read_points.1 = (f32[8,128]{1,0:T(8,128)S(1)}, f32[56,128]{1,0:T(8,128)S(1)}) custom-call(s32[4]{0:T(128)} %points_hbm.1, s32[16]{0:T(128)} %targets_hbm.1, f32[4,4]{1,0:T(4,128)} %fit_hbm.1, bf16[64,27648]{1,0:T(8,128)(2,1)} %orbitals_ref.5), custom_call_target="tpu_custom_call" | custom-call | tf_op jit(solution)/shard_map/read_points/pallas_call | solution.py:326
  2.2 2.5 %collective-permute-start.2 = (f32[8,128]{1,0:T(8,128)S(1)}, f32[8,128]{1,0:T(8,128)S(1)}, u32[]{:S(2)}, u32[]{:S(2)}) collective-permute-start(f32[8,128]{1,0:T(8,128)S(1)} %get-tuple-element.13.refs_0_), channel_id=1, source_target_pairs={{0,3},{1,2},{2,1},{3,0},{4,7},{5,6},{6,5},{7,4},{8,11},{9,10},{10,... | collective-permute-start | bytes 12296 | tf_op jit(solution)/shard_map/ppermute | solution.py:501
  4.7 0.6 %collective-permute-start.1 = (f32[8,128]{1,0:T(8,128)S(1)}, f32[8,128]{1,0:T(8,128)S(1)}, u32[]{:S(2)}, u32[]{:S(2)}) collective-permute-start(f32[8,128]{1,0:T(8,128)S(1)} %get-tuple-element.13.refs_0_), channel_id=1, source_target_pairs={{0,2},{1,3},{2,0},{3,1},{4,6},{5,7},{6,4},{7,5},{8,10},{9,11},{10,... | collective-permute-start | bytes 12296 | tf_op jit(solution)/shard_map/ppermute | solution.py:501
  5.3 0.0 collective-permute-start
  5.4 0.6 %collective-permute-done.2.refs_3_ = f32[8,128]{1,0:T(8,128)S(1)} collective-permute-done((f32[8,128]{1,0:T(8,128)S(1)}, f32[8,128]{1,0:T(8,128)S(1)}, u32[]{:S(2)}, u32[]{:S(2)}) %collective-permute-start.2) | collective-permute-done | bytes 4128 | tf_op jit(solution)/shard_map/ppermute | solution.py:501
  6.0 2.3 %collective-permute-done.1.refs_2_ = f32[8,128]{1,0:T(8,128)S(1)} collective-permute-done((f32[8,128]{1,0:T(8,128)S(1)}, f32[8,128]{1,0:T(8,128)S(1)}, u32[]{:S(2)}, u32[]{:S(2)}) %collective-permute-start.1) | collective-permute-done | bytes 4128 | tf_op jit(solution)/shard_map/ppermute | solution.py:501
  8.3 0.0 collective-permute-done.refs_1_
  8.3 0.0 copy-done
  8.3 0.7 %fit_pairs.1 = (bf16[216,128]{1,0:T(8,128)(2,1)S(1)}, bf16[216,128]{1,0:T(8,128)(2,1)S(1)}, bf16[216,128]{1,0:T(8,128)(2,1)S(1)}, bf16[216,128]{1,0:T(8,128)(2,1)S(1)}, f32[8,128]{1,0:T(8,128)S(1)}) custom-call(f32[56,128]{1,0:T(8,128)S(1)} %get-tuple-element.12.notes_ref, bf16[64,27648]{1,0:T(8,128)(2,1)S(1)} %copy-done, ...), custom_call_target="tpu_custom_call" | custom-call | tf_op jit(solution)/shard_map/fit_pairs/pallas_call | solution.py:378
  9.0 0.1 collective-permute-start.3
  9.1 1.1 %collective-permute-start.4 = (bf16[216,128]{1,0:T(8,128)(2,1)S(1)}, bf16[216,128]{1,0:T(8,128)(2,1)S(1)}, u32[]{:S(2)}, u32[]{:S(2)}) collective-permute-start(bf16[216,128]{1,0:T(8,128)(2,1)S(1)} %get-tuple-element.17), channel_id=1, source_target_pairs={{0,2},{1,3},{2,0},{3,1},{4,6},{5,7},{6,4},{7,5},{8,10},{9,11},{10,... | collective-permute-start | bytes 165896 | tf_op jit(solution)/shard_map/ppermute | solution.py:501
  10.2 0.7 %collective-permute-start.5 = (bf16[216,128]{1,0:T(8,128)(2,1)S(1)}, bf16[216,128]{1,0:T(8,128)(2,1)S(1)}, u32[]{:S(2)}, u32[]{:S(2)}) collective-permute-start(bf16[216,128]{1,0:T(8,128)(2,1)S(1)} %get-tuple-element.18), channel_id=1, source_target_pairs={{0,1},{1,0},{2,3},{3,2},{4,5},{5,4},{6,7},{7,6},{8,9},{9,8},{10,11... | collective-permute-start | bytes 165896 | tf_op jit(solution)/shard_map/ppermute | solution.py:501
  10.9 2.3 %collective-permute-done.3.refs_1_ = bf16[216,128]{1,0:T(8,128)(2,1)S(1)} collective-permute-done((bf16[216,128]{1,0:T(8,128)(2,1)S(1)}, bf16[216,128]{1,0:T(8,128)(2,1)S(1)}, u32[]{:S(2)}, u32[]{:S(2)}) %collective-permute-start.3) | collective-permute-done | bytes 55328 | tf_op jit(solution)/shard_map/ppermute | solution.py:501
  13.3 0.6 %collective-permute-done.4.refs_2_ = bf16[216,128]{1,0:T(8,128)(2,1)S(1)} collective-permute-done((bf16[216,128]{1,0:T(8,128)(2,1)S(1)}, bf16[216,128]{1,0:T(8,128)(2,1)S(1)}, u32[]{:S(2)}, u32[]{:S(2)}) %collective-permute-start.4) | collective-permute-done | bytes 55328 | tf_op jit(solution)/shard_map/ppermute | solution.py:501
  13.9 0.0 collective-permute-done.5.refs_3_
  13.9 0.0 copy-done.1
  13.9 0.0 copy-done.2
  13.9 0.0 copy-done.3
  13.9 0.0 copy-done.4
  13.9 1.4 %potentials.1 = bf16[16,56,128]{2,1,0:T(8,128)(2,1)S(1)} custom-call(f32[8,128]{1,0:T(8,128)S(1)} %get-tuple-element.14.at_ref, bf16[216,128]{1,0:T(8,128)(2,1)S(1)} %get-tuple-element.15.refs_0_, bf16[216,128]{1,0:T(8,128)(2,1)S(1)} %collective-permute-done.3.refs_1_, bf16[216,128]{1,0:T(8,128)(2,1)S(1)} %collective-permute-done.4.refs_2_, ...), custom_call_target="tpu_custom_call" | custom-call | tf_op jit(solution)/shard_map/potentials/pallas_call | solution.py:410
  15.3 9.2 %all_to_all.10.received_ref = bf16[16,56,128]{2,1,0:T(8,128)(2,1)S(1)} all-to-all(bf16[16,56,128]{2,1,0:T(8,128)(2,1)S(1)} %potentials.1), channel_id=1, replica_groups={{15,7,11,3,13,5,9,1,14,6,10,2,12,4,8,0},{31,23,27,19,29,21,25,17,30,22,..., dimensions={0} | all-to-all | bytes 458752 | tf_op jit(solution)/shard_map/all_to_all | solution.py:520
  24.5 0.6 %apply_part.1 = bf16[8,108,128]{2,1,0:T(8,128)(2,1)S(1)} custom-call(f32[56,128]{1,0:T(8,128)S(1)} %get-tuple-element.12.notes_ref, bf16[64,27648]{1,0:T(8,128)(2,1)S(1)} %copy-done, bf16[16,56,128]{2,1,0:T(8,128)(2,1)S(1)} %all_to_all.10.received_ref), custom_call_target="tpu_custom_call" | custom-call | tf_op jit(solution)/shard_map/apply_part/pallas_call | solution.py:450
  25.1 11.3 %all_to_all.11.kept_ref = bf16[8,108,128]{2,1,0:T(8,128)(2,1)S(1)} all-to-all(bf16[8,108,128]{2,1,0:T(8,128)(2,1)S(1)} %apply_part.1), channel_id=1, replica_groups={{20,16,24,28,12,8,0,4},{17,21,29,25,9,13,5,1},{22,18,26,30,14,10,2,6},{..., dimensions={0} | all-to-all | bytes 442368 | tf_op jit(solution)/shard_map/all_to_all | solution.py:522
  36.4 0.8 %settle.1 = f32[216,2,128]{2,1,0:T(2,128)} custom-call(bf16[8,108,128]{2,1,0:T(8,128)(2,1)S(1)} %all_to_all.11.kept_ref), custom_call_target="tpu_custom_call" | custom-call | tf_op jit(solution)/shard_map/settle/pallas_call | solution.py:478
Async XLA Ops:
  0.0 8.3 %copy-start = (bf16[64,27648]{1,0:T(8,128)(2,1)S(1)}, bf16[64,27648]{1,0:T(8,128)(2,1)}, u32[]{:S(2)}) copy-start(bf16[64,27648]{1,0:T(8,128)(2,1)} %orbitals_ref.5) | copy-start | bytes 10616836
  0.0 13.9 %copy-start.1 = (f32[24,48,128]{2,1,0:T(8,128)S(1)}, f32[24,48,128]{2,1,0:T(8,128)}, u32[]{:S(2)}) copy-start(f32[24,48,128]{2,1,0:T(8,128)} %constant.11.clone.refs_7_) | copy-start | bytes 1769476
  0.0 13.9 %copy-start.2 = (bf16[1024,256]{1,0:T(8,128)(2,1)S(1)}, bf16[1024,256]{1,0:T(8,128)(2,1)}, u32[]{:S(2)}) copy-start(bf16[1024,256]{1,0:T(8,128)(2,1)} %constant.10.clone.refs_6_) | copy-start | bytes 1572868
  0.0 13.9 %copy-start.3 = (bf16[1024,256]{1,0:T(8,128)(2,1)S(1)}, bf16[1024,256]{1,0:T(8,128)(2,1)}, u32[]{:S(2)}) copy-start(bf16[1024,256]{1,0:T(8,128)(2,1)} %constant.9.clone.refs_5_) | copy-start | bytes 1572868
  0.0 13.9 %copy-start.4 = (bf16[48,96]{1,0:T(8,128)(2,1)S(1)}, bf16[48,96]{1,0:T(8,128)(2,1)}, u32[]{:S(2)}) copy-start(bf16[48,96]{1,0:T(8,128)(2,1)} %constant.8.clone.refs_4_) | copy-start | bytes 27652
  2.2 3.8 %collective-permute-start.2 = (f32[8,128]{1,0:T(8,128)S(1)}, f32[8,128]{1,0:T(8,128)S(1)}, u32[]{:S(2)}, u32[]{:S(2)}) collective-permute-start(f32[8,128]{1,0:T(8,128)S(1)} %get-tuple-element.13.refs_0_), channel_id=1, source_target_pairs={{0,3},{1,2},{2,1},{3,0},{4,7},{5,6},{6,5},{7,4},{8,11},{9,10},{10,... | collective-permute-start | bytes 12296 | tf_op jit(solution)/shard_map/ppermute | solution.py:501
  4.7 3.6 %collective-permute-start.1 = (f32[8,128]{1,0:T(8,128)S(1)}, f32[8,128]{1,0:T(8,128)S(1)}, u32[]{:S(2)}, u32[]{:S(2)}) collective-permute-start(f32[8,128]{1,0:T(8,128)S(1)} %get-tuple-element.13.refs_0_), channel_id=1, source_target_pairs={{0,2},{1,3},{2,0},{3,1},{4,6},{5,7},{6,4},{7,5},{8,10},{9,11},{10,... | collective-permute-start | bytes 12296 | tf_op jit(solution)/shard_map/ppermute | solution.py:501
  5.3 3.0 %collective-permute-start = (f32[8,128]{1,0:T(8,128)S(1)}, f32[8,128]{1,0:T(8,128)S(1)}, u32[]{:S(2)}, u32[]{:S(2)}) collective-permute-start(f32[8,128]{1,0:T(8,128)S(1)} %get-tuple-element.13.refs_0_), channel_id=1, source_target_pairs={{0,1},{1,0},{2,3},{3,2},{4,5},{5,4},{6,7},{7,6},{8,9},{9,8},{10,11... | collective-permute-start | bytes 12296 | tf_op jit(solution)/shard_map/ppermute | solution.py:501
  9.0 4.2 %collective-permute-start.3 = (bf16[216,128]{1,0:T(8,128)(2,1)S(1)}, bf16[216,128]{1,0:T(8,128)(2,1)S(1)}, u32[]{:S(2)}, u32[]{:S(2)}) collective-permute-start(bf16[216,128]{1,0:T(8,128)(2,1)S(1)} %get-tuple-element.16), channel_id=1, source_target_pairs={{0,3},{1,2},{2,1},{3,0},{4,7},{5,6},{6,5},{7,4},{8,11},{9,10},{10,... | collective-permute-start | bytes 165896 | tf_op jit(solution)/shard_map/ppermute | solution.py:501
  9.1 4.8 %collective-permute-start.4 = (bf16[216,128]{1,0:T(8,128)(2,1)S(1)}, bf16[216,128]{1,0:T(8,128)(2,1)S(1)}, u32[]{:S(2)}, u32[]{:S(2)}) collective-permute-start(bf16[216,128]{1,0:T(8,128)(2,1)S(1)} %get-tuple-element.17), channel_id=1, source_target_pairs={{0,2},{1,3},{2,0},{3,1},{4,6},{5,7},{6,4},{7,5},{8,10},{9,11},{10,... | collective-permute-start | bytes 165896 | tf_op jit(solution)/shard_map/ppermute | solution.py:501
  10.2 3.6 %collective-permute-start.5 = (bf16[216,128]{1,0:T(8,128)(2,1)S(1)}, bf16[216,128]{1,0:T(8,128)(2,1)S(1)}, u32[]{:S(2)}, u32[]{:S(2)}) collective-permute-start(bf16[216,128]{1,0:T(8,128)(2,1)S(1)} %get-tuple-element.18), channel_id=1, source_target_pairs={{0,1},{1,0},{2,3},{3,2},{4,5},{5,4},{6,7},{7,6},{8,9},{9,8},{10,11... | collective-permute-start | bytes 165896 | tf_op jit(solution)/shard_map/ppermute | solution.py:501

commit v11 on v10

--- a/solution.py
+++ b/solution.py
@@ -380,7 +380,7 @@
         out_shape=[piece] * group + [jax.ShapeDtypeStruct((8, lanes), f32)],
         in_specs=[whole] * (2 + group),
         out_specs=[whole] * (group + 1),
-        scratch_shapes=[pltpu.VMEM((shard_rows * 8, lanes), f32)],
+        scratch_shapes=[pltpu.VMEM((shard_rows * 8 + 8, lanes), f32)],
         compiler_params=params(16),
         name="fit_pairs",
     )(notes, orbitals, *shares)
@@ -413,8 +413,8 @@
         in_specs=[whole] * (1 + grid_count + len(tables)),
         out_specs=whole,
         scratch_shapes=[
-            pltpu.VMEM((plan.rows + 8, lanes), f32),
-            pltpu.VMEM((plan.edge * plan.half, lanes), f32),
+            pltpu.VMEM((plan.rows + plan.plane_rows + sent, lanes), f32),
+            pltpu.VMEM((plan.edge * plan.half + plan.half, lanes), f32),
         ],
         compiler_params=params(24),
         name="potentials",
@@ -445,7 +445,7 @@
         for s in range(slab_count):
             for k in range(keep):
                 stage[s, k * part:(k + 1) * part, :] = mid[pl.ds(s * keep + k, part, stride=count), :]
-            out_ref[jnp.where(swapped, place[s ^ 1], place[s])] = stage[s].astype(bf16)
+            out_ref[jnp.where(swapped, place[s ^ 1], place[s])] = stage[s, :keep * part, :].astype(bf16)
 
     return pl.pallas_call(
         kernel,
@@ -453,9 +453,9 @@
         in_specs=[whole] * 3,
         out_specs=whole,
         scratch_shapes=[
-            pltpu.VMEM((points * pitch, lanes), f32),
-            pltpu.VMEM((part * count, lanes), f32),
-            pltpu.VMEM((slab_count, keep * part, lanes), f32),
+            pltpu.VMEM(((points + 1) * pitch, lanes), f32),
+            pltpu.VMEM((pitch * count + count, lanes), f32),
+            pltpu.VMEM((slab_count, keep * pitch, lanes), f32),
         ],
         compiler_params=params(16),
         name="apply_part",
@@ -467,20 +467,31 @@
     parts = slab_count // halves
     part = rows // keep
 
-    def kernel(kept_ref, out_ref, stage):
+    room = -(-part // 8) * 8
+
+    def kernel(kept_ref, out_ref, stage, rowed, sems):
         swapped = lax.axis_index("grid") % 2 == 1
+        copies = []
         for q in range(parts):
-            stage[q] = sum(kept_ref[j].astype(f32) for j in range(slab_count) if order[j] % parts == q)
+            stage[q, :rows, :] = sum(kept_ref[j].astype(f32) for j in range(slab_count) if order[j] % parts == q)
+            for k in range(keep):
+                rowed[q, :part, k, :] = stage[q, k * part:(k + 1) * part, :]
             first = jnp.where(swapped, q ^ 1, q) * part
-            for k in range(keep):
-                out_ref[pl.ds(first, part), k, :] = stage[q, k * part:(k + 1) * part, :]
+            copies.append(pltpu.make_async_copy(rowed.at[q, pl.ds(0, part)], out_ref.at[pl.ds(first, part)], sems.at[q]))
+            copies[-1].start()
+        for copy in copies:
+            copy.wait()
 
     return pl.pallas_call(
         kernel,
         out_shape=jax.ShapeDtypeStruct((parts * part, keep, lanes), f32),
         in_specs=[whole],
-        out_specs=whole,
-        scratch_shapes=[pltpu.VMEM((parts, rows, lanes), f32)],
+        out_specs=far,
+        scratch_shapes=[
+            pltpu.VMEM((parts, keep * room, lanes), f32),
+            pltpu.VMEM((parts, room, keep, lanes), f32),
+            pltpu.SemaphoreType.DMA((parts,)),
+        ],
         compiler_params=params(4),
         name="settle",
     )(kept)

time: 37.5 us -> 37.5 us (level)
  no operation moved by 1% of the time
where the time goes in v11:
time: 37.5 us; the launch traced here: 37.2 us
  blocking collectives  20.6 us (55%)
  waiting for transfers between devices  5.84 us (16%)
  Pallas kernels  5.67 us (15%)
  starting transfers between devices  5.07 us (14%)
    all_to_all x1, blocking collectives, quick_body(): lax.all_to_all(blocks, ('half', 'part', 'grid'), 0, 0, axis_index_groups=...  11.3 us
    all_to_all x1, blocking collectives, quick_body(): lax.all_to_all(sent, ('part', 'grid'), 0, 0, axis_index_groups=[near])  9.25 us
    ppermute x6, waiting for transfers between devices, exchange(): lax.ppermute(value, 'grid', [(i, i ^ offset) for i in range(grid_count)])  5.84 us
    ppermute x6, starting transfers between devices, exchange(): lax.ppermute(value, 'grid', [(i, i ^ offset) for i in range(grid_count)])  5.07 us
    pallas_call x1, Pallas kernels, read_points(): pl.pallas_call(kernel, out_shape=[pltpu.VMEM((8, lanes), f32), pltpu.VMEM...  2.18 us
    pallas_call x1, Pallas kernels, potentials(): pl.pallas_call(kernel, out_shape=jax.ShapeDtypeStruct((parts * grid_count...  1.4 us
    pallas_call x1, Pallas kernels, settle(): pl.pallas_call(kernel, out_shape=jax.ShapeDtypeStruct((parts * part, keep...  0.81 us
  transfers between devices with their start and end apart: 6, of which 4 were waited for; matrix products, arithmetic and copies ran while one was open for 0% of the time, Pallas kernels for 0%

profile of v11, /device:TPU:0, one launch (start us, length us, event | category | flops | bytes accessed | tf_op | source)
XLA Modules:
  0.0 37.2 jit_solution(2399117255671209557)
XLA Ops:
  0.0 0.0 copy-start
  0.0 0.0 copy-start.1
  0.0 0.0 copy-start.2
  0.0 0.0 copy-start.3
  0.0 0.0 copy-start.4
  0.0 2.2 %read_points.1 = (f32[8,128]{1,0:T(8,128)S(1)}, f32[56,128]{1,0:T(8,128)S(1)}) custom-call(s32[4]{0:T(128)} %points_hbm.1, s32[16]{0:T(128)} %targets_hbm.1, f32[4,4]{1,0:T(4,128)} %fit_hbm.1, bf16[64,27648]{1,0:T(8,128)(2,1)} %orbitals_ref.5), custom_call_target="tpu_custom_call" | custom-call | tf_op jit(solution)/shard_map/read_points/pallas_call | solution.py:326
  2.2 2.5 %collective-permute-start.2 = (f32[8,128]{1,0:T(8,128)S(1)}, f32[8,128]{1,0:T(8,128)S(1)}, u32[]{:S(2)}, u32[]{:S(2)}) collective-permute-start(f32[8,128]{1,0:T(8,128)S(1)} %get-tuple-element.13.refs_0_), channel_id=1, source_target_pairs={{0,3},{1,2},{2,1},{3,0},{4,7},{5,6},{6,5},{7,4},{8,11},{9,10},{10,... | collective-permute-start | bytes 12296 | tf_op jit(solution)/shard_map/ppermute | solution.py:512
  4.7 0.6 %collective-permute-start.1 = (f32[8,128]{1,0:T(8,128)S(1)}, f32[8,128]{1,0:T(8,128)S(1)}, u32[]{:S(2)}, u32[]{:S(2)}) collective-permute-start(f32[8,128]{1,0:T(8,128)S(1)} %get-tuple-element.13.refs_0_), channel_id=1, source_target_pairs={{0,2},{1,3},{2,0},{3,1},{4,6},{5,7},{6,4},{7,5},{8,10},{9,11},{10,... | collective-permute-start | bytes 12296 | tf_op jit(solution)/shard_map/ppermute | solution.py:512
  5.3 0.0 collective-permute-start
  5.4 0.6 %collective-permute-done.2.refs_3_ = f32[8,128]{1,0:T(8,128)S(1)} collective-permute-done((f32[8,128]{1,0:T(8,128)S(1)}, f32[8,128]{1,0:T(8,128)S(1)}, u32[]{:S(2)}, u32[]{:S(2)}) %collective-permute-start.2) | collective-permute-done | bytes 4128 | tf_op jit(solution)/shard_map/ppermute | solution.py:512
  6.0 2.3 %collective-permute-done.1.refs_2_ = f32[8,128]{1,0:T(8,128)S(1)} collective-permute-done((f32[8,128]{1,0:T(8,128)S(1)}, f32[8,128]{1,0:T(8,128)S(1)}, u32[]{:S(2)}, u32[]{:S(2)}) %collective-permute-start.1) | collective-permute-done | bytes 4128 | tf_op jit(solution)/shard_map/ppermute | solution.py:512
  8.3 0.0 collective-permute-done.refs_1_
  8.3 0.0 copy-done
  8.3 0.7 %fit_pairs.1 = (bf16[216,128]{1,0:T(8,128)(2,1)S(1)}, bf16[216,128]{1,0:T(8,128)(2,1)S(1)}, bf16[216,128]{1,0:T(8,128)(2,1)S(1)}, bf16[216,128]{1,0:T(8,128)(2,1)S(1)}, f32[8,128]{1,0:T(8,128)S(1)}) custom-call(f32[56,128]{1,0:T(8,128)S(1)} %get-tuple-element.12.notes_ref, bf16[64,27648]{1,0:T(8,128)(2,1)S(1)} %copy-done, ...), custom_call_target="tpu_custom_call" | custom-call | tf_op jit(solution)/shard_map/fit_pairs/pallas_call | solution.py:378
  9.0 0.1 collective-permute-start.3
  9.1 1.1 %collective-permute-start.4 = (bf16[216,128]{1,0:T(8,128)(2,1)S(1)}, bf16[216,128]{1,0:T(8,128)(2,1)S(1)}, u32[]{:S(2)}, u32[]{:S(2)}) collective-permute-start(bf16[216,128]{1,0:T(8,128)(2,1)S(1)} %get-tuple-element.17), channel_id=1, source_target_pairs={{0,2},{1,3},{2,0},{3,1},{4,6},{5,7},{6,4},{7,5},{8,10},{9,11},{10,... | collective-permute-start | bytes 165896 | tf_op jit(solution)/shard_map/ppermute | solution.py:512
  10.2 0.7 %collective-permute-start.5 = (bf16[216,128]{1,0:T(8,128)(2,1)S(1)}, bf16[216,128]{1,0:T(8,128)(2,1)S(1)}, u32[]{:S(2)}, u32[]{:S(2)}) collective-permute-start(bf16[216,128]{1,0:T(8,128)(2,1)S(1)} %get-tuple-element.18), channel_id=1, source_target_pairs={{0,1},{1,0},{2,3},{3,2},{4,5},{5,4},{6,7},{7,6},{8,9},{9,8},{10,11... | collective-permute-start | bytes 165896 | tf_op jit(solution)/shard_map/ppermute | solution.py:512
  10.9 2.3 %collective-permute-done.3.refs_1_ = bf16[216,128]{1,0:T(8,128)(2,1)S(1)} collective-permute-done((bf16[216,128]{1,0:T(8,128)(2,1)S(1)}, bf16[216,128]{1,0:T(8,128)(2,1)S(1)}, u32[]{:S(2)}, u32[]{:S(2)}) %collective-permute-start.3) | collective-permute-done | bytes 55328 | tf_op jit(solution)/shard_map/ppermute | solution.py:512
  13.3 0.6 %collective-permute-done.4.refs_2_ = bf16[216,128]{1,0:T(8,128)(2,1)S(1)} collective-permute-done((bf16[216,128]{1,0:T(8,128)(2,1)S(1)}, bf16[216,128]{1,0:T(8,128)(2,1)S(1)}, u32[]{:S(2)}, u32[]{:S(2)}) %collective-permute-start.4) | collective-permute-done | bytes 55328 | tf_op jit(solution)/shard_map/ppermute | solution.py:512
  13.9 0.0 collective-permute-done.5.refs_3_
  13.9 0.0 copy-done.1
  13.9 0.0 copy-done.2
  13.9 0.0 copy-done.3
  13.9 0.0 copy-done.4
  13.9 1.4 %potentials.1 = bf16[16,56,128]{2,1,0:T(8,128)(2,1)S(1)} custom-call(f32[8,128]{1,0:T(8,128)S(1)} %get-tuple-element.14.at_ref, bf16[216,128]{1,0:T(8,128)(2,1)S(1)} %get-tuple-element.15.refs_0_, bf16[216,128]{1,0:T(8,128)(2,1)S(1)} %collective-permute-done.3.refs_1_, bf16[216,128]{1,0:T(8,128)(2,1)S(1)} %collective-permute-done.4.refs_2_, ...), custom_call_target="tpu_custom_call" | custom-call | tf_op jit(solution)/shard_map/potentials/pallas_call | solution.py:410
  15.3 9.2 %all_to_all.10.received_ref = bf16[16,56,128]{2,1,0:T(8,128)(2,1)S(1)} all-to-all(bf16[16,56,128]{2,1,0:T(8,128)(2,1)S(1)} %potentials.1), channel_id=1, replica_groups={{15,7,11,3,13,5,9,1,14,6,10,2,12,4,8,0},{31,23,27,19,29,21,25,17,30,22,..., dimensions={0} | all-to-all | bytes 458752 | tf_op jit(solution)/shard_map/all_to_all | solution.py:531
  24.5 0.6 %apply_part.1 = bf16[8,108,128]{2,1,0:T(8,128)(2,1)S(1)} custom-call(f32[56,128]{1,0:T(8,128)S(1)} %get-tuple-element.12.notes_ref, bf16[64,27648]{1,0:T(8,128)(2,1)S(1)} %copy-done, bf16[16,56,128]{2,1,0:T(8,128)(2,1)S(1)} %all_to_all.10.received_ref), custom_call_target="tpu_custom_call" | custom-call | tf_op jit(solution)/shard_map/apply_part/pallas_call | solution.py:450
  25.1 11.3 %all_to_all.11.kept_ref = bf16[8,108,128]{2,1,0:T(8,128)(2,1)S(1)} all-to-all(bf16[8,108,128]{2,1,0:T(8,128)(2,1)S(1)} %apply_part.1), channel_id=1, replica_groups={{20,16,24,28,12,8,0,4},{17,21,29,25,9,13,5,1},{22,18,26,30,14,10,2,6},{..., dimensions={0} | all-to-all | bytes 442368 | tf_op jit(solution)/shard_map/all_to_all | solution.py:533
  36.4 0.8 %settle.1 = f32[216,2,128]{2,1,0:T(2,128)} custom-call(bf16[8,108,128]{2,1,0:T(8,128)(2,1)S(1)} %all_to_all.11.kept_ref), custom_call_target="tpu_custom_call" | custom-call | tf_op jit(solution)/shard_map/settle/pallas_call | solution.py:485
Async XLA Ops:
  0.0 8.3 %copy-start = (bf16[64,27648]{1,0:T(8,128)(2,1)S(1)}, bf16[64,27648]{1,0:T(8,128)(2,1)}, u32[]{:S(2)}) copy-start(bf16[64,27648]{1,0:T(8,128)(2,1)} %orbitals_ref.5) | copy-start | bytes 10616836
  0.0 13.9 %copy-start.1 = (f32[24,48,128]{2,1,0:T(8,128)S(1)}, f32[24,48,128]{2,1,0:T(8,128)}, u32[]{:S(2)}) copy-start(f32[24,48,128]{2,1,0:T(8,128)} %constant.11.clone.refs_7_) | copy-start | bytes 1769476
  0.0 13.9 %copy-start.2 = (bf16[1024,256]{1,0:T(8,128)(2,1)S(1)}, bf16[1024,256]{1,0:T(8,128)(2,1)}, u32[]{:S(2)}) copy-start(bf16[1024,256]{1,0:T(8,128)(2,1)} %constant.10.clone.refs_6_) | copy-start | bytes 1572868
  0.0 13.9 %copy-start.3 = (bf16[1024,256]{1,0:T(8,128)(2,1)S(1)}, bf16[1024,256]{1,0:T(8,128)(2,1)}, u32[]{:S(2)}) copy-start(bf16[1024,256]{1,0:T(8,128)(2,1)} %constant.9.clone.refs_5_) | copy-start | bytes 1572868
  0.0 13.9 %copy-start.4 = (bf16[48,96]{1,0:T(8,128)(2,1)S(1)}, bf16[48,96]{1,0:T(8,128)(2,1)}, u32[]{:S(2)}) copy-start(bf16[48,96]{1,0:T(8,128)(2,1)} %constant.8.clone.refs_4_) | copy-start | bytes 27652
  2.2 3.8 %collective-permute-start.2 = (f32[8,128]{1,0:T(8,128)S(1)}, f32[8,128]{1,0:T(8,128)S(1)}, u32[]{:S(2)}, u32[]{:S(2)}) collective-permute-start(f32[8,128]{1,0:T(8,128)S(1)} %get-tuple-element.13.refs_0_), channel_id=1, source_target_pairs={{0,3},{1,2},{2,1},{3,0},{4,7},{5,6},{6,5},{7,4},{8,11},{9,10},{10,... | collective-permute-start | bytes 12296 | tf_op jit(solution)/shard_map/ppermute | solution.py:512
  4.7 3.6 %collective-permute-start.1 = (f32[8,128]{1,0:T(8,128)S(1)}, f32[8,128]{1,0:T(8,128)S(1)}, u32[]{:S(2)}, u32[]{:S(2)}) collective-permute-start(f32[8,128]{1,0:T(8,128)S(1)} %get-tuple-element.13.refs_0_), channel_id=1, source_target_pairs={{0,2},{1,3},{2,0},{3,1},{4,6},{5,7},{6,4},{7,5},{8,10},{9,11},{10,... | collective-permute-start | bytes 12296 | tf_op jit(solution)/shard_map/ppermute | solution.py:512
  5.3 3.0 %collective-permute-start = (f32[8,128]{1,0:T(8,128)S(1)}, f32[8,128]{1,0:T(8,128)S(1)}, u32[]{:S(2)}, u32[]{:S(2)}) collective-permute-start(f32[8,128]{1,0:T(8,128)S(1)} %get-tuple-element.13.refs_0_), channel_id=1, source_target_pairs={{0,1},{1,0},{2,3},{3,2},{4,5},{5,4},{6,7},{7,6},{8,9},{9,8},{10,11... | collective-permute-start | bytes 12296 | tf_op jit(solution)/shard_map/ppermute | solution.py:512
  9.0 4.2 %collective-permute-start.3 = (bf16[216,128]{1,0:T(8,128)(2,1)S(1)}, bf16[216,128]{1,0:T(8,128)(2,1)S(1)}, u32[]{:S(2)}, u32[]{:S(2)}) collective-permute-start(bf16[216,128]{1,0:T(8,128)(2,1)S(1)} %get-tuple-element.16), channel_id=1, source_target_pairs={{0,3},{1,2},{2,1},{3,0},{4,7},{5,6},{6,5},{7,4},{8,11},{9,10},{10,... | collective-permute-start | bytes 165896 | tf_op jit(solution)/shard_map/ppermute | solution.py:512
  9.1 4.8 %collective-permute-start.4 = (bf16[216,128]{1,0:T(8,128)(2,1)S(1)}, bf16[216,128]{1,0:T(8,128)(2,1)S(1)}, u32[]{:S(2)}, u32[]{:S(2)}) collective-permute-start(bf16[216,128]{1,0:T(8,128)(2,1)S(1)} %get-tuple-element.17), channel_id=1, source_target_pairs={{0,2},{1,3},{2,0},{3,1},{4,6},{5,7},{6,4},{7,5},{8,10},{9,11},{10,... | collective-permute-start | bytes 165896 | tf_op jit(solution)/shard_map/ppermute | solution.py:512
  10.2 3.6 %collective-permute-start.5 = (bf16[216,128]{1,0:T(8,128)(2,1)S(1)}, bf16[216,128]{1,0:T(8,128)(2,1)S(1)}, u32[]{:S(2)}, u32[]{:S(2)}) collective-permute-start(bf16[216,128]{1,0:T(8,128)(2,1)S(1)} %get-tuple-element.18), channel_id=1, source_target_pairs={{0,1},{1,0},{2,3},{3,2},{4,5},{5,4},{6,7},{7,6},{8,9},{9,8},{10,11... | collective-permute-start | bytes 165896 | tf_op jit(solution)/shard_map/ppermute | solution.py:512

commit v12 on v7

--- a/solution.py
+++ b/solution.py
@@ -385,7 +385,7 @@
         out_shape=[piece] * group + [jax.ShapeDtypeStruct((8, lanes), f32)],
         in_specs=[whole] * (2 + group),
         out_specs=[whole] * (group + 1),
-        scratch_shapes=[pltpu.VMEM((shard_rows * 8, lanes), f32)],
+        scratch_shapes=[pltpu.VMEM((shard_rows * 8 + 8, lanes), f32)],
         compiler_params=params(16),
         name="fit_pairs",
     )(notes, orbitals, *shares)
@@ -418,8 +418,8 @@
         in_specs=[whole] * (1 + grid_count + len(tables)),
         out_specs=whole,
         scratch_shapes=[
-            pltpu.VMEM((plan.rows + 8, lanes), f32),
-            pltpu.VMEM((plan.edge * plan.half, lanes), f32),
+            pltpu.VMEM((plan.rows + plan.plane_rows + sent, lanes), f32),
+            pltpu.VMEM((plan.edge * plan.half + plan.half, lanes), f32),
         ],
         compiler_params=params(24),
         name="potentials",
@@ -438,6 +438,7 @@
             spread[m * pitch:(m + 1) * pitch, :] = received_ref[m].astype(f32)
         at = spread[pl.ds(part, points, stride=pitch), :][:, :occupied].astype(bf16)
         first = pl.multiple_of(lax.axis_index("part") * (part * lanes), lanes)
+        swapped = lax.axis_index("grid") % 2 == 1
         density = jnp.dot(at, orbitals_ref[:, pl.ds(first, part * lanes)], preferred_element_type=f32)
         chosen = notes_ref[notes_ref.shape[0] - count:, :][:, :occupied].astype(bf16)
         target_points = lax.dot_general(chosen, at, contract_last, preferred_element_type=f32).astype(bf16)
@@ -449,7 +450,7 @@
         for s in range(slab_count):
             for k in range(keep):
                 stage[s, k * part:(k + 1) * part, :] = mid[pl.ds(s * keep + k, part, stride=count), :]
-            out_ref[place[s]] = stage[s].astype(bf16)
+            out_ref[jnp.where(swapped, place[s ^ 1], place[s])] = stage[s, :keep * part, :].astype(bf16)
 
     return pl.pallas_call(
         kernel,
@@ -457,9 +458,9 @@
         in_specs=[whole] * 3,
         out_specs=whole,
         scratch_shapes=[
-            pltpu.VMEM((points * pitch, lanes), f32),
-            pltpu.VMEM((part * count, lanes), f32),
-            pltpu.VMEM((slab_count, keep * part, lanes), f32),
+            pltpu.VMEM(((points + 1) * pitch, lanes), f32),
+            pltpu.VMEM((pitch * count + count, lanes), f32),
+            pltpu.VMEM((slab_count, keep * pitch, lanes), f32),
         ],
         compiler_params=params(16),
         name="apply_part",
@@ -471,21 +472,41 @@
     parts = slab_count // halves
     part = rows // keep
 
-    def kernel(kept_ref, out_ref, stage):
+    room = -(-part // 8) * 8
+
+    def kernel(kept_ref, out_ref, stage, rowed, sems):
+        swapped = lax.axis_index("grid") % 2 == 1
+        copies = []
         for q in range(parts):
-            stage[q] = sum(kept_ref[j].astype(f32) for j in range(slab_count) if order[j] % parts == q)
+            stage[q, :rows, :] = sum(kept_ref[j].astype(f32) for j in range(slab_count) if order[j] % parts == q)
             for k in range(keep):
-                out_ref[q * part:(q + 1) * part, k, :] = stage[q, k * part:(k + 1) * part, :]
+                rowed[q, :part, k, :] = stage[q, k * part:(k + 1) * part, :]
+            first = jnp.where(swapped, q ^ 1, q) * part
+            copies.append(pltpu.make_async_copy(rowed.at[q, pl.ds(0, part)], out_ref.at[pl.ds(first, part)], sems.at[q]))
+            copies[-1].start()
+        for copy in copies:
+            copy.wait()
 
     return pl.pallas_call(
         kernel,
         out_shape=jax.ShapeDtypeStruct((parts * part, keep, lanes), f32),
         in_specs=[whole],
-        out_specs=whole,
-        scratch_shapes=[pltpu.VMEM((parts, rows, lanes), f32)],
+        out_specs=far,
+        scratch_shapes=[
+            pltpu.VMEM((parts, keep * room, lanes), f32),
+            pltpu.VMEM((parts, room, keep, lanes), f32),
+            pltpu.SemaphoreType.DMA((parts,)),
+        ],
         compiler_params=params(4),
         name="settle",
     )(kept)
+
+
+def bits_reversed(count):
+    order = [0]
+    while len(order) < count:
+        order = [2 * i for i in order] + [2 * i + 1 for i in order]
+    return order
 
 
 def places(order):
@@ -508,12 +529,13 @@
     *pieces, at = fit_pairs(orbitals, notes, shares)
     offsets = [0] + list(reversed(range(1, grid_count)))
     pieces = [exchange(pieces[d], grid_count, d) if d else pieces[d] for d in offsets]
-    near = list(reversed(range(part_count * grid_count)))
-    far = [s ^ (s >> 1) for s in reversed(range(slab_count))]
+    near = bits_reversed(part_count * grid_count)[::-1]
+    far = [s ^ (s >> 1) ^ 1 for s in reversed(range(slab_count))]
+    far_groups = [[(s ^ g % 2) * grid_count + g for s in far] for g in range(grid_count)]
     sent = potentials(plan, pieces, offsets, at, part_count, places(near))
     received = lax.all_to_all(sent, ("part", "grid"), 0, 0, axis_index_groups=[near])
     blocks = apply_part(orbitals, notes, received, part, count, places(far), halves)
-    kept = lax.all_to_all(blocks, ("half", "part"), 0, 0, axis_index_groups=[far])
+    kept = lax.all_to_all(blocks, ("half", "part", "grid"), 0, 0, axis_index_groups=far_groups)
     return jnp.transpose(settle(kept, keep, halves, far), (1, 0, 2)).reshape(keep, shard_len)
 
 
@@ -532,7 +554,8 @@
         and edge <= lanes // 2
         and cells % (grid_count * lanes) == 0
         and shard_rows % 8 == 0
-        and slab_count % 2 == 0
+        and slab_count > 2
+        and (slab_count * grid_count).bit_count() == 1
         and shard_rows % (slab_count // 2) == 0
         and targets.shape[0] % slab_count == 0
         and targets.shape[0] % 8 == 0

time: 38.5 us -> 37.8 us (0.982)
  blocking collectives: 21.3 us -> 20.6 us
    all_to_all x1, blocking collectives: 11.8 us -> 11.3 us  [quick_body(): lax.all_to_all(blocks, ('half', 'part', 'grid'), 0, 0, axis_index_groups=...]
where the time goes in v12:
time: 37.8 us; the launch traced here: 37.6 us
  blocking collectives  20.6 us (54%)
  Pallas kernels  5.96 us (16%)
  waiting for transfers between devices  5.84 us (15%)
  starting transfers between devices  5.07 us (13%)
    all_to_all x1, blocking collectives, quick_body(): lax.all_to_all(blocks, ('half', 'part', 'grid'), 0, 0, axis_index_groups=...  11.3 us
    all_to_all x1, blocking collectives, quick_body(): lax.all_to_all(sent, ('part', 'grid'), 0, 0, axis_index_groups=[near])  9.24 us
    ppermute x6, waiting for transfers between devices, exchange(): lax.ppermute(value, 'grid', [(i, i ^ offset) for i in range(grid_count)])  5.84 us
    ppermute x6, starting transfers between devices, exchange(): lax.ppermute(value, 'grid', [(i, i ^ offset) for i in range(grid_count)])  5.07 us
    pallas_call x1, Pallas kernels, read_points(): pl.pallas_call(kernel, out_shape=[pltpu.VMEM((8, lanes), f32), pltpu.VMEM...  2.17 us
    pallas_call x1, Pallas kernels, potentials(): pl.pallas_call(kernel, out_shape=jax.ShapeDtypeStruct((parts * grid_count...  1.68 us
    pallas_call x1, Pallas kernels, settle(): pl.pallas_call(kernel, out_shape=jax.ShapeDtypeStruct((parts * part, keep...  0.81 us
  transfers between devices with their start and end apart: 6, of which 4 were waited for; matrix products, arithmetic and copies ran while one was open for 0% of the time, Pallas kernels for 0%

profile of v12, /device:TPU:0, one launch (start us, length us, event | category | flops | bytes accessed | tf_op | source)
XLA Modules:
  0.0 37.6 jit_solution(10380035486187814382)
XLA Ops:
  0.0 0.0 copy-start
  0.0 0.0 copy-start.1
  0.0 0.0 copy-start.2
  0.0 0.0 copy-start.3
  0.0 0.0 copy-start.4
  0.0 0.0 copy-start.5
  0.0 0.0 copy-start.6
  0.0 2.2 %read_points.1 = (f32[8,128]{1,0:T(8,128)S(1)}, f32[56,128]{1,0:T(8,128)S(1)}) custom-call(s32[4]{0:T(128)} %points_hbm.1, s32[16]{0:T(128)} %targets_hbm.1, f32[4,4]{1,0:T(4,128)} %fit_hbm.1, bf16[64,27648]{1,0:T(8,128)(2,1)} %orbitals_ref.5), custom_call_target="tpu_custom_call" | custom-call | tf_op jit(solution)/shard_map/read_points/pallas_call | solution.py:331
  2.2 2.5 %collective-permute-start.2 = (f32[8,128]{1,0:T(8,128)S(1)}, f32[8,128]{1,0:T(8,128)S(1)}, u32[]{:S(2)}, u32[]{:S(2)}) collective-permute-start(f32[8,128]{1,0:T(8,128)S(1)} %get-tuple-element.13.refs_0_), channel_id=1, source_target_pairs={{0,3},{1,2},{2,1},{3,0},{4,7},{5,6},{6,5},{7,4},{8,11},{9,10},{10,... | collective-permute-start | bytes 12296 | tf_op jit(solution)/shard_map/ppermute | solution.py:517
  4.7 0.6 %collective-permute-start.1 = (f32[8,128]{1,0:T(8,128)S(1)}, f32[8,128]{1,0:T(8,128)S(1)}, u32[]{:S(2)}, u32[]{:S(2)}) collective-permute-start(f32[8,128]{1,0:T(8,128)S(1)} %get-tuple-element.13.refs_0_), channel_id=1, source_target_pairs={{0,2},{1,3},{2,0},{3,1},{4,6},{5,7},{6,4},{7,5},{8,10},{9,11},{10,... | collective-permute-start | bytes 12296 | tf_op jit(solution)/shard_map/ppermute | solution.py:517
  5.3 0.0 collective-permute-start
  5.4 0.6 %collective-permute-done.2.refs_3_ = f32[8,128]{1,0:T(8,128)S(1)} collective-permute-done((f32[8,128]{1,0:T(8,128)S(1)}, f32[8,128]{1,0:T(8,128)S(1)}, u32[]{:S(2)}, u32[]{:S(2)}) %collective-permute-start.2) | collective-permute-done | bytes 4128 | tf_op jit(solution)/shard_map/ppermute | solution.py:517
  6.0 2.3 %collective-permute-done.1.refs_2_ = f32[8,128]{1,0:T(8,128)S(1)} collective-permute-done((f32[8,128]{1,0:T(8,128)S(1)}, f32[8,128]{1,0:T(8,128)S(1)}, u32[]{:S(2)}, u32[]{:S(2)}) %collective-permute-start.1) | collective-permute-done | bytes 4128 | tf_op jit(solution)/shard_map/ppermute | solution.py:517
  8.3 0.0 collective-permute-done.refs_1_
  8.3 0.0 copy-done
  8.3 0.7 %fit_pairs.1 = (bf16[216,128]{1,0:T(8,128)(2,1)S(1)}, bf16[216,128]{1,0:T(8,128)(2,1)S(1)}, bf16[216,128]{1,0:T(8,128)(2,1)S(1)}, bf16[216,128]{1,0:T(8,128)(2,1)S(1)}, f32[8,128]{1,0:T(8,128)S(1)}) custom-call(f32[56,128]{1,0:T(8,128)S(1)} %get-tuple-element.12.notes_ref, bf16[64,27648]{1,0:T(8,128)(2,1)S(1)} %copy-done, ...), custom_call_target="tpu_custom_call" | custom-call | tf_op jit(solution)/shard_map/fit_pairs/pallas_call | solution.py:383
  9.1 0.1 collective-permute-start.3
  9.1 1.1 %collective-permute-start.4 = (bf16[216,128]{1,0:T(8,128)(2,1)S(1)}, bf16[216,128]{1,0:T(8,128)(2,1)S(1)}, u32[]{:S(2)}, u32[]{:S(2)}) collective-permute-start(bf16[216,128]{1,0:T(8,128)(2,1)S(1)} %get-tuple-element.17), channel_id=1, source_target_pairs={{0,2},{1,3},{2,0},{3,1},{4,6},{5,7},{6,4},{7,5},{8,10},{9,11},{10,... | collective-permute-start | bytes 165896 | tf_op jit(solution)/shard_map/ppermute | solution.py:517
  10.3 0.7 %collective-permute-start.5 = (bf16[216,128]{1,0:T(8,128)(2,1)S(1)}, bf16[216,128]{1,0:T(8,128)(2,1)S(1)}, u32[]{:S(2)}, u32[]{:S(2)}) collective-permute-start(bf16[216,128]{1,0:T(8,128)(2,1)S(1)} %get-tuple-element.18), channel_id=1, source_target_pairs={{0,1},{1,0},{2,3},{3,2},{4,5},{5,4},{6,7},{7,6},{8,9},{9,8},{10,11... | collective-permute-start | bytes 165896 | tf_op jit(solution)/shard_map/ppermute | solution.py:517
  11.0 2.3 %collective-permute-done.3.refs_1_ = bf16[216,128]{1,0:T(8,128)(2,1)S(1)} collective-permute-done((bf16[216,128]{1,0:T(8,128)(2,1)S(1)}, bf16[216,128]{1,0:T(8,128)(2,1)S(1)}, u32[]{:S(2)}, u32[]{:S(2)}) %collective-permute-start.3) | collective-permute-done | bytes 55328 | tf_op jit(solution)/shard_map/ppermute | solution.py:517
  13.3 0.6 %collective-permute-done.4.refs_2_ = bf16[216,128]{1,0:T(8,128)(2,1)S(1)} collective-permute-done((bf16[216,128]{1,0:T(8,128)(2,1)S(1)}, bf16[216,128]{1,0:T(8,128)(2,1)S(1)}, u32[]{:S(2)}, u32[]{:S(2)}) %collective-permute-start.4) | collective-permute-done | bytes 55328 | tf_op jit(solution)/shard_map/ppermute | solution.py:517
  13.9 0.0 collective-permute-done.5.refs_3_
  13.9 0.0 copy-done.1
  13.9 0.0 copy-done.2
  13.9 0.0 copy-done.3
  13.9 0.0 copy-done.4
  13.9 0.0 copy-done.5
  13.9 0.0 copy-done.6
  13.9 1.7 %potentials.1 = bf16[16,56,128]{2,1,0:T(8,128)(2,1)S(1)} custom-call(f32[8,128]{1,0:T(8,128)S(1)} %get-tuple-element.14.at_ref, bf16[216,128]{1,0:T(8,128)(2,1)S(1)} %get-tuple-element.15.refs_0_, bf16[216,128]{1,0:T(8,128)(2,1)S(1)} %collective-permute-done.3.refs_1_, bf16[216,128]{1,0:T(8,128)(2,1)S(1)} %collective-permute-done.4.refs_2_, ...), custom_call_target="tpu_custom_call" | custom-call | tf_op jit(solution)/shard_map/potentials/pallas_call | solution.py:415
  15.6 9.2 %all_to_all.10.received_ref = bf16[16,56,128]{2,1,0:T(8,128)(2,1)S(1)} all-to-all(bf16[16,56,128]{2,1,0:T(8,128)(2,1)S(1)} %potentials.1), channel_id=1, replica_groups={{15,7,11,3,13,5,9,1,14,6,10,2,12,4,8,0},{31,23,27,19,29,21,25,17,30,22,..., dimensions={0} | all-to-all | bytes 458752 | tf_op jit(solution)/shard_map/all_to_all | solution.py:536
  24.9 0.6 %apply_part.1 = bf16[8,108,128]{2,1,0:T(8,128)(2,1)S(1)} custom-call(f32[56,128]{1,0:T(8,128)S(1)} %get-tuple-element.12.notes_ref, bf16[64,27648]{1,0:T(8,128)(2,1)S(1)} %copy-done, bf16[16,56,128]{2,1,0:T(8,128)(2,1)S(1)} %all_to_all.10.received_ref), custom_call_target="tpu_custom_call" | custom-call | tf_op jit(solution)/shard_map/apply_part/pallas_call | solution.py:455
  25.4 11.3 %all_to_all.11.kept_ref = bf16[8,108,128]{2,1,0:T(8,128)(2,1)S(1)} all-to-all(bf16[8,108,128]{2,1,0:T(8,128)(2,1)S(1)} %apply_part.1), channel_id=1, replica_groups={{20,16,24,28,12,8,0,4},{17,21,29,25,9,13,5,1},{22,18,26,30,14,10,2,6},{..., dimensions={0} | all-to-all | bytes 442368 | tf_op jit(solution)/shard_map/all_to_all | solution.py:538
  36.8 0.8 %settle.1 = f32[216,2,128]{2,1,0:T(2,128)} custom-call(bf16[8,108,128]{2,1,0:T(8,128)(2,1)S(1)} %all_to_all.11.kept_ref), custom_call_target="tpu_custom_call" | custom-call | tf_op jit(solution)/shard_map/settle/pallas_call | solution.py:490
Async XLA Ops:
  0.0 8.3 %copy-start = (bf16[64,27648]{1,0:T(8,128)(2,1)S(1)}, bf16[64,27648]{1,0:T(8,128)(2,1)}, u32[]{:S(2)}) copy-start(bf16[64,27648]{1,0:T(8,128)(2,1)} %orbitals_ref.5) | copy-start | bytes 10616836
  0.0 13.9 %copy-start.1 = (f32[24,48,128]{2,1,0:T(8,128)S(1)}, f32[24,48,128]{2,1,0:T(8,128)}, u32[]{:S(2)}) copy-start(f32[24,48,128]{2,1,0:T(8,128)} %constant.17.clone.refs_9_) | copy-start | bytes 1769476
  0.0 13.9 %copy-start.2 = (bf16[1024,256]{1,0:T(8,128)(2,1)S(1)}, bf16[1024,256]{1,0:T(8,128)(2,1)}, u32[]{:S(2)}) copy-start(bf16[1024,256]{1,0:T(8,128)(2,1)} %constant.16.clone.refs_8_) | copy-start | bytes 1572868
  0.0 13.9 %copy-start.3 = (bf16[1024,256]{1,0:T(8,128)(2,1)S(1)}, bf16[1024,256]{1,0:T(8,128)(2,1)}, u32[]{:S(2)}) copy-start(bf16[1024,256]{1,0:T(8,128)(2,1)} %constant.15.clone.refs_7_) | copy-start | bytes 1572868
  0.0 13.9 %copy-start.4 = (bf16[1024,256]{1,0:T(8,128)(2,1)S(1)}, bf16[1024,256]{1,0:T(8,128)(2,1)}, u32[]{:S(2)}) copy-start(bf16[1024,256]{1,0:T(8,128)(2,1)} %constant.14.clone.refs_6_) | copy-start | bytes 1572868
  0.0 13.9 %copy-start.5 = (bf16[1024,256]{1,0:T(8,128)(2,1)S(1)}, bf16[1024,256]{1,0:T(8,128)(2,1)}, u32[]{:S(2)}) copy-start(bf16[1024,256]{1,0:T(8,128)(2,1)} %constant.13.clone.refs_5_) | copy-start | bytes 1572868
  0.0 13.9 %copy-start.6 = (bf16[48,144]{1,0:T(8,128)(2,1)S(1)}, bf16[48,144]{1,0:T(8,128)(2,1)}, u32[]{:S(2)}) copy-start(bf16[48,144]{1,0:T(8,128)(2,1)} %constant.12.clone.refs_4_) | copy-start | bytes 41476
  2.2 3.8 %collective-permute-start.2 = (f32[8,128]{1,0:T(8,128)S(1)}, f32[8,128]{1,0:T(8,128)S(1)}, u32[]{:S(2)}, u32[]{:S(2)}) collective-permute-start(f32[8,128]{1,0:T(8,128)S(1)} %get-tuple-element.13.refs_0_), channel_id=1, source_target_pairs={{0,3},{1,2},{2,1},{3,0},{4,7},{5,6},{6,5},{7,4},{8,11},{9,10},{10,... | collective-permute-start | bytes 12296 | tf_op jit(solution)/shard_map/ppermute | solution.py:517
  4.7 3.6 %collective-permute-start.1 = (f32[8,128]{1,0:T(8,128)S(1)}, f32[8,128]{1,0:T(8,128)S(1)}, u32[]{:S(2)}, u32[]{:S(2)}) collective-permute-start(f32[8,128]{1,0:T(8,128)S(1)} %get-tuple-element.13.refs_0_), channel_id=1, source_target_pairs={{0,2},{1,3},{2,0},{3,1},{4,6},{5,7},{6,4},{7,5},{8,10},{9,11},{10,... | collective-permute-start | bytes 12296 | tf_op jit(solution)/shard_map/ppermute | solution.py:517
  5.3 3.0 %collective-permute-start = (f32[8,128]{1,0:T(8,128)S(1)}, f32[8,128]{1,0:T(8,128)S(1)}, u32[]{:S(2)}, u32[]{:S(2)}) collective-permute-start(f32[8,128]{1,0:T(8,128)S(1)} %get-tuple-element.13.refs_0_), channel_id=1, source_target_pairs={{0,1},{1,0},{2,3},{3,2},{4,5},{5,4},{6,7},{7,6},{8,9},{9,8},{10,11... | collective-permute-start | bytes 12296 | tf_op jit(solution)/shard_map/ppermute | solution.py:517
  9.1 4.2 %collective-permute-start.3 = (bf16[216,128]{1,0:T(8,128)(2,1)S(1)}, bf16[216,128]{1,0:T(8,128)(2,1)S(1)}, u32[]{:S(2)}, u32[]{:S(2)}) collective-permute-start(bf16[216,128]{1,0:T(8,128)(2,1)S(1)} %get-tuple-element.16), channel_id=1, source_target_pairs={{0,3},{1,2},{2,1},{3,0},{4,7},{5,6},{6,5},{7,4},{8,11},{9,10},{10,... | collective-permute-start | bytes 165896 | tf_op jit(solution)/shard_map/ppermute | solution.py:517
  9.1 4.8 %collective-permute-start.4 = (bf16[216,128]{1,0:T(8,128)(2,1)S(1)}, bf16[216,128]{1,0:T(8,128)(2,1)S(1)}, u32[]{:S(2)}, u32[]{:S(2)}) collective-permute-start(bf16[216,128]{1,0:T(8,128)(2,1)S(1)} %get-tuple-element.17), channel_id=1, source_target_pairs={{0,2},{1,3},{2,0},{3,1},{4,6},{5,7},{6,4},{7,5},{8,10},{9,11},{10,... | collective-permute-start | bytes 165896 | tf_op jit(solution)/shard_map/ppermute | solution.py:517
  10.3 3.6 %collective-permute-start.5 = (bf16[216,128]{1,0:T(8,128)(2,1)S(1)}, bf16[216,128]{1,0:T(8,128)(2,1)S(1)}, u32[]{:S(2)}, u32[]{:S(2)}) collective-permute-start(bf16[216,128]{1,0:T(8,128)(2,1)S(1)} %get-tuple-element.18), channel_id=1, source_target_pairs={{0,1},{1,0},{2,3},{3,2},{4,5},{5,4},{6,7},{7,6},{8,9},{9,8},{10,11... | collective-permute-start | bytes 165896 | tf_op jit(solution)/shard_map/ppermute | solution.py:517

commit v13 on v11

--- a/solution.py
+++ b/solution.py
@@ -522,7 +522,7 @@
     share, notes = read_points(orbitals, targets, points, fit)
     shares = [share] + [exchange(share, grid_count, d) for d in range(1, grid_count)]
     *pieces, at = fit_pairs(orbitals, notes, shares)
-    offsets = [0] + list(reversed(range(1, grid_count)))
+    offsets = [0, grid_count - 1, *range(1, grid_count - 1)]
     pieces = [exchange(pieces[d], grid_count, d) if d else pieces[d] for d in offsets]
     near = bits_reversed(part_count * grid_count)[::-1]
     far = [s ^ (s >> 1) ^ 1 for s in reversed(range(slab_count))]

time: 37.5 us -> 37.3 us (level)
  blocking collectives: 20.6 us -> 20.1 us
    all_to_all x1, blocking collectives: 9.25 us -> 8.53 us  [quick_body(): lax.all_to_all(sent, ('part', 'grid'), 0, 0, axis_index_groups=[near])]
where the time goes in v13:
time: 37.3 us; the launch traced here: 37 us
  blocking collectives  20.1 us (54%)
  waiting for transfers between devices  5.85 us (16%)
  Pallas kernels  5.67 us (15%)
  starting transfers between devices  5.35 us (14%)
    all_to_all x1, blocking collectives, quick_body(): lax.all_to_all(blocks, ('half', 'part', 'grid'), 0, 0, axis_index_groups=...  11.6 us
    all_to_all x1, blocking collectives, quick_body(): lax.all_to_all(sent, ('part', 'grid'), 0, 0, axis_index_groups=[near])  8.53 us
    ppermute x6, waiting for transfers between devices, exchange(): lax.ppermute(value, 'grid', [(i, i ^ offset) for i in range(grid_count)])  5.85 us
    ppermute x6, starting transfers between devices, exchange(): lax.ppermute(value, 'grid', [(i, i ^ offset) for i in range(grid_count)])  5.35 us
    pallas_call x1, Pallas kernels, read_points(): pl.pallas_call(kernel, out_shape=[pltpu.VMEM((8, lanes), f32), pltpu.VMEM...  2.18 us
    pallas_call x1, Pallas kernels, potentials(): pl.pallas_call(kernel, out_shape=jax.ShapeDtypeStruct((parts * grid_count...  1.4 us
    pallas_call x1, Pallas kernels, settle(): pl.pallas_call(kernel, out_shape=jax.ShapeDtypeStruct((parts * part, keep...  0.81 us
  transfers between devices with their start and end apart: 6, of which 4 were waited for; matrix products, arithmetic and copies ran while one was open for 0% of the time, Pallas kernels for 0%

profile of v13, /device:TPU:0, one launch (start us, length us, event | category | flops | bytes accessed | tf_op | source)
XLA Modules:
  0.0 37.0 jit_solution(1445398124931679246)
XLA Ops:
  0.0 0.0 copy-start
  0.0 0.0 copy-start.1
  0.0 0.0 copy-start.2
  0.0 0.0 copy-start.3
  0.0 0.0 copy-start.4
  0.0 2.2 %read_points.1 = (f32[8,128]{1,0:T(8,128)S(1)}, f32[56,128]{1,0:T(8,128)S(1)}) custom-call(s32[4]{0:T(128)} %points_hbm.1, s32[16]{0:T(128)} %targets_hbm.1, f32[4,4]{1,0:T(4,128)} %fit_hbm.1, bf16[64,27648]{1,0:T(8,128)(2,1)} %orbitals_ref.5), custom_call_target="tpu_custom_call" | custom-call | tf_op jit(solution)/shard_map/read_points/pallas_call | solution.py:326
  2.2 2.5 %collective-permute-start.2 = (f32[8,128]{1,0:T(8,128)S(1)}, f32[8,128]{1,0:T(8,128)S(1)}, u32[]{:S(2)}, u32[]{:S(2)}) collective-permute-start(f32[8,128]{1,0:T(8,128)S(1)} %get-tuple-element.13.refs_0_), channel_id=1, source_target_pairs={{0,3},{1,2},{2,1},{3,0},{4,7},{5,6},{6,5},{7,4},{8,11},{9,10},{10,... | collective-permute-start | bytes 12296 | tf_op jit(solution)/shard_map/ppermute | solution.py:512
  4.7 0.6 %collective-permute-start.1 = (f32[8,128]{1,0:T(8,128)S(1)}, f32[8,128]{1,0:T(8,128)S(1)}, u32[]{:S(2)}, u32[]{:S(2)}) collective-permute-start(f32[8,128]{1,0:T(8,128)S(1)} %get-tuple-element.13.refs_0_), channel_id=1, source_target_pairs={{0,2},{1,3},{2,0},{3,1},{4,6},{5,7},{6,4},{7,5},{8,10},{9,11},{10,... | collective-permute-start | bytes 12296 | tf_op jit(solution)/shard_map/ppermute | solution.py:512
  5.3 0.0 collective-permute-start
  5.4 0.6 %collective-permute-done.2.refs_3_ = f32[8,128]{1,0:T(8,128)S(1)} collective-permute-done((f32[8,128]{1,0:T(8,128)S(1)}, f32[8,128]{1,0:T(8,128)S(1)}, u32[]{:S(2)}, u32[]{:S(2)}) %collective-permute-start.2) | collective-permute-done | bytes 4128 | tf_op jit(solution)/shard_map/ppermute | solution.py:512
  6.0 2.3 %collective-permute-done.1.refs_2_ = f32[8,128]{1,0:T(8,128)S(1)} collective-permute-done((f32[8,128]{1,0:T(8,128)S(1)}, f32[8,128]{1,0:T(8,128)S(1)}, u32[]{:S(2)}, u32[]{:S(2)}) %collective-permute-start.1) | collective-permute-done | bytes 4128 | tf_op jit(solution)/shard_map/ppermute | solution.py:512
  8.3 0.0 collective-permute-done.refs_1_
  8.3 0.0 copy-done
  8.3 0.7 %fit_pairs.1 = (bf16[216,128]{1,0:T(8,128)(2,1)S(1)}, bf16[216,128]{1,0:T(8,128)(2,1)S(1)}, bf16[216,128]{1,0:T(8,128)(2,1)S(1)}, bf16[216,128]{1,0:T(8,128)(2,1)S(1)}, f32[8,128]{1,0:T(8,128)S(1)}) custom-call(f32[56,128]{1,0:T(8,128)S(1)} %get-tuple-element.12.notes_ref, bf16[64,27648]{1,0:T(8,128)(2,1)S(1)} %copy-done, ...), custom_call_target="tpu_custom_call" | custom-call | tf_op jit(solution)/shard_map/fit_pairs/pallas_call | solution.py:378
  9.0 0.1 collective-permute-start.3
  9.1 0.7 %collective-permute-start.4 = (bf16[216,128]{1,0:T(8,128)(2,1)S(1)}, bf16[216,128]{1,0:T(8,128)(2,1)S(1)}, u32[]{:S(2)}, u32[]{:S(2)}) collective-permute-start(bf16[216,128]{1,0:T(8,128)(2,1)S(1)} %get-tuple-element.17), channel_id=1, source_target_pairs={{0,1},{1,0},{2,3},{3,2},{4,5},{5,4},{6,7},{7,6},{8,9},{9,8},{10,11... | collective-permute-start | bytes 165896 | tf_op jit(solution)/shard_map/ppermute | solution.py:512
  9.8 1.4 %collective-permute-start.5 = (bf16[216,128]{1,0:T(8,128)(2,1)S(1)}, bf16[216,128]{1,0:T(8,128)(2,1)S(1)}, u32[]{:S(2)}, u32[]{:S(2)}) collective-permute-start(bf16[216,128]{1,0:T(8,128)(2,1)S(1)} %get-tuple-element.18), channel_id=1, source_target_pairs={{0,2},{1,3},{2,0},{3,1},{4,6},{5,7},{6,4},{7,5},{8,10},{9,11},{10,... | collective-permute-start | bytes 165896 | tf_op jit(solution)/shard_map/ppermute | solution.py:512
  11.2 1.7 %collective-permute-done.3.refs_1_ = bf16[216,128]{1,0:T(8,128)(2,1)S(1)} collective-permute-done((bf16[216,128]{1,0:T(8,128)(2,1)S(1)}, bf16[216,128]{1,0:T(8,128)(2,1)S(1)}, u32[]{:S(2)}, u32[]{:S(2)}) %collective-permute-start.3) | collective-permute-done | bytes 55328 | tf_op jit(solution)/shard_map/ppermute | solution.py:512
  13.0 0.0 collective-permute-done.4.refs_2_
  13.0 1.2 %collective-permute-done.5.refs_3_ = bf16[216,128]{1,0:T(8,128)(2,1)S(1)} collective-permute-done((bf16[216,128]{1,0:T(8,128)(2,1)S(1)}, bf16[216,128]{1,0:T(8,128)(2,1)S(1)}, u32[]{:S(2)}, u32[]{:S(2)}) %collective-permute-start.5) | collective-permute-done | bytes 55328 | tf_op jit(solution)/shard_map/ppermute | solution.py:512
  14.2 0.0 copy-done.1
  14.2 0.0 copy-done.2
  14.2 0.0 copy-done.3
  14.2 0.0 copy-done.4
  14.2 1.4 %potentials.1 = bf16[16,56,128]{2,1,0:T(8,128)(2,1)S(1)} custom-call(f32[8,128]{1,0:T(8,128)S(1)} %get-tuple-element.14.at_ref, bf16[216,128]{1,0:T(8,128)(2,1)S(1)} %get-tuple-element.15.refs_0_, bf16[216,128]{1,0:T(8,128)(2,1)S(1)} %collective-permute-done.3.refs_1_, bf16[216,128]{1,0:T(8,128)(2,1)S(1)} %collective-permute-done.4.refs_2_, ...), custom_call_target="tpu_custom_call" | custom-call | tf_op jit(solution)/shard_map/potentials/pallas_call | solution.py:410
  15.6 8.5 %all_to_all.10.received_ref = bf16[16,56,128]{2,1,0:T(8,128)(2,1)S(1)} all-to-all(bf16[16,56,128]{2,1,0:T(8,128)(2,1)S(1)} %potentials.1), channel_id=1, replica_groups={{15,7,11,3,13,5,9,1,14,6,10,2,12,4,8,0},{31,23,27,19,29,21,25,17,30,22,..., dimensions={0} | all-to-all | bytes 458752 | tf_op jit(solution)/shard_map/all_to_all | solution.py:531
  24.1 0.6 %apply_part.1 = bf16[8,108,128]{2,1,0:T(8,128)(2,1)S(1)} custom-call(f32[56,128]{1,0:T(8,128)S(1)} %get-tuple-element.12.notes_ref, bf16[64,27648]{1,0:T(8,128)(2,1)S(1)} %copy-done, bf16[16,56,128]{2,1,0:T(8,128)(2,1)S(1)} %all_to_all.10.received_ref), custom_call_target="tpu_custom_call" | custom-call | tf_op jit(solution)/shard_map/apply_part/pallas_call | solution.py:450
  24.7 11.6 %all_to_all.11.kept_ref = bf16[8,108,128]{2,1,0:T(8,128)(2,1)S(1)} all-to-all(bf16[8,108,128]{2,1,0:T(8,128)(2,1)S(1)} %apply_part.1), channel_id=1, replica_groups={{20,16,24,28,12,8,0,4},{17,21,29,25,9,13,5,1},{22,18,26,30,14,10,2,6},{..., dimensions={0} | all-to-all | bytes 442368 | tf_op jit(solution)/shard_map/all_to_all | solution.py:533
  36.2 0.8 %settle.1 = f32[216,2,128]{2,1,0:T(2,128)} custom-call(bf16[8,108,128]{2,1,0:T(8,128)(2,1)S(1)} %all_to_all.11.kept_ref), custom_call_target="tpu_custom_call" | custom-call | tf_op jit(solution)/shard_map/settle/pallas_call | solution.py:485
Async XLA Ops:
  0.0 8.3 %copy-start = (bf16[64,27648]{1,0:T(8,128)(2,1)S(1)}, bf16[64,27648]{1,0:T(8,128)(2,1)}, u32[]{:S(2)}) copy-start(bf16[64,27648]{1,0:T(8,128)(2,1)} %orbitals_ref.5) | copy-start | bytes 10616836
  0.0 14.2 %copy-start.1 = (f32[24,48,128]{2,1,0:T(8,128)S(1)}, f32[24,48,128]{2,1,0:T(8,128)}, u32[]{:S(2)}) copy-start(f32[24,48,128]{2,1,0:T(8,128)} %constant.11.clone.refs_7_) | copy-start | bytes 1769476
  0.0 14.2 %copy-start.2 = (bf16[1024,256]{1,0:T(8,128)(2,1)S(1)}, bf16[1024,256]{1,0:T(8,128)(2,1)}, u32[]{:S(2)}) copy-start(bf16[1024,256]{1,0:T(8,128)(2,1)} %constant.10.clone.refs_6_) | copy-start | bytes 1572868
  0.0 14.2 %copy-start.3 = (bf16[1024,256]{1,0:T(8,128)(2,1)S(1)}, bf16[1024,256]{1,0:T(8,128)(2,1)}, u32[]{:S(2)}) copy-start(bf16[1024,256]{1,0:T(8,128)(2,1)} %constant.9.clone.refs_5_) | copy-start | bytes 1572868
  0.0 14.2 %copy-start.4 = (bf16[48,96]{1,0:T(8,128)(2,1)S(1)}, bf16[48,96]{1,0:T(8,128)(2,1)}, u32[]{:S(2)}) copy-start(bf16[48,96]{1,0:T(8,128)(2,1)} %constant.8.clone.refs_4_) | copy-start | bytes 27652
  2.2 3.8 %collective-permute-start.2 = (f32[8,128]{1,0:T(8,128)S(1)}, f32[8,128]{1,0:T(8,128)S(1)}, u32[]{:S(2)}, u32[]{:S(2)}) collective-permute-start(f32[8,128]{1,0:T(8,128)S(1)} %get-tuple-element.13.refs_0_), channel_id=1, source_target_pairs={{0,3},{1,2},{2,1},{3,0},{4,7},{5,6},{6,5},{7,4},{8,11},{9,10},{10,... | collective-permute-start | bytes 12296 | tf_op jit(solution)/shard_map/ppermute | solution.py:512
  4.7 3.6 %collective-permute-start.1 = (f32[8,128]{1,0:T(8,128)S(1)}, f32[8,128]{1,0:T(8,128)S(1)}, u32[]{:S(2)}, u32[]{:S(2)}) collective-permute-start(f32[8,128]{1,0:T(8,128)S(1)} %get-tuple-element.13.refs_0_), channel_id=1, source_target_pairs={{0,2},{1,3},{2,0},{3,1},{4,6},{5,7},{6,4},{7,5},{8,10},{9,11},{10,... | collective-permute-start | bytes 12296 | tf_op jit(solution)/shard_map/ppermute | solution.py:512
  5.3 3.0 %collective-permute-start = (f32[8,128]{1,0:T(8,128)S(1)}, f32[8,128]{1,0:T(8,128)S(1)}, u32[]{:S(2)}, u32[]{:S(2)}) collective-permute-start(f32[8,128]{1,0:T(8,128)S(1)} %get-tuple-element.13.refs_0_), channel_id=1, source_target_pairs={{0,1},{1,0},{2,3},{3,2},{4,5},{5,4},{6,7},{7,6},{8,9},{9,8},{10,11... | collective-permute-start | bytes 12296 | tf_op jit(solution)/shard_map/ppermute | solution.py:512
  9.0 3.9 %collective-permute-start.3 = (bf16[216,128]{1,0:T(8,128)(2,1)S(1)}, bf16[216,128]{1,0:T(8,128)(2,1)S(1)}, u32[]{:S(2)}, u32[]{:S(2)}) collective-permute-start(bf16[216,128]{1,0:T(8,128)(2,1)S(1)} %get-tuple-element.16), channel_id=1, source_target_pairs={{0,3},{1,2},{2,1},{3,0},{4,7},{5,6},{6,5},{7,4},{8,11},{9,10},{10,... | collective-permute-start | bytes 165896 | tf_op jit(solution)/shard_map/ppermute | solution.py:512
  9.1 3.9 %collective-permute-start.4 = (bf16[216,128]{1,0:T(8,128)(2,1)S(1)}, bf16[216,128]{1,0:T(8,128)(2,1)S(1)}, u32[]{:S(2)}, u32[]{:S(2)}) collective-permute-start(bf16[216,128]{1,0:T(8,128)(2,1)S(1)} %get-tuple-element.17), channel_id=1, source_target_pairs={{0,1},{1,0},{2,3},{3,2},{4,5},{5,4},{6,7},{7,6},{8,9},{9,8},{10,11... | collective-permute-start | bytes 165896 | tf_op jit(solution)/shard_map/ppermute | solution.py:512
  9.8 4.3 %collective-permute-start.5 = (bf16[216,128]{1,0:T(8,128)(2,1)S(1)}, bf16[216,128]{1,0:T(8,128)(2,1)S(1)}, u32[]{:S(2)}, u32[]{:S(2)}) collective-permute-start(bf16[216,128]{1,0:T(8,128)(2,1)S(1)} %get-tuple-element.18), channel_id=1, source_target_pairs={{0,2},{1,3},{2,0},{3,1},{4,6},{5,7},{6,4},{7,5},{8,10},{9,11},{10,... | collective-permute-start | bytes 165896 | tf_op jit(solution)/shard_map/ppermute | solution.py:512

commit v14 on v11

--- a/solution.py
+++ b/solution.py
@@ -520,7 +520,7 @@
     part = shard_len // lanes // part_count
     plan = Plan(round((shard_len * grid_count) ** (1 / 3)))
     share, notes = read_points(orbitals, targets, points, fit)
-    shares = [share] + [exchange(share, grid_count, d) for d in range(1, grid_count)]
+    shares = [share] + [exchange(share, grid_count, d) for d in (1, *reversed(range(2, grid_count)))]
     *pieces, at = fit_pairs(orbitals, notes, shares)
     offsets = [0] + list(reversed(range(1, grid_count)))
     pieces = [exchange(pieces[d], grid_count, d) if d else pieces[d] for d in offsets]

time: 37.5 us -> 37.4 us (level)
  no operation moved by 1% of the time
where the time goes in v14:
time: 37.4 us; the launch traced here: 37.2 us
  blocking collectives  20.3 us (54%)
  waiting for transfers between devices  6 us (16%)
  Pallas kernels  5.67 us (15%)
  starting transfers between devices  5.15 us (14%)
    all_to_all x1, blocking collectives, quick_body(): lax.all_to_all(blocks, ('half', 'part', 'grid'), 0, 0, axis_index_groups=...  11.3 us
    all_to_all x1, blocking collectives, quick_body(): lax.all_to_all(sent, ('part', 'grid'), 0, 0, axis_index_groups=[near])  8.98 us
    ppermute x6, waiting for transfers between devices, exchange(): lax.ppermute(value, 'grid', [(i, i ^ offset) for i in range(grid_count)])  6 us
    ppermute x6, starting transfers between devices, exchange(): lax.ppermute(value, 'grid', [(i, i ^ offset) for i in range(grid_count)])  5.15 us
    pallas_call x1, Pallas kernels, read_points(): pl.pallas_call(kernel, out_shape=[pltpu.VMEM((8, lanes), f32), pltpu.VMEM...  2.18 us
    pallas_call x1, Pallas kernels, potentials(): pl.pallas_call(kernel, out_shape=jax.ShapeDtypeStruct((parts * grid_count...  1.4 us
    pallas_call x1, Pallas kernels, settle(): pl.pallas_call(kernel, out_shape=jax.ShapeDtypeStruct((parts * part, keep...  0.81 us
  transfers between devices with their start and end apart: 6, of which 4 were waited for; matrix products, arithmetic and copies ran while one was open for 0% of the time, Pallas kernels for 0%

profile of v14, /device:TPU:0, one launch (start us, length us, event | category | flops | bytes accessed | tf_op | source)
XLA Modules:
  0.0 37.2 jit_solution(15862869792014617490)
XLA Ops:
  0.0 0.0 copy-start
  0.0 0.0 copy-start.1
  0.0 0.0 copy-start.2
  0.0 0.0 copy-start.3
  0.0 0.0 copy-start.4
  0.0 2.2 %read_points.1 = (f32[8,128]{1,0:T(8,128)S(1)}, f32[56,128]{1,0:T(8,128)S(1)}) custom-call(s32[4]{0:T(128)} %points_hbm.1, s32[16]{0:T(128)} %targets_hbm.1, f32[4,4]{1,0:T(4,128)} %fit_hbm.1, bf16[64,27648]{1,0:T(8,128)(2,1)} %orbitals_ref.5), custom_call_target="tpu_custom_call" | custom-call | tf_op jit(solution)/shard_map/read_points/pallas_call | solution.py:326
  2.2 3.0 %collective-permute-start.2 = (f32[8,128]{1,0:T(8,128)S(1)}, f32[8,128]{1,0:T(8,128)S(1)}, u32[]{:S(2)}, u32[]{:S(2)}) collective-permute-start(f32[8,128]{1,0:T(8,128)S(1)} %get-tuple-element.13.refs_0_), channel_id=1, source_target_pairs={{0,2},{1,3},{2,0},{3,1},{4,6},{5,7},{6,4},{7,5},{8,10},{9,11},{10,... | collective-permute-start | bytes 12296 | tf_op jit(solution)/shard_map/ppermute | solution.py:512
  5.2 0.0 collective-permute-start.1
  5.2 0.2 collective-permute-start
  5.4 1.4 %collective-permute-done.2.refs_3_ = f32[8,128]{1,0:T(8,128)S(1)} collective-permute-done((f32[8,128]{1,0:T(8,128)S(1)}, f32[8,128]{1,0:T(8,128)S(1)}, u32[]{:S(2)}, u32[]{:S(2)}) %collective-permute-start.2) | collective-permute-done | bytes 4128 | tf_op jit(solution)/shard_map/ppermute | solution.py:512
  6.8 1.4 %collective-permute-done.1.refs_2_ = f32[8,128]{1,0:T(8,128)S(1)} collective-permute-done((f32[8,128]{1,0:T(8,128)S(1)}, f32[8,128]{1,0:T(8,128)S(1)}, u32[]{:S(2)}, u32[]{:S(2)}) %collective-permute-start.1) | collective-permute-done | bytes 4128 | tf_op jit(solution)/shard_map/ppermute | solution.py:512
  8.3 0.0 collective-permute-done.refs_1_
  8.3 0.0 copy-done
  8.3 0.7 %fit_pairs.1 = (bf16[216,128]{1,0:T(8,128)(2,1)S(1)}, bf16[216,128]{1,0:T(8,128)(2,1)S(1)}, bf16[216,128]{1,0:T(8,128)(2,1)S(1)}, bf16[216,128]{1,0:T(8,128)(2,1)S(1)}, f32[8,128]{1,0:T(8,128)S(1)}) custom-call(f32[56,128]{1,0:T(8,128)S(1)} %get-tuple-element.12.notes_ref, bf16[64,27648]{1,0:T(8,128)(2,1)S(1)} %copy-done, ...), custom_call_target="tpu_custom_call" | custom-call | tf_op jit(solution)/shard_map/fit_pairs/pallas_call | solution.py:378
  9.0 0.4 collective-permute-start.3
  9.4 0.9 %collective-permute-start.4 = (bf16[216,128]{1,0:T(8,128)(2,1)S(1)}, bf16[216,128]{1,0:T(8,128)(2,1)S(1)}, u32[]{:S(2)}, u32[]{:S(2)}) collective-permute-start(bf16[216,128]{1,0:T(8,128)(2,1)S(1)} %get-tuple-element.17), channel_id=1, source_target_pairs={{0,2},{1,3},{2,0},{3,1},{4,6},{5,7},{6,4},{7,5},{8,10},{9,11},{10,... | collective-permute-start | bytes 165896 | tf_op jit(solution)/shard_map/ppermute | solution.py:512
  10.3 0.7 %collective-permute-start.5 = (bf16[216,128]{1,0:T(8,128)(2,1)S(1)}, bf16[216,128]{1,0:T(8,128)(2,1)S(1)}, u32[]{:S(2)}, u32[]{:S(2)}) collective-permute-start(bf16[216,128]{1,0:T(8,128)(2,1)S(1)} %get-tuple-element.18), channel_id=1, source_target_pairs={{0,1},{1,0},{2,3},{3,2},{4,5},{5,4},{6,7},{7,6},{8,9},{9,8},{10,11... | collective-permute-start | bytes 165896 | tf_op jit(solution)/shard_map/ppermute | solution.py:512
  10.9 2.1 %collective-permute-done.3.refs_1_ = bf16[216,128]{1,0:T(8,128)(2,1)S(1)} collective-permute-done((bf16[216,128]{1,0:T(8,128)(2,1)S(1)}, bf16[216,128]{1,0:T(8,128)(2,1)S(1)}, u32[]{:S(2)}, u32[]{:S(2)}) %collective-permute-start.3) | collective-permute-done | bytes 55328 | tf_op jit(solution)/shard_map/ppermute | solution.py:512
  13.1 1.0 %collective-permute-done.4.refs_2_ = bf16[216,128]{1,0:T(8,128)(2,1)S(1)} collective-permute-done((bf16[216,128]{1,0:T(8,128)(2,1)S(1)}, bf16[216,128]{1,0:T(8,128)(2,1)S(1)}, u32[]{:S(2)}, u32[]{:S(2)}) %collective-permute-start.4) | collective-permute-done | bytes 55328 | tf_op jit(solution)/shard_map/ppermute | solution.py:512
  14.1 0.0 collective-permute-done.5.refs_3_
  14.1 0.0 copy-done.1
  14.1 0.0 copy-done.2
  14.1 0.0 copy-done.3
  14.1 0.0 copy-done.4
  14.1 1.4 %potentials.1 = bf16[16,56,128]{2,1,0:T(8,128)(2,1)S(1)} custom-call(f32[8,128]{1,0:T(8,128)S(1)} %get-tuple-element.14.at_ref, bf16[216,128]{1,0:T(8,128)(2,1)S(1)} %get-tuple-element.15.refs_0_, bf16[216,128]{1,0:T(8,128)(2,1)S(1)} %collective-permute-done.3.refs_1_, bf16[216,128]{1,0:T(8,128)(2,1)S(1)} %collective-permute-done.4.refs_2_, ...), custom_call_target="tpu_custom_call" | custom-call | tf_op jit(solution)/shard_map/potentials/pallas_call | solution.py:410
  15.5 9.0 %all_to_all.10.received_ref = bf16[16,56,128]{2,1,0:T(8,128)(2,1)S(1)} all-to-all(bf16[16,56,128]{2,1,0:T(8,128)(2,1)S(1)} %potentials.1), channel_id=1, replica_groups={{15,7,11,3,13,5,9,1,14,6,10,2,12,4,8,0},{31,23,27,19,29,21,25,17,30,22,..., dimensions={0} | all-to-all | bytes 458752 | tf_op jit(solution)/shard_map/all_to_all | solution.py:531
  24.5 0.6 %apply_part.1 = bf16[8,108,128]{2,1,0:T(8,128)(2,1)S(1)} custom-call(f32[56,128]{1,0:T(8,128)S(1)} %get-tuple-element.12.notes_ref, bf16[64,27648]{1,0:T(8,128)(2,1)S(1)} %copy-done, bf16[16,56,128]{2,1,0:T(8,128)(2,1)S(1)} %all_to_all.10.received_ref), custom_call_target="tpu_custom_call" | custom-call | tf_op jit(solution)/shard_map/apply_part/pallas_call | solution.py:450
  25.1 11.3 %all_to_all.11.kept_ref = bf16[8,108,128]{2,1,0:T(8,128)(2,1)S(1)} all-to-all(bf16[8,108,128]{2,1,0:T(8,128)(2,1)S(1)} %apply_part.1), channel_id=1, replica_groups={{20,16,24,28,12,8,0,4},{17,21,29,25,9,13,5,1},{22,18,26,30,14,10,2,6},{..., dimensions={0} | all-to-all | bytes 442368 | tf_op jit(solution)/shard_map/all_to_all | solution.py:533
  36.4 0.8 %settle.1 = f32[216,2,128]{2,1,0:T(2,128)} custom-call(bf16[8,108,128]{2,1,0:T(8,128)(2,1)S(1)} %all_to_all.11.kept_ref), custom_call_target="tpu_custom_call" | custom-call | tf_op jit(solution)/shard_map/settle/pallas_call | solution.py:485
Async XLA Ops:
  0.0 8.3 %copy-start = (bf16[64,27648]{1,0:T(8,128)(2,1)S(1)}, bf16[64,27648]{1,0:T(8,128)(2,1)}, u32[]{:S(2)}) copy-start(bf16[64,27648]{1,0:T(8,128)(2,1)} %orbitals_ref.5) | copy-start | bytes 10616836
  0.0 14.1 %copy-start.1 = (f32[24,48,128]{2,1,0:T(8,128)S(1)}, f32[24,48,128]{2,1,0:T(8,128)}, u32[]{:S(2)}) copy-start(f32[24,48,128]{2,1,0:T(8,128)} %constant.11.clone.refs_7_) | copy-start | bytes 1769476
  0.0 14.1 %copy-start.2 = (bf16[1024,256]{1,0:T(8,128)(2,1)S(1)}, bf16[1024,256]{1,0:T(8,128)(2,1)}, u32[]{:S(2)}) copy-start(bf16[1024,256]{1,0:T(8,128)(2,1)} %constant.10.clone.refs_6_) | copy-start | bytes 1572868
  0.0 14.1 %copy-start.3 = (bf16[1024,256]{1,0:T(8,128)(2,1)S(1)}, bf16[1024,256]{1,0:T(8,128)(2,1)}, u32[]{:S(2)}) copy-start(bf16[1024,256]{1,0:T(8,128)(2,1)} %constant.9.clone.refs_5_) | copy-start | bytes 1572868
  0.0 14.1 %copy-start.4 = (bf16[48,96]{1,0:T(8,128)(2,1)S(1)}, bf16[48,96]{1,0:T(8,128)(2,1)}, u32[]{:S(2)}) copy-start(bf16[48,96]{1,0:T(8,128)(2,1)} %constant.8.clone.refs_4_) | copy-start | bytes 27652
  2.2 4.6 %collective-permute-start.2 = (f32[8,128]{1,0:T(8,128)S(1)}, f32[8,128]{1,0:T(8,128)S(1)}, u32[]{:S(2)}, u32[]{:S(2)}) collective-permute-start(f32[8,128]{1,0:T(8,128)S(1)} %get-tuple-element.13.refs_0_), channel_id=1, source_target_pairs={{0,2},{1,3},{2,0},{3,1},{4,6},{5,7},{6,4},{7,5},{8,10},{9,11},{10,... | collective-permute-start | bytes 12296 | tf_op jit(solution)/shard_map/ppermute | solution.py:512
  5.2 3.0 %collective-permute-start.1 = (f32[8,128]{1,0:T(8,128)S(1)}, f32[8,128]{1,0:T(8,128)S(1)}, u32[]{:S(2)}, u32[]{:S(2)}) collective-permute-start(f32[8,128]{1,0:T(8,128)S(1)} %get-tuple-element.13.refs_0_), channel_id=1, source_target_pairs={{0,3},{1,2},{2,1},{3,0},{4,7},{5,6},{6,5},{7,4},{8,11},{9,10},{10,... | collective-permute-start | bytes 12296 | tf_op jit(solution)/shard_map/ppermute | solution.py:512
  5.2 3.0 %collective-permute-start = (f32[8,128]{1,0:T(8,128)S(1)}, f32[8,128]{1,0:T(8,128)S(1)}, u32[]{:S(2)}, u32[]{:S(2)}) collective-permute-start(f32[8,128]{1,0:T(8,128)S(1)} %get-tuple-element.13.refs_0_), channel_id=1, source_target_pairs={{0,1},{1,0},{2,3},{3,2},{4,5},{5,4},{6,7},{7,6},{8,9},{9,8},{10,11... | collective-permute-start | bytes 12296 | tf_op jit(solution)/shard_map/ppermute | solution.py:512
  9.0 4.0 %collective-permute-start.3 = (bf16[216,128]{1,0:T(8,128)(2,1)S(1)}, bf16[216,128]{1,0:T(8,128)(2,1)S(1)}, u32[]{:S(2)}, u32[]{:S(2)}) collective-permute-start(bf16[216,128]{1,0:T(8,128)(2,1)S(1)} %get-tuple-element.16), channel_id=1, source_target_pairs={{0,3},{1,2},{2,1},{3,0},{4,7},{5,6},{6,5},{7,4},{8,11},{9,10},{10,... | collective-permute-start | bytes 165896 | tf_op jit(solution)/shard_map/ppermute | solution.py:512
  9.4 4.7 %collective-permute-start.4 = (bf16[216,128]{1,0:T(8,128)(2,1)S(1)}, bf16[216,128]{1,0:T(8,128)(2,1)S(1)}, u32[]{:S(2)}, u32[]{:S(2)}) collective-permute-start(bf16[216,128]{1,0:T(8,128)(2,1)S(1)} %get-tuple-element.17), channel_id=1, source_target_pairs={{0,2},{1,3},{2,0},{3,1},{4,6},{5,7},{6,4},{7,5},{8,10},{9,11},{10,... | collective-permute-start | bytes 165896 | tf_op jit(solution)/shard_map/ppermute | solution.py:512
  10.3 3.8 %collective-permute-start.5 = (bf16[216,128]{1,0:T(8,128)(2,1)S(1)}, bf16[216,128]{1,0:T(8,128)(2,1)S(1)}, u32[]{:S(2)}, u32[]{:S(2)}) collective-permute-start(bf16[216,128]{1,0:T(8,128)(2,1)S(1)} %get-tuple-element.18), channel_id=1, source_target_pairs={{0,1},{1,0},{2,3},{3,2},{4,5},{5,4},{6,7},{7,6},{8,9},{9,8},{10,11... | collective-permute-start | bytes 165896 | tf_op jit(solution)/shard_map/ppermute | solution.py:512
